TPU v7x, 512 devices: a whole 4x8x8 slice. The times are simulated.
512 devices in a mesh: view: 4 (over x), space: 128 (over y, z, core).
Axes of the slice: x: 4, y: 8, z: 8, core: 2. Of those that a mesh axis runs over, the one named last changes fastest.
Arguments:
- estimate: bfloat16 [512, 512, 256], P('space'), may hold values from 0.1 to 10
- measured: bfloat16 [4, 512, 512, 256], P('view', 'space'), may hold values from 0.1 to 10
- psf_x: float32 [4, 31], P('view'), may hold values from 0.05 to 1
- psf_y: float32 [4, 31], P('view'), may hold values from 0.05 to 1
- psf_z: float32 [4, 63], P('view'), may hold values from 0.05 to 1
- tissue_mask: int32 [8], replicated, may hold values from 0 to 1, as said below
- column_owner: int32 [1024], replicated, may hold values from 0 to 127, as said below
Outputs:
- updated: bfloat16 [512, 512, 256], P('space')
- column_blur: bfloat16 [4, 512, 1024, 128], P('view', None, 'space')
Inputs may be any that keep to these rules, and one draw needn't show every extreme that they name: `tissue_mask`: exactly half of the 8 tiles are tissue. `column_owner`: each index of space owns at most 8 tissue units, and some own exactly 8. Owners of units in non-tissue tiles carry no meaning.
All inputs are finite; a program needn't handle non-finite values.
Results may differ from a plain program's by a relative error of at most 0.001.
The roundings to bfloat16 on the way count: a program that leaves them out, or rounds other values in their place, can miss the bound.
Values may be sent and summed in bfloat16 or wider, within the bound.
No kernel may reach another device: no remote copies, remote signals or barrier semaphores. Data moves between devices by JAX's collectives and lax.ppermute only.
A program may use at most 64 MiB of HBM per device.

v0:
```python
import jax
import jax.numpy as jnp
from jax import lax
from jax.sharding import PartitionSpec as P

TILE = 128


def kernel_matrix(tap_values, length):
    normed = tap_values / jnp.sum(tap_values)
    rounded = normed.astype(jnp.bfloat16)
    half_len = tap_values.shape[0] // 2
    offset = (
        jnp.arange(length, dtype=jnp.int32)[None, :]
        - jnp.arange(length, dtype=jnp.int32)[:, None]
        + half_len
    )
    inside = (offset >= 0) & (offset < tap_values.shape[0])
    picked = jnp.take(rounded, jnp.clip(offset, 0, tap_values.shape[0] - 1))
    return jnp.where(inside, picked, jnp.zeros_like(picked))


def unit_tissue(tissue_mask, rows_x, tiles_y):
    unit_index = jnp.arange(rows_x * tiles_y, dtype=jnp.int32)
    tile_index = unit_index // tiles_y // TILE * tiles_y + unit_index % tiles_y
    matching = tile_index[:, None] == jnp.arange(tissue_mask.shape[0], dtype=jnp.int32)[None, :]
    return jnp.sum(jnp.where(matching, tissue_mask[None, :], 0), axis=1)


def slot_layout(tissue, column_owner, devices, capacity):
    unit_count = tissue.shape[0]
    unit_index = jnp.arange(unit_count, dtype=jnp.int32)
    member = (
        (column_owner[:, None] == jnp.arange(devices, dtype=jnp.int32)[None, :])
        & (tissue[:, None] > 0)
    ).astype(jnp.int32)
    before = jnp.cumsum(member, axis=0) - member
    position = jnp.sum(before * member, axis=1)
    target = jnp.where(tissue > 0, column_owner * capacity + position, devices * capacity)
    return (
        jnp.full((devices * capacity,), unit_count, jnp.int32)
        .at[target]
        .set(unit_index, mode="drop")
    )


def shards(estimate, measured, psf_x, psf_y, psf_z, tissue_mask, column_owner):
    devices = lax.axis_size("space")
    views = lax.axis_size("view")
    slab_depth, rows_x, rows_y = estimate.shape
    tiles_y = rows_y // TILE
    unit_count = rows_x * tiles_y
    full_depth = slab_depth * devices
    capacity = 2 * (unit_count // 2 // devices)
    tissue = unit_tissue(tissue_mask, rows_x, tiles_y)
    slot_table = slot_layout(tissue, column_owner, devices, capacity)
    filled = (
        lax.dynamic_slice_in_dim(slot_table, lax.axis_index("space") * capacity, capacity)
        < unit_count
    )
    matrix_x = kernel_matrix(psf_x[0], rows_x)
    matrix_y = kernel_matrix(psf_y[0], rows_y)
    matrix_z = kernel_matrix(psf_z[0], full_depth)
    along_x = jnp.einsum(
        "ab,kby->kay", matrix_x, estimate, preferred_element_type=jnp.float32
    ).astype(jnp.bfloat16)
    blurred_xy = jnp.einsum(
        "kxb,ab->kxa", along_x, matrix_y, preferred_element_type=jnp.float32
    ).astype(jnp.bfloat16)
    blur_pieces = jnp.take(
        blurred_xy.reshape(slab_depth, unit_count, TILE),
        slot_table,
        axis=1,
        mode="fill",
        fill_value=0,
    )
    data_pieces = jnp.take(
        measured[0].reshape(slab_depth, unit_count, TILE),
        slot_table,
        axis=1,
        mode="fill",
        fill_value=0,
    )
    blur_pieces = blur_pieces.reshape(slab_depth, devices, capacity, TILE)
    data_pieces = data_pieces.reshape(slab_depth, devices, capacity, TILE)
    blur_cols, data_cols = (
        lax.all_to_all(blur_pieces, "space", split_axis=1, concat_axis=0, tiled=True),
        lax.all_to_all(data_pieces, "space", split_axis=1, concat_axis=0, tiled=True),
    )
    blur_cols = blur_cols.reshape(full_depth, capacity, TILE)
    data_cols = data_cols.reshape(full_depth, capacity, TILE)
    column_values = jnp.einsum(
        "wz,zca->wca", matrix_z, blur_cols, preferred_element_type=jnp.float32
    )
    column_out = column_values.astype(jnp.bfloat16)
    slot_live = filled[None, :, None]
    safe_values = jnp.where(slot_live, column_values, jnp.ones_like(column_values))
    ratio_cols = jnp.where(
        slot_live, data_cols.astype(jnp.float32) / safe_values, jnp.zeros_like(safe_values)
    ).astype(jnp.bfloat16)
    back_cols = jnp.einsum(
        "wz,wca->zca", matrix_z, ratio_cols, preferred_element_type=jnp.float32
    ).astype(jnp.bfloat16)
    returned = lax.all_to_all(
        back_cols.reshape(full_depth, 1, capacity, TILE),
        "space",
        split_axis=0,
        concat_axis=1,
        tiled=True,
    )
    back_units = jnp.ones((slab_depth, unit_count, TILE), jnp.bfloat16)
    back_units = back_units.at[:, slot_table, :].set(
        returned.reshape(slab_depth, devices * capacity, TILE), mode="drop"
    )
    back_slab = back_units.reshape(slab_depth, rows_x, rows_y)
    back_y = jnp.einsum(
        "kxa,ab->kxb", back_slab, matrix_y, preferred_element_type=jnp.float32
    ).astype(jnp.bfloat16)
    back_x = jnp.einsum("kay,ab->kby", back_y, matrix_x, preferred_element_type=jnp.float32)
    summed = lax.psum(back_x, "view")
    updated = (estimate.astype(jnp.float32) * summed / views).astype(jnp.bfloat16)
    return (updated, column_out[None])


def solution(mesh):
    placed = (
        P("space", None, None),
        P("view", "space", None, None),
        P("view", None),
        P("view", None),
        P("view", None),
        P(),
        P(),
    )
    return jax.shard_map(
        shards,
        mesh=mesh,
        in_specs=placed,
        out_specs=(P("space", None, None), P("view", None, "space", None)),
        check_vma=False,
    )
```

profile of v0, /device:TPU:1, one launch (start us, length us, event | category | flops | bytes accessed | tf_op | source)
XLA Modules:
  0.0 376.3 jit_solution(7479119035025687086)
XLA Ops:
  7.2 1.4 reduce_sum.45
  8.5 1.3 divide_convert_fusion.2
  11.3 1.3 reduce_sum.49
  12.5 1.3 divide_convert_fusion
  18.1 4.3 %scatter_custom_fusion = s32[1024]{0:T(1024)S(1)} fusion(s32[1024]{0:T(1024)S(1)} %compare_select_fusion.9, s32[1024]{0:T(1024)S(1)} %iota.108, s32[]{:T(128)} %constant.121.clone.1), kind=kCustom, calls=%fused_computation.512 | custom fusion | bytes 4100 | tf_op jit(solution)/shard_map/scatter | solution.py:43
  22.4 40.6 %convolution_convert_fusion.1 = bf16[4,512,256]{2,1,0:T(8,128)(2,1)S(1)} fusion(bf16[4,512,256]{2,1,0:T(8,128)(2,1)S(1)} %copy-done.3, bf16[]{:T(256)} %bitcast.48, bf16[]{:T(256)} %bitcast.49, bf16[]{:T(256)} %bitcast.50, bf16[]{:T(256)} %bitcast.51, bf16[]{:T(256)} %bitcast.52, bf16[]{:T(256)} %bitcast.54, bf16[]{:T(256)} %bitcast.53, bf16[]{:T(256)} %bitcast.1, ...), kind=kOutput, calls=%fused_computation.14 | convolution fusion | flops 832569344 | bytes 2097276 | tf_op jit(solution)/shard_map/kxb,ab->kxa/dot_general | solution.py:67
  64.2 1.4 reshape_squeeze.3
  66.5 3.6 gather_fusion.1
  70.0 3.6 gather_fusion
  73.6 4.5 %broadcast_select_fusion = (bf16[1024,4,128]{2,1,0:T(4,128)(2,1)}, bf16[1024,4,128]{2,1,0:T(4,128)(2,1)S(1)}) fusion(bf16[1024,4,128]{2,1,0:T(4,128)(2,1)S(1)} %gather_fusion.1, pred[1024]{0:T(1024)(128)(4,1)S(1)} %compare_and_fusion, bf16[1024,4,128]{2,1,0:T(4,128)(2,1)S(1)} %gather_fusion), kind=kLoop, calls=%fused_computation.129 | loop fusion | flops 1048576 | bytes 4195328 | tf_op jit(solution)/shard_map/jit(_take)/select_n | solution.py:70
  78.2 1.2 copy.57
  79.3 18.4 %all-to-all-start = ((bf16[4,128,8,128]{3,2,0,1:T(8,128)(2,1)}), bf16[4,128,8,128]{3,2,0,1:T(8,128)(2,1)S(1)}, u32[]{:S(2)}, u32[]{:S(2)}) async-start(bf16[4,128,8,128]{3,2,0,1:T(8,128)(2,1)} %copy.57), calls=%async_computation | async-start | bytes 2097152 | tf_op jit(solution)/shard_map/all_to_all | solution.py:88
  99.1 29.0 %all-to-all-done = bf16[4,128,8,128]{3,2,0,1:T(8,128)(2,1)S(1)} async-done(((bf16[4,128,8,128]{3,2,0,1:T(8,128)(2,1)}), bf16[4,128,8,128]{3,2,0,1:T(8,128)(2,1)S(1)}, u32[]{:S(2)}, u32[]{:S(2)}) %all-to-all-start) | async-done | bytes 1048608 | tf_op jit(solution)/shard_map/all_to_all | solution.py:88
  128.2 6.9 %all-to-all-start.1 = ((bf16[4,128,8,128]{3,0,2,1:T(4,128)(2,1)}), bf16[4,128,8,128]{3,0,2,1:T(4,128)(2,1)S(1)}, u32[]{:S(2)}, u32[]{:S(2)}) async-start(bf16[4,128,8,128]{3,0,2,1:T(4,128)(2,1)} %bitcast.251), calls=%async_computation.1 | async-start | bytes 2097152 | tf_op jit(solution)/shard_map/all_to_all | solution.py:87
  138.1 43.9 %fusion.176 = bf16[512,512]{0,1:T(8,128)(2,1)S(1)} fusion(bf16[]{:T(256)} %bitcast.174, bf16[]{:T(256)} %bitcast.175, bf16[]{:T(256)} %bitcast.176, bf16[]{:T(256)} %bitcast.177, bf16[]{:T(256)} %bitcast.178, bf16[]{:T(256)} %bitcast.180, bf16[]{:T(256)} %bitcast.179, bf16[]{:T(256)} %bitcast.63, bf16[]{:T(256)} %bitcast.65, bf16[]{:T(256)} %bitcast.67, ...), kind=kLoop, calls=%fused_computation.199 | loop fusion | flops 34078720 | bytes 524414 | tf_op jit(solution)/shard_map/jit(_take)/gather | solution.py:19
  182.3 1.8 copy.58
  186.1 1.0 fusion.1
  187.8 44.0 %all_to_all.39 = bf16[512,1,8,128]{3,2,1,0:T(8,128)(2,1)S(1)} all-to-all(bf16[512,1,8,128]{3,2,1,0:T(8,128)(2,1)S(1)} %copy.63), channel_id=1, replica_groups=mesh['view'=4,'space'=128] {'space'}, dimensions={0} | all-to-all | bytes 2097152 | tf_op jit(solution)/shard_map/all_to_all | solution.py:104
  232.5 27.9 %scatter_fusion = bf16[4,1024,128]{2,0,1:T(4,128)(2,1)S(1)} fusion(bf16[4,1024,128]{2,0,1:T(4,128)(2,1)S(1)} %broadcast_in_dim.91, s32[1024]{0:T(1024)S(1)} %get-tuple-element.14, bf16[1024,4,128]{2,1,0:T(4,128)(2,1)S(1)} %bitcast.5425), kind=kCustom, calls=%fused_computation.3 | custom fusion | bytes 3149824 | tf_op jit(solution)/shard_map/scatter | solution.py:112
  261.0 42.0 %convolution_bitcast_fusion = f32[4,512,256]{2,1,0:T(8,128)} fusion(bf16[4,512,256]{2,1,0:T(8,128)(2,1)S(1)} %reshape.399, bf16[]{:T(256)} %bitcast.48, bf16[]{:T(256)} %bitcast.49, bf16[]{:T(256)} %bitcast.50, bf16[]{:T(256)} %bitcast.51, bf16[]{:T(256)} %bitcast.52, bf16[]{:T(256)} %bitcast.54, bf16[]{:T(256)} %bitcast.53, bf16[]{:T(256)} %bitcast.1, ...), kind=kOutput, calls=%fused_computation.12 | convolution fusion | flops 832045056 | bytes 3145852 | tf_op jit(solution)/shard_map/kay,ab->kby/dot_general | solution.py:119
  303.0 1.6 copy-done.1
  304.8 1.6 copy.66
  306.4 60.2 %all-reduce.2.cloned.1.call-done = f32[4,512,256]{2,1,0:T(8,128)} async-done(((f32[4,512,256]{2,1,0:T(8,128)}), f32[4,512,256]{2,1,0:T(8,128)}) %all-reduce.2.cloned.1.call-update) | async-done | bytes 2097168 | tf_op jit(solution)/shard_map/psum | solution.py:120
  366.6 2.8 multiply_convert_fusion
  (56 shorter events, 16.3 us)
Async XLA Ops:
  7.2 10.4 %copy-start.5 = (s32[1024]{0:T(1024)S(1)}, s32[1024]{0:T(1024)}, u32[]{:S(2)}) copy-start(s32[1024]{0:T(1024)} %param.15) | copy-start | bytes 12292
  7.2 15.2 %copy-start.3 = (bf16[4,512,256]{2,1,0:T(8,128)(2,1)S(1)}, bf16[4,512,256]{2,1,0:T(8,128)(2,1)}, u32[]{:S(2)}) copy-start(bf16[4,512,256]{2,1,0:T(8,128)(2,1)} %param.9) | copy-start | bytes 3145732
  78.2 19.6 %copy-start.6 = (f32[1,63]{1,0:T(1,128)S(1)}, f32[1,63]{1,0:T(1,128)}, u32[]{:S(2)}) copy-start(f32[1,63]{1,0:T(1,128)} %param.13) | copy-start | bytes 760
  79.3 48.9 %all-to-all-start = ((bf16[4,128,8,128]{3,2,0,1:T(8,128)(2,1)}), bf16[4,128,8,128]{3,2,0,1:T(8,128)(2,1)S(1)}, u32[]{:S(2)}, u32[]{:S(2)}) async-start(bf16[4,128,8,128]{3,2,0,1:T(8,128)(2,1)} %copy.57), calls=%async_computation | async-start | bytes 2097152 | tf_op jit(solution)/shard_map/all_to_all | solution.py:88
  128.2 56.0 %all-to-all-start.1 = ((bf16[4,128,8,128]{3,0,2,1:T(4,128)(2,1)}), bf16[4,128,8,128]{3,0,2,1:T(4,128)(2,1)S(1)}, u32[]{:S(2)}, u32[]{:S(2)}) async-start(bf16[4,128,8,128]{3,0,2,1:T(4,128)(2,1)} %bitcast.251), calls=%async_computation.1 | async-start | bytes 2097152 | tf_op jit(solution)/shard_map/all_to_all | solution.py:87
  135.1 231.5 %all-reduce.2.cloned.1.call-start = ((), (), s32[]{:S(2)}) async-start(), calls=%async_computation.3 | async-start | bytes 4194304 | tf_op jit(solution)/shard_map/psum | solution.py:120
  184.5 1.6 copy-start.2
  185.3 1.8 copy-start
  303.0 1.6 copy-start.1
  304.6 62.0 %copy-start.4 = (bf16[4,512,256]{2,1,0:T(8,128)(2,1)S(1)}, bf16[4,512,256]{2,1,0:T(8,128)(2,1)}, u32[]{:S(2)}) copy-start(bf16[4,512,256]{2,1,0:T(8,128)(2,1)} %param.9) | copy-start | bytes 3145732
Sparse Core Ops, SparseCore 0:
  303.2 63.3 all-reduce.1
where the time goes:
time: 378 us; the launch traced here: 376 us
  waiting for transfers between devices  89.2 us (24%)
  matrix products  84.4 us (22%)
  other arithmetic  60.1 us (16%)
  local copies, waits for them, and re-layouts  58.8 us (16%)
  blocking collectives  44 us (12%)
  starting transfers between devices  25.4 us (7%)
  between operations  14.4 us (4%)
    psum x1, waiting for transfers between devices, shards(): summed = lax.psum(back_x, 'view')  60.2 us
    all_to_all x1, blocking collectives, shards(): lax.all_to_all(back_cols.reshape(full_depth, 1, capacity, TILE), 'space',...  44 us
    gather x1, other arithmetic, kernel_matrix(): picked = jnp.take(rounded, jnp.clip(offset, 0, tap_values.shape[0] - 1))  43.9 us
    dot_general x1, matrix products, shards(): jnp.einsum('kay,ab->kby', back_y, matrix_x, preferred_element_type=jnp.fl...  42 us
    dot_general x1, matrix products, shards(): jnp.einsum('kxb,ab->kxa', along_x, matrix_y, preferred_element_type=jnp.f...  40.6 us
    all_to_all x1, waiting for transfers between devices, shards(): lax.all_to_all(data_pieces, 'space', split_axis=1, concat_axis=0, tiled=T...  29 us
    scatter x2, local copies, waits for them, and re-layouts, shards(): back_units.at[:, slot_table, :]  28.1 us
    all_to_all x1, starting transfers between devices, shards(): lax.all_to_all(data_pieces, 'space', split_axis=1, concat_axis=0, tiled=T...  18.4 us
  transfers between devices with their start and end apart: 3, of which 2 were waited for; matrix products, arithmetic and copies ran while one was open for 14% of the time, Pallas kernels for 0%

commit v1 on v0

v1 whole, which is shorter than its diff:
```python
import jax
import jax.numpy as jnp
from jax import lax
from jax.experimental import pallas as pl
from jax.experimental.pallas import tpu as pltpu
from jax.sharding import PartitionSpec as P

F32 = jnp.float32
BF16 = jnp.bfloat16
I32 = jnp.int32

VIEWS, DEVS = 4, 128
SLAB, NX, NY, TILE = 4, 512, 256, 128
UNITS = 1024
HALF = 4
MSG = 3 * SLAB * HALF
TAPS_XY, TAPS_Z = 31, 63
ZB = 256
VMEM_LIMIT = 48 * 1024 * 1024


def iota(shape, dim):
    return lax.broadcasted_iota(I32, shape, dim)


def placed_taps(read, count, lanes, place):
    lane = iota((1, lanes), 1)
    total = read(0)
    for m in range(1, count):
        total = total + read(m)
    row = jnp.zeros((1, lanes), F32)
    for m in range(count):
        row = jnp.where(lane == place(m) % lanes, read(m), row)
    return (row / jnp.full((1, lanes), total, F32)).astype(BF16).astype(F32)


def rolled(row, rows):
    return pltpu.roll(
        jnp.broadcast_to(row, (rows, row.shape[1])), 0, 1, stride=1, stride_axis=0
    )


def band(row, n, half):
    distance = jnp.abs(iota((n, n), 1) - iota((n, n), 0))
    return jnp.where(distance <= half, rolled(row, n), 0.0).astype(BF16)


def dot(a, b, dims=((1,), (0,))):
    return lax.dot_general(a, b, (dims, ((), ())), preferred_element_type=F32)


def one_hot(condition):
    return jnp.where(condition, 1.0, 0.0).astype(BF16)


def slot_tables(mask_ref, owner_ref):
    device = iota((DEVS, ZB), 0)
    lane = iota((DEVS, ZB), 1)
    before_tri = one_hot(iota((ZB, ZB), 0) < iota((ZB, ZB), 1))
    count = jnp.zeros((DEVS, 1), F32)
    unit_of = [jnp.zeros((DEVS, 1), F32) for _ in range(2 * HALF)]
    for block in range(UNITS // ZB):
        tissue = jnp.where(lane % 2 == 0, mask_ref[2 * block], mask_ref[2 * block + 1])
        owner = owner_ref[0:1, block * ZB : (block + 1) * ZB]
        member = (owner == device) & (tissue > 0)
        before = dot(one_hot(member), before_tri) + count
        unit = (lane + block * ZB).astype(F32)
        for slot in range(2 * HALF):
            here = member & (before == float(slot))
            unit_of[slot] += jnp.sum(jnp.where(here, unit, 0.0), axis=1, keepdims=True)
        count += jnp.sum(jnp.where(member, 1.0, 0.0), axis=1, keepdims=True)
    over = jnp.maximum(count - HALF, 0.0)
    free = jnp.maximum(HALF - count, 0.0)
    lower = one_hot(iota((DEVS, DEVS), 1) < iota((DEVS, DEVS), 0))
    square = (DEVS, DEVS)
    starts = dot(
        lower,
        jnp.where(iota(square, 1) == 0, over, jnp.where(iota(square, 1) == 1, free, 0.0)).astype(BF16),
    )
    over_start, free_start = starts[:, 0:1], starts[:, 1:2]
    columns = jnp.zeros(square, F32)
    for i, column in enumerate([over_start, over, *unit_of[HALF:]]):
        columns = jnp.where(iota(square, 1) == i, column, columns)
    rows = columns.T
    balanced = []
    for slot in range(HALF):
        rank = free_start + (slot - count)
        filler = jnp.zeros((DEVS, 1), F32)
        for extra in range(HALF):
            match = (rows[0:1] + extra == rank) & (rows[1:2] > extra)
            filler += jnp.sum(jnp.where(match, rows[2 + extra : 3 + extra], 0.0), axis=1, keepdims=True)
        balanced.append(jnp.where(count > slot, unit_of[slot], filler))
    return balanced, unit_of[HALF:], count


def pack_kernel(mask_ref, px_ref, py_ref, owner_ref, est_ref, meas_ref, out_ref, table_ref, count_ref, wide):
    balanced, overflow, count = slot_tables(mask_ref, owner_ref)
    count_ref[...] = jnp.broadcast_to(count, (DEVS, TILE)).astype(I32)
    units = jnp.concatenate(balanced + overflow, axis=0).astype(I32)
    row_x = units // 2
    odd = units % 2 == 1
    slots = HALF * DEVS
    lane = iota((DEVS, slots), 1)
    along = jnp.zeros((DEVS, slots), F32)
    for slot in range(HALF):
        mine = (lane // HALF == iota((DEVS, slots), 0)) & (lane % HALF == slot)
        along = jnp.where(mine, balanced[slot], along)
    table_ref[...] = jnp.broadcast_to(jnp.sum(along, axis=0, keepdims=True), (8, slots)).astype(I32)

    half_xy = TAPS_XY // 2
    matrix_x = band(placed_taps(lambda m: px_ref[0, m], TAPS_XY, NX, lambda m: m - half_xy), NX, half_xy)
    matrix_y = band(placed_taps(lambda m: py_ref[0, m], TAPS_XY, NY, lambda m: m - half_xy), NY, half_xy)
    pick = one_hot(row_x == iota((2 * slots, NX), 1))
    picked_x = dot(pick, matrix_x).astype(BF16)
    for plane in range(SLAB):
        along_x = dot(picked_x, est_ref[plane]).astype(BF16)
        blurred = dot(along_x, matrix_y, ((1,), (1,)))
        blurred = jnp.where(odd, blurred[:, TILE:], blurred[:, :TILE])
        seen = dot(pick[:slots], meas_ref[0, plane])
        seen = jnp.where(odd[:slots], seen[:, TILE:], seen[:, :TILE])
        for slot in range(HALF):
            row = plane * HALF + slot
            here = slice(slot * DEVS, (slot + 1) * DEVS)
            past = slice(slots + slot * DEVS, slots + (slot + 1) * DEVS)
            wide[pl.ds(row, DEVS, stride=MSG), :] = blurred[here]
            wide[pl.ds(SLAB * HALF + row, DEVS, stride=MSG), :] = blurred[past]
            wide[pl.ds(2 * SLAB * HALF + row, DEVS, stride=MSG), :] = seen[here]
    out_ref[...] = wide[...].astype(BF16).reshape(DEVS, MSG, TILE)


def z_kernel(me_ref, pz_ref, count_ref, in_ref, column_ref, back_ref, padded, ratio):
    group = SLAB * HALF
    rows = DEVS * group
    edge = ZB // 2
    half_z = TAPS_Z // 2
    near = edge - HALF * half_z
    far = edge + HALF * half_z
    forward = rolled(placed_taps(lambda m: pz_ref[0, m], TAPS_Z, 2 * ZB, lambda m: near + HALF * m), ZB).astype(BF16)
    adjoint = rolled(placed_taps(lambda m: pz_ref[0, m], TAPS_Z, 2 * ZB, lambda m: far - HALF * m), ZB).astype(BF16)
    r = iota((ZB, ZB), 0)
    part = ZB // SLAB
    source = r % part // HALF * group + r // part * HALF + r % HALF
    adjoint = dot(one_hot(iota((ZB, ZB), 1) == source), adjoint).astype(BF16)

    padded[0:edge, :] = jnp.zeros((edge, 2 * TILE), BF16)
    padded[edge + rows :, :] = jnp.zeros((edge, 2 * TILE), BF16)
    ratio[0:edge, :] = jnp.zeros((edge, TILE), BF16)
    ratio[edge + rows :, :] = jnp.zeros((edge, TILE), BF16)
    padded[edge : edge + rows, 0:TILE] = in_ref[:, 0:group, :].reshape(rows, TILE)
    padded[edge : edge + rows, TILE:] = in_ref[:, group : 2 * group, :].reshape(rows, TILE)
    count = count_ref[pl.ds(me_ref[0], 1), :].reshape(1, 1, TILE)
    planes = ZB // HALF
    pairs = planes // 2
    sub = iota((pairs, 8, TILE), 1)
    live = sub < count
    for block in range(rows // ZB):
        values = dot(forward, padded[block * ZB : block * ZB + 2 * ZB, :])
        own = values[:, :TILE]
        seen = in_ref[block * ZB // group : (block + 1) * ZB // group, 2 * group :, :].reshape(ZB, TILE)
        ratio[edge + block * ZB : edge + (block + 1) * ZB, :] = (seen.astype(F32) / own).astype(BF16)
        own = own.reshape(pairs, 8, TILE)
        more = values[:, TILE:].reshape(pairs, 8, TILE)
        first = jnp.where(sub < HALF, own, pltpu.roll(more, HALF, 1))
        second = jnp.where(sub < HALF, pltpu.roll(own, HALF, 1), more)
        both = jnp.stack([jnp.where(live, first, 0.0), jnp.where(live, second, 0.0)], axis=1)
        column_ref[block * planes : (block + 1) * planes] = both.reshape(planes, 8, TILE).astype(BF16)
    for block in range(rows // ZB):
        values = dot(adjoint, ratio[block * ZB : block * ZB + 2 * ZB, :]).astype(BF16)
        for plane in range(SLAB):
            back_ref[plane, block * part : (block + 1) * part, :] = values[plane * part : (plane + 1) * part]


def back_kernel(me_ref, mask_ref, px_ref, py_ref, table_ref, est_ref, in_ref, out_ref, stacked_x, stacked_y):
    half_xy = TAPS_XY // 2
    units = table_ref[0:1, :]
    row_x = units // 2
    slots = units.shape[1]
    here = row_x == iota((NX, slots), 0)
    cols = jnp.concatenate([in_ref[view] for view in range(VIEWS)], axis=1)
    tile_row = iota((NX, 1), 0) // TILE
    spread = []
    for t in range(2):
        found = dot(one_hot(here & (units % 2 == t)), cols)
        tissue = jnp.zeros((NX, 1), I32)
        for i in range(NX // TILE):
            tissue = jnp.where(tile_row == i, mask_ref[2 * i + t], tissue)
        spread.append(jnp.where(tissue > 0, found, 1.0).astype(BF16))
    for view in range(VIEWS):
        matrix_y = band(
            placed_taps(lambda m: py_ref[view, m], TAPS_XY, NY, lambda m: m - half_xy), NY, half_xy
        )
        stacked_x[:, view * NX : (view + 1) * NX] = band(
            placed_taps(lambda m: px_ref[view, m], TAPS_XY, NX, lambda m: half_xy - m), NX, half_xy
        )
        lanes = slice(view * TILE, (view + 1) * TILE)
        back_z = jnp.concatenate([spread[0][:, lanes], spread[1][:, lanes]], axis=1)
        stacked_y[view * NX : (view + 1) * NX, :] = dot(back_z, matrix_y).astype(BF16)
    summed = dot(stacked_x[...], stacked_y[...])
    out_ref[0] = (est_ref[0].astype(F32) * summed / VIEWS).astype(BF16)


def shards(estimate, measured, psf_x, psf_y, psf_z, tissue_mask, column_owner):
    smem = pl.BlockSpec(memory_space=pltpu.SMEM)
    vmem = pl.BlockSpec(memory_space=pltpu.VMEM)
    params = pltpu.CompilerParams(vmem_limit_bytes=VMEM_LIMIT)
    taps = lax.all_gather(jnp.concatenate([psf_x, psf_y], axis=1), "view", axis=0, tiled=True)
    slots = HALF * DEVS
    message, table, count = pl.pallas_call(
        pack_kernel,
        out_shape=(
            jax.ShapeDtypeStruct((DEVS, MSG, TILE), BF16),
            jax.ShapeDtypeStruct((8, slots), I32),
            jax.ShapeDtypeStruct((DEVS, TILE), I32),
        ),
        in_specs=[smem, smem, smem, vmem, vmem, vmem],
        out_specs=(vmem, vmem, vmem),
        scratch_shapes=[pltpu.VMEM((DEVS * MSG, TILE), F32)],
        compiler_params=params,
        name="pack",
    )(tissue_mask, psf_x, psf_y, column_owner.reshape(1, UNITS), estimate, measured)
    arrived = lax.all_to_all(message, "space", split_axis=0, concat_axis=0, tiled=True)
    rows = DEVS * SLAB * HALF
    space_index = lax.axis_index("space").astype(I32).reshape(1)
    view_index = lax.axis_index("view").astype(I32).reshape(1)
    column_blur, back = pl.pallas_call(
        z_kernel,
        out_shape=(
            jax.ShapeDtypeStruct((SLAB * DEVS, 2 * HALF, TILE), BF16),
            jax.ShapeDtypeStruct((VIEWS, slots, TILE), BF16),
        ),
        in_specs=[smem, smem, vmem, vmem],
        out_specs=(vmem, vmem),
        scratch_shapes=[
            pltpu.VMEM((rows + ZB, 2 * TILE), BF16),
            pltpu.VMEM((rows + ZB, TILE), BF16),
        ],
        compiler_params=params,
        name="zpair",
    )(space_index, psf_z, count, arrived)
    returned = lax.all_to_all(
        back.reshape(VIEWS * DEVS, HALF, TILE),
        ("view", "space"),
        split_axis=0,
        concat_axis=0,
        tiled=True,
    ).reshape(VIEWS, slots, TILE)
    updated = pl.pallas_call(
        back_kernel,
        grid_spec=pltpu.PrefetchScalarGridSpec(
            num_scalar_prefetch=1,
            grid=(1,),
            in_specs=[
                smem,
                smem,
                smem,
                pl.BlockSpec((8, slots), lambda i, me: (0, 0)),
                pl.BlockSpec((1, NX, NY), lambda i, me: (me[0], 0, 0)),
                pl.BlockSpec((VIEWS, slots, TILE), lambda i, me: (0, 0, 0)),
            ],
            out_specs=pl.BlockSpec((1, NX, NY), lambda i, me: (0, 0, 0)),
            scratch_shapes=[
                pltpu.VMEM((NX, VIEWS * NX), BF16),
                pltpu.VMEM((VIEWS * NX, NY), BF16),
            ],
        ),
        out_shape=jax.ShapeDtypeStruct((1, NX, NY), BF16),
        compiler_params=params,
        name="back",
    )(view_index, tissue_mask, taps[:, :TAPS_XY], taps[:, TAPS_XY:], table, estimate, returned)
    updated = lax.all_gather(updated, "view", axis=0, tiled=True)
    return updated, column_blur[None]


def solution(mesh):
    placed = (
        P("space", None, None),
        P("view", "space", None, None),
        P("view", None),
        P("view", None),
        P("view", None),
        P(),
        P(),
    )
    return jax.shard_map(
        shards,
        mesh=mesh,
        in_specs=placed,
        out_specs=(P("space", None, None), P("view", None, "space", None)),
        check_vma=False,
    )
```

time: 378 us -> 150 us (0.40)
  matrix products: 84.4 us -> 0 us
  other arithmetic: 60.1 us -> 0.08 us
  local copies, waits for them, and re-layouts: 58.8 us -> 7.46 us
  blocking collectives: 44 us -> 7.76 us
  Pallas kernels: 0 us -> 14.3 us
  waiting for transfers between devices: 89.2 us -> 75.6 us
  starting transfers between devices: 25.4 us -> 30 us
    dot_general x4 -> x0, matrix products: 84.4 us -> none  [the longest x1 42 us: shards(): jnp.einsum('kay,ab->kby', back_y, matrix_x, preferred_element_type=jnp.fl...]
    psum x1 -> x0, waiting for transfers between devices: 60.2 us -> none  [shards(): summed = lax.psum(back_x, 'view')]
    all_to_all x1 -> x0, blocking collectives: 44 us -> none  [shards(): lax.all_to_all(back_cols.reshape(full_depth, 1, capacity, TILE), 'space',...]
    gather x2 -> x0, other arithmetic: 43.9 us -> none  [the longest x1 43.9 us: kernel_matrix(): picked = jnp.take(rounded, jnp.clip(offset, 0, tap_values.shape[0] - 1))]
    scatter x3 -> x0, local copies, waits for them, and re-layouts: 32.4 us -> none  [the longest x2 28.1 us: shards(): back_units.at[:, slot_table, :]]
    all_to_all x2, waiting for transfers between devices: 29 us -> 54.9 us  [the longest x1 41 us: shards(): lax.all_to_all(message, 'space', split_axis=0, concat_axis=0, tiled=True)]
    all_gather x0 -> x1, waiting for transfers between devices: none -> 20.6 us  [shards(): updated = lax.all_gather(updated, 'view', axis=0, tiled=True)]
    pallas_call x0 -> x3, Pallas kernels: none -> 14.3 us  [the longest x1 7.6 us: shards(): pl.pallas_call(pack_kernel, out_shape=(jax.ShapeDtypeStruct((DEVS, MSG, T...]
  transfers between devices with their start and end apart: 3 -> 3, of which waited for: 2 -> 3; matrix products, arithmetic and copies ran while one was open for 14% -> 0% of each run, Pallas kernels for 0% -> 0%
where the time goes in v1:
time: 150 us; the launch traced here: 149 us
  waiting for transfers between devices  75.6 us (50%)
  starting transfers between devices  30 us (20%)
  Pallas kernels  14.3 us (10%)
  between operations  14.1 us (9%)
  blocking collectives  7.76 us (5%)
  local copies, waits for them, and re-layouts  7.46 us (5%)
    all_to_all x1, waiting for transfers between devices, shards(): lax.all_to_all(message, 'space', split_axis=0, concat_axis=0, tiled=True)  41 us
    all_gather x1, waiting for transfers between devices, shards(): updated = lax.all_gather(updated, 'view', axis=0, tiled=True)  20.6 us
    all_to_all x1, starting transfers between devices, shards(): lax.all_to_all(message, 'space', split_axis=0, concat_axis=0, tiled=True)  18.6 us
    all_to_all x1, waiting for transfers between devices, shards(): lax.all_to_all(back.reshape(VIEWS * DEVS, HALF, TILE), ('view', 'space'),...  13.9 us
    all_to_all x1, starting transfers between devices, shards(): lax.all_to_all(back.reshape(VIEWS * DEVS, HALF, TILE), ('view', 'space'),...  11.4 us
    all_gather x1, blocking collectives, shards(): lax.all_gather(jnp.concatenate([psf_x, psf_y], axis=1), 'view', axis=0, t...  7.76 us
    pallas_call x1, Pallas kernels, shards(): pl.pallas_call(pack_kernel, out_shape=(jax.ShapeDtypeStruct((DEVS, MSG, T...  7.6 us
    unnamed x23, local copies, waits for them, and re-layouts  7.38 us
  transfers between devices with their start and end apart: 3, of which 3 were waited for; matrix products, arithmetic and copies ran while one was open for 0% of the time, Pallas kernels for 0%

profile of v1, /device:TPU:1, one launch (start us, length us, event | category | flops | bytes accessed | tf_op | source)
XLA Modules:
  0.0 149.3 jit_solution(13684881702271619744)
XLA Ops:
  7.2 0.0 copy-start
  7.2 1.2 copy-done
  8.4 1.2 copy-done.2
  9.6 0.7 copy-done.3
  10.3 0.7 copy-done.4
  11.0 0.7 copy-done.7
  11.6 0.7 copy-done.9
  12.3 7.6 %pack.1 = (bf16[128,48,128]{2,1,0:T(8,128)(2,1)}, s32[8,512]{1,0:T(8,128)S(1)}, s32[128,128]{1,0:T(8,128)S(1)}) custom-call(s32[8]{0:T(128)S(1)} %copy-done.4, f32[1,31]{1,0:T(1,128)S(1)} %copy-done.9, f32[1,31]{1,0:T(1,128)S(1)} %copy-done.7, s32[1,1024]{1,0:T(1,128)S(1)} %bitcast.10, bf16[4,512,256]{2,1,0:T(8,128)(2,1)S(1)} %copy-done, ...), custom_call_target="tpu_custom_call" | custom-call | tf_op jit(solution)/shard_map/pack/pallas_call | solution.py:208
  19.9 18.6 %all-to-all-start = ((bf16[128,48,128]{2,1,0:T(8,128)(2,1)}), bf16[128,48,128]{2,1,0:T(8,128)(2,1)S(1)}, u32[]{:S(2)}, u32[]{:S(2)}) async-start(bf16[128,48,128]{2,1,0:T(8,128)(2,1)} %get-tuple-element.9), calls=%async_computation | async-start | bytes 3145728 | tf_op jit(solution)/shard_map/all_to_all | solution.py:221
  38.4 0.0 copy-start.8
  38.5 0.0 copy-start.1
  38.5 0.0 copy-start.5
  38.5 41.0 %all-to-all-done.in_ref = bf16[128,48,128]{2,1,0:T(8,128)(2,1)S(1)} async-done(((bf16[128,48,128]{2,1,0:T(8,128)(2,1)}), bf16[128,48,128]{2,1,0:T(8,128)(2,1)S(1)}, u32[]{:S(2)}, u32[]{:S(2)}) %all-to-all-start) | async-done | bytes 1572896 | tf_op jit(solution)/shard_map/all_to_all | solution.py:221
  79.5 2.9 %zpair.1 = (bf16[512,8,128]{2,1,0:T(8,128)(2,1)}, bf16[4,512,128]{2,1,0:T(8,128)(2,1)}) custom-call(s32[1]{0:T(128)} %bitcast.4.me_ref, f32[1,63]{1,0:T(1,128)S(1)} %copy-done.6, s32[128,128]{1,0:T(8,128)S(1)} %get-tuple-element.8.count_ref, bf16[128,48,128]{2,1,0:T(8,128)(2,1)S(1)} %all-to-all-done.in_ref), custom_call_target="tpu_custom_call" | custom-call | tf_op jit(solution)/shard_map/zpair/pallas_call | solution.py:225
  82.5 11.4 %all-to-all-start.1 = ((bf16[512,4,128]{2,1,0:T(4,128)(2,1)}), bf16[512,4,128]{2,1,0:T(4,128)(2,1)S(1)}, u32[]{:S(2)}, u32[]{:S(2)}) async-start(bf16[512,4,128]{2,1,0:T(4,128)(2,1)} %bitcast.5), calls=%async_computation.1 | async-start | bytes 1048576 | tf_op jit(solution)/shard_map/all_to_all | solution.py:240
  93.9 0.0 all-gather.3.cloned.1.call-start
  93.9 0.1 maximum_bitcast_fusion
  94.0 7.8 %all-gather = f32[4,1,62]{2,1,0:T(1,128)S(1)} all-gather(f32[1,1,62]{2,1,0:T(1,128)S(1)} %maximum_bitcast_fusion), channel_id=1, replica_groups=mesh['view'=4,'space'=128] {'view'}, dimensions={0}, use_global_device_ids=true | all-gather | bytes 1240 | tf_op jit(solution)/shard_map/all_gather | solution.py:206
  101.8 0.1 fusion
  101.8 13.9 %all-to-all-done.1 = bf16[512,4,128]{2,1,0:T(4,128)(2,1)S(1)} async-done(((bf16[512,4,128]{2,1,0:T(4,128)(2,1)}), bf16[512,4,128]{2,1,0:T(4,128)(2,1)S(1)}, u32[]{:S(2)}, u32[]{:S(2)}) %all-to-all-start.1) | async-done | bytes 524320 | tf_op jit(solution)/shard_map/all_to_all | solution.py:240
  115.7 3.8 %back.1 = bf16[1,512,256]{2,1,0:T(8,128)(2,1)} custom-call(s32[1]{0:T(128)} %bitcast.me_ref, s32[8]{0:T(128)S(1)} %copy-done.5, f32[4,31]{1,0:T(4,128)S(1)} %get-tuple-element.13.px_ref, f32[4,31]{1,0:T(4,128)S(1)} %get-tuple-element.12.py_ref, s32[8,512]{1,0:T(8,128)S(1)} %get-tuple-element.7.table_ref, bf16[4,512,256]{2,1,0:T(8,128)(2,1)S(1)} %copy-done.1, ...), custom_call_target="tpu_custom_call" | custom-call | tf_op jit(solution)/shard_map/back/pallas_call | solution.py:247
  119.5 0.0 all-gather.3.cloned.1.call-update
  119.5 20.6 %all-gather.3.cloned.1.call-done = bf16[4,512,256]{2,1,0:T(8,128)(2,1)} async-done(((bf16[1,512,256]{2,1,0:T(8,128)(2,1)}), bf16[4,512,256]{2,1,0:T(8,128)(2,1)}) %all-gather.3.cloned.1.call-update) | async-done | bytes 1048592 | tf_op jit(solution)/shard_map/all_gather | solution.py:270
  140.1 2.3 %copy.11 = bf16[4,512,256]{2,1,0:T(8,128)(2,1)} copy(bf16[4,512,256]{2,1,0:T(8,128)(2,1)} %all-gather.3.cloned.1.call-done) | data formatting | bytes 2097152
  (12 shorter events, 0.0 us)
Async XLA Ops:
  7.2 1.2 copy-start
  8.4 1.2 copy-start.2
  9.6 0.7 copy-start.3
  10.3 0.7 copy-start.4
  11.0 0.7 copy-start.7
  11.6 0.7 copy-start.9
  19.9 59.7 %copy-start.6 = (f32[1,63]{1,0:T(1,128)S(1)}, f32[1,63]{1,0:T(1,128)}, u32[]{:S(2)}) copy-start(f32[1,63]{1,0:T(1,128)} %pz_ref.1) | copy-start | bytes 760
  19.9 59.7 %all-to-all-start = ((bf16[128,48,128]{2,1,0:T(8,128)(2,1)}), bf16[128,48,128]{2,1,0:T(8,128)(2,1)S(1)}, u32[]{:S(2)}, u32[]{:S(2)}) async-start(bf16[128,48,128]{2,1,0:T(8,128)(2,1)} %get-tuple-element.9), calls=%async_computation | async-start | bytes 3145728 | tf_op jit(solution)/shard_map/all_to_all | solution.py:221
  38.4 55.5 %copy-start.8 = (f32[1,31]{1,0:T(1,128)S(1)}, f32[1,31]{1,0:T(1,128)}, u32[]{:S(2)}) copy-start(f32[1,31]{1,0:T(1,128)} %py_ref.1) | copy-start | bytes 376
  38.4 55.5 %copy-start.10 = (f32[1,31]{1,0:T(1,128)S(1)}, f32[1,31]{1,0:T(1,128)}, u32[]{:S(2)}) copy-start(f32[1,31]{1,0:T(1,128)} %px_ref.1) | copy-start | bytes 376
  38.5 77.3 %copy-start.1 = (bf16[4,512,256]{2,1,0:T(8,128)(2,1)S(1)}, bf16[4,512,256]{2,1,0:T(8,128)(2,1)}, u32[]{:S(2)}) copy-start(bf16[4,512,256]{2,1,0:T(8,128)(2,1)} %est_ref.3) | copy-start | bytes 3145732
  38.5 77.3 %copy-start.5 = (s32[8]{0:T(128)S(1)}, s32[8]{0:T(128)}, u32[]{:S(2)}) copy-start(s32[8]{0:T(128)} %mask_ref.3) | copy-start | bytes 100
  82.5 33.3 %all-to-all-start.1 = ((bf16[512,4,128]{2,1,0:T(4,128)(2,1)}), bf16[512,4,128]{2,1,0:T(4,128)(2,1)S(1)}, u32[]{:S(2)}, u32[]{:S(2)}) async-start(bf16[512,4,128]{2,1,0:T(4,128)(2,1)} %bitcast.5), calls=%async_computation.1 | async-start | bytes 1048576 | tf_op jit(solution)/shard_map/all_to_all | solution.py:240
  93.9 46.3 %all-gather.3.cloned.1.call-start = ((), (), s32[]{:S(2)}) async-start(), calls=%async_computation.2 | async-start | bytes 1310720 | tf_op jit(solution)/shard_map/all_gather | solution.py:270
Sparse Core Ops, SparseCore 0:
  119.6 20.4 all-gather.2

commit v2 on v1

v2 whole, which is shorter than its diff:
```python
import jax
import jax.numpy as jnp
from jax import lax
from jax.experimental import pallas as pl
from jax.experimental.pallas import tpu as pltpu
from jax.sharding import PartitionSpec as P

F32 = jnp.float32
BF16 = jnp.bfloat16
I32 = jnp.int32

VIEWS, DEVS = 4, 128
SLAB, NX, NY, TILE = 4, 512, 256, 128
UNITS = 1024
HALF = 4
MSG = 3 * SLAB * HALF
TAPS_XY, TAPS_Z = 31, 63
ZB = 256
PACK_LIMIT, LIMIT = 60, 24
OUT_PARTS = 4

SMEM = pl.BlockSpec(memory_space=pltpu.SMEM)
VMEM = pl.BlockSpec(memory_space=pltpu.VMEM)
ANY = pl.BlockSpec(memory_space=pl.ANY)


def shape(*dims, dtype=BF16):
    return jax.ShapeDtypeStruct(dims, dtype)


def iota(shape, dim):
    return lax.broadcasted_iota(I32, shape, dim)


def placed_taps(read, count, lanes, place):
    lane = iota((1, lanes), 1)
    total = read(0)
    for m in range(1, count):
        total = total + read(m)
    row = jnp.zeros((1, lanes), F32)
    for m in range(count):
        row = jnp.where(lane == place(m) % lanes, read(m), row)
    return (row / jnp.full((1, lanes), total, F32)).astype(BF16).astype(F32)


def rolled(row, rows):
    return pltpu.roll(
        jnp.broadcast_to(row, (rows, row.shape[1])), 0, 1, stride=1, stride_axis=0
    )


def band(row, n, half):
    distance = jnp.abs(iota((n, n), 1) - iota((n, n), 0))
    return jnp.where(distance <= half, rolled(row, n), 0.0).astype(BF16)


def dot(a, b, dims=((1,), (0,))):
    return lax.dot_general(a, b, (dims, ((), ())), preferred_element_type=F32)


def one_hot(condition):
    return jnp.where(condition, 1.0, 0.0).astype(BF16)


def slot_tables(mask_ref, owner_ref):
    device = iota((DEVS, ZB), 0)
    lane = iota((DEVS, ZB), 1)
    before_tri = one_hot(iota((ZB, ZB), 0) < iota((ZB, ZB), 1))
    count = jnp.zeros((DEVS, 1), F32)
    unit_of = [jnp.zeros((DEVS, 1), F32) for _ in range(2 * HALF)]
    for block in range(UNITS // ZB):
        tissue = jnp.where(lane % 2 == 0, mask_ref[2 * block], mask_ref[2 * block + 1])
        owner = owner_ref[0:1, block * ZB : (block + 1) * ZB]
        member = (owner == device) & (tissue > 0)
        before = dot(one_hot(member), before_tri) + count
        unit = (lane + block * ZB).astype(F32)
        for slot in range(2 * HALF):
            here = member & (before == float(slot))
            unit_of[slot] += jnp.sum(jnp.where(here, unit, 0.0), axis=1, keepdims=True)
        count += jnp.sum(jnp.where(member, 1.0, 0.0), axis=1, keepdims=True)
    over = jnp.maximum(count - HALF, 0.0)
    free = jnp.maximum(HALF - count, 0.0)
    lower = one_hot(iota((DEVS, DEVS), 1) < iota((DEVS, DEVS), 0))
    square = (DEVS, DEVS)
    starts = dot(
        lower,
        jnp.where(iota(square, 1) == 0, over, jnp.where(iota(square, 1) == 1, free, 0.0)).astype(BF16),
    )
    over_start, free_start = starts[:, 0:1], starts[:, 1:2]
    columns = jnp.zeros(square, F32)
    for i, column in enumerate([over_start, over, *unit_of[HALF:]]):
        columns = jnp.where(iota(square, 1) == i, column, columns)
    rows = columns.T
    balanced = []
    for slot in range(HALF):
        rank = free_start + (slot - count)
        filler = jnp.zeros((DEVS, 1), F32)
        for extra in range(HALF):
            match = (rows[0:1] + extra == rank) & (rows[1:2] > extra)
            filler += jnp.sum(jnp.where(match, rows[2 + extra : 3 + extra], 0.0), axis=1, keepdims=True)
        balanced.append(jnp.where(count > slot, unit_of[slot], filler))
    return balanced, unit_of[HALF:], count


def pack_kernel(
    mask_ref, px_ref, py_ref, owner_ref, est_hbm, meas_hbm, out_hbm, table_ref, count_ref,
    est_ref, meas_ref, wide, out_ref, est_sem, meas_sem, out_sem,
):
    est_copy = pltpu.make_async_copy(est_hbm, est_ref, est_sem)
    meas_copy = pltpu.make_async_copy(meas_hbm, meas_ref, meas_sem)
    est_copy.start()
    meas_copy.start()
    balanced, overflow, count = slot_tables(mask_ref, owner_ref)
    count_ref[...] = jnp.broadcast_to(count, (DEVS, TILE)).astype(I32)
    units = jnp.concatenate(balanced, axis=0).astype(I32)
    odd = units % 2 == 1
    slots = HALF * DEVS
    lane = iota((DEVS, slots), 1)
    along = jnp.zeros((DEVS, slots), F32)
    across = jnp.zeros((DEVS, slots), F32)
    for slot in range(HALF):
        mine = (lane // HALF == iota((DEVS, slots), 0)) & (lane % HALF == slot)
        along = jnp.where(mine, balanced[slot], along)
        mine = (lane % DEVS == iota((DEVS, slots), 0)) & (lane // DEVS == slot)
        across = jnp.where(mine, balanced[slot], across)
    table_ref[...] = jnp.broadcast_to(jnp.sum(along, axis=0, keepdims=True), (8, slots)).astype(I32)
    across = jnp.sum(across, axis=0, keepdims=True)
    past = jnp.concatenate(
        [jnp.where(count > HALF + i, overflow[i], -1.0) for i in range(HALF)], axis=0
    )
    again = one_hot(past == across)

    half_xy = TAPS_XY // 2
    matrix_x = band(placed_taps(lambda m: px_ref[0, m], TAPS_XY, NX, lambda m: m - half_xy), NX, half_xy)
    matrix_y = band(placed_taps(lambda m: py_ref[0, m], TAPS_XY, NY, lambda m: m - half_xy), NY, half_xy)
    pick = one_hot(units // 2 == iota((slots, NX), 1))
    picked_x = dot(pick, matrix_x).astype(BF16)
    est_copy.wait()
    narrow = []
    for plane in range(SLAB):
        along_x = dot(picked_x, est_ref[plane]).astype(BF16)
        blurred = dot(along_x, matrix_y, ((1,), (1,)))
        blurred = jnp.where(odd, blurred[:, TILE:], blurred[:, :TILE])
        narrow.append(blurred.astype(BF16))
        for slot in range(HALF):
            row = plane * HALF + slot
            wide[pl.ds(row, DEVS, stride=MSG), :] = blurred[slot * DEVS : (slot + 1) * DEVS]
    blurred = dot(again, jnp.concatenate(narrow, axis=1))
    for plane in range(SLAB):
        for slot in range(HALF):
            row = (SLAB + plane) * HALF + slot
            wide[pl.ds(row, DEVS, stride=MSG), :] = blurred[
                slot * DEVS : (slot + 1) * DEVS, plane * TILE : (plane + 1) * TILE
            ]
    meas_copy.wait()
    for plane in range(SLAB):
        seen = dot(pick, meas_ref[0, plane])
        seen = jnp.where(odd, seen[:, TILE:], seen[:, :TILE])
        for slot in range(HALF):
            row = (2 * SLAB + plane) * HALF + slot
            wide[pl.ds(row, DEVS, stride=MSG), :] = seen[slot * DEVS : (slot + 1) * DEVS]
    part = DEVS // OUT_PARTS
    copies = []
    for i in range(OUT_PARTS):
        here = pl.ds(i * part, part)
        out_ref[here] = wide[pl.ds(i * part * MSG, part * MSG), :].astype(BF16).reshape(part, MSG, TILE)
        copies.append(pltpu.make_async_copy(out_ref.at[here], out_hbm.at[here], out_sem.at[i]))
        copies[-1].start()
    for copy in copies:
        copy.wait()


def prep_kernel(pz_ref, taps_ref, table_ref, forward_ref, adjoint_ref, spread_ref, x_ref, y_ref):
    group = SLAB * HALF
    edge = ZB // 2
    half_z = TAPS_Z // 2
    near = edge - HALF * half_z
    far = edge + HALF * half_z
    forward_ref[...] = rolled(
        placed_taps(lambda m: pz_ref[0, m], TAPS_Z, 2 * ZB, lambda m: near + HALF * m), ZB
    ).astype(BF16)
    adjoint = rolled(
        placed_taps(lambda m: pz_ref[0, m], TAPS_Z, 2 * ZB, lambda m: far - HALF * m), ZB
    ).astype(BF16)
    r = iota((ZB, ZB), 0)
    part = ZB // SLAB
    source = r % part // HALF * group + r // part * HALF + r % HALF
    adjoint_ref[...] = dot(one_hot(iota((ZB, ZB), 1) == source), adjoint).astype(BF16)

    units = table_ref[0:1, :]
    here = units // 2 == iota((NX, units.shape[1]), 0)
    for t in range(2):
        spread_ref[t] = one_hot(here & (units % 2 == t))
    half_xy = TAPS_XY // 2
    for view in range(VIEWS):
        x_ref[:, view * NX : (view + 1) * NX] = band(
            placed_taps(lambda m: taps_ref[view, m], TAPS_XY, NX, lambda m: half_xy - m), NX, half_xy
        )
        y_ref[view] = band(
            placed_taps(lambda m: taps_ref[view, TAPS_XY + m], TAPS_XY, NY, lambda m: m - half_xy), NY, half_xy
        )


def z_kernel(forward_ref, adjoint_ref, in_ref, back_ref, padded, ratio):
    group = SLAB * HALF
    rows = DEVS * group
    edge = ZB // 2
    for ref in (padded, ratio):
        ref[0:edge, :] = jnp.zeros((edge, TILE), BF16)
        ref[edge + rows :, :] = jnp.zeros((edge, TILE), BF16)
    padded[edge : edge + rows, :] = in_ref[:, 0:group, :].reshape(rows, TILE)
    for block in range(rows // ZB):
        own = dot(forward_ref[...], padded[block * ZB : block * ZB + 2 * ZB, :])
        seen = in_ref[block * ZB // group : (block + 1) * ZB // group, 2 * group :, :].reshape(ZB, TILE)
        ratio[edge + block * ZB : edge + (block + 1) * ZB, :] = (seen.astype(F32) / own).astype(BF16)
    part = ZB // SLAB
    for block in range(rows // ZB):
        values = dot(adjoint_ref[...], ratio[block * ZB : block * ZB + 2 * ZB, :]).astype(BF16)
        for plane in range(SLAB):
            back_ref[plane, block * part : (block + 1) * part, :] = values[plane * part : (plane + 1) * part]


def column_kernel(me_ref, forward_ref, count_ref, in_ref, column_ref, padded):
    group = SLAB * HALF
    rows = DEVS * group
    edge = ZB // 2
    padded[0:edge, :] = jnp.zeros((edge, 2 * TILE), BF16)
    padded[edge + rows :, :] = jnp.zeros((edge, 2 * TILE), BF16)
    padded[edge : edge + rows, 0:TILE] = in_ref[:, 0:group, :].reshape(rows, TILE)
    padded[edge : edge + rows, TILE:] = in_ref[:, group : 2 * group, :].reshape(rows, TILE)
    count = count_ref[pl.ds(me_ref[0], 1), :].reshape(1, 1, TILE)
    planes = ZB // HALF
    pairs = planes // 2
    sub = iota((pairs, 8, TILE), 1)
    live = sub < count
    for block in range(rows // ZB):
        values = dot(forward_ref[...], padded[block * ZB : block * ZB + 2 * ZB, :])
        own = values[:, :TILE].reshape(pairs, 8, TILE)
        more = values[:, TILE:].reshape(pairs, 8, TILE)
        first = jnp.where(sub < HALF, own, pltpu.roll(more, HALF, 1))
        second = jnp.where(sub < HALF, pltpu.roll(own, HALF, 1), more)
        both = jnp.stack([jnp.where(live, first, 0.0), jnp.where(live, second, 0.0)], axis=1)
        column_ref[block * planes : (block + 1) * planes] = both.reshape(planes, 8, TILE).astype(BF16)


def back_kernel(me_ref, mask_ref, spread_ref, x_ref, y_ref, est_ref, in_ref, out_ref, stacked):
    cols = jnp.concatenate([in_ref[view] for view in range(VIEWS)], axis=1)
    tile_row = iota((NX, 1), 0) // TILE
    back_z = []
    for t in range(2):
        found = dot(spread_ref[t], cols)
        tissue = jnp.zeros((NX, 1), I32)
        for i in range(NX // TILE):
            tissue = jnp.where(tile_row == i, mask_ref[2 * i + t], tissue)
        back_z.append(jnp.where(tissue > 0, found, 1.0).astype(BF16))
    for view in range(VIEWS):
        lanes = slice(view * TILE, (view + 1) * TILE)
        one_view = jnp.concatenate([back_z[0][:, lanes], back_z[1][:, lanes]], axis=1)
        stacked[view * NX : (view + 1) * NX, :] = dot(one_view, y_ref[view]).astype(BF16)
    summed = dot(x_ref[...], stacked[...])
    updated = (est_ref[0].astype(F32) * summed / VIEWS).astype(BF16)
    for view in range(VIEWS):
        out_ref[view] = updated


def call(kernel, name, out_shape, in_specs, scratch, limit, flops=0, moved=0):
    return pl.pallas_call(
        kernel,
        out_shape=out_shape,
        in_specs=in_specs,
        out_specs=jax.tree.map(lambda s: ANY if name == "pack" and s.shape == (DEVS, MSG, TILE) else VMEM, out_shape),
        scratch_shapes=scratch,
        compiler_params=pltpu.CompilerParams(vmem_limit_bytes=limit * 1024 * 1024),
        cost_estimate=pl.CostEstimate(flops=flops, bytes_accessed=moved, transcendentals=0),
        name=name,
    )


def pack(estimate, measured, psf_x, psf_y, tissue_mask, column_owner):
    return call(
        pack_kernel,
        "pack",
        (shape(DEVS, MSG, TILE), shape(8, HALF * DEVS, dtype=I32), shape(DEVS, TILE, dtype=I32)),
        [SMEM, SMEM, SMEM, VMEM, ANY, ANY],
        [
            pltpu.VMEM((SLAB, NX, NY), BF16),
            pltpu.VMEM((1, SLAB, NX, NY), BF16),
            pltpu.VMEM((DEVS * MSG, TILE), F32),
            pltpu.VMEM((DEVS, MSG, TILE), BF16),
            pltpu.SemaphoreType.DMA,
            pltpu.SemaphoreType.DMA,
            pltpu.SemaphoreType.DMA((OUT_PARTS,)),
        ],
        PACK_LIMIT,
        flops=2_000_000_000,
        moved=4_000_000,
    )(tissue_mask, psf_x, psf_y, column_owner.reshape(1, UNITS), estimate, measured)


def prep(psf_z, taps, table):
    return call(
        prep_kernel,
        "prep",
        (
            shape(ZB, 2 * ZB),
            shape(ZB, 2 * ZB),
            shape(2, NX, HALF * DEVS),
            shape(NX, VIEWS * NX),
            shape(VIEWS, NY, NY),
        ),
        [SMEM, SMEM, VMEM],
        [],
        LIMIT,
        flops=1_000_000_000,
        moved=4_000_000,
    )(psf_z, taps, table)


def z_pair(forward, adjoint, arrived):
    rows = DEVS * SLAB * HALF
    return call(
        z_kernel,
        "zpair",
        shape(VIEWS, HALF * DEVS, TILE),
        [VMEM, VMEM, VMEM],
        [pltpu.VMEM((rows + ZB, TILE), BF16), pltpu.VMEM((rows + ZB, TILE), BF16)],
        LIMIT,
        flops=540_000_000,
        moved=3_000_000,
    )(forward, adjoint, arrived)


def column(space_index, forward, count, arrived):
    rows = DEVS * SLAB * HALF
    return call(
        column_kernel,
        "column",
        shape(SLAB * DEVS, 2 * HALF, TILE),
        [SMEM, VMEM, VMEM, VMEM],
        [pltpu.VMEM((rows + ZB, 2 * TILE), BF16)],
        LIMIT,
        flops=540_000_000,
        moved=3_000_000,
    )(space_index, forward, count, arrived)


def back(view_index, tissue_mask, spread, matrix_x, matrix_y, estimate, returned):
    whole = lambda *dims: pl.BlockSpec(dims, lambda i, me: (0,) * len(dims))
    return pl.pallas_call(
        back_kernel,
        grid_spec=pltpu.PrefetchScalarGridSpec(
            num_scalar_prefetch=1,
            grid=(1,),
            in_specs=[
                SMEM,
                whole(2, NX, HALF * DEVS),
                whole(NX, VIEWS * NX),
                whole(VIEWS, NY, NY),
                pl.BlockSpec((1, NX, NY), lambda i, me: (me[0], 0, 0)),
                whole(VIEWS, HALF * DEVS, TILE),
            ],
            out_specs=whole(VIEWS, NX, NY),
            scratch_shapes=[pltpu.VMEM((VIEWS * NX, NY), BF16)],
        ),
        out_shape=shape(VIEWS, NX, NY),
        compiler_params=pltpu.CompilerParams(vmem_limit_bytes=LIMIT * 1024 * 1024),
        cost_estimate=pl.CostEstimate(flops=1_400_000_000, bytes_accessed=5_000_000, transcendentals=0),
        name="back",
    )(view_index, tissue_mask, spread, matrix_x, matrix_y, estimate, returned)


def shards(estimate, measured, psf_x, psf_y, psf_z, tissue_mask, column_owner):
    message, table, count = pack(estimate, measured, psf_x, psf_y, tissue_mask, column_owner)
    arrived = lax.all_to_all(message, "space", split_axis=0, concat_axis=0, tiled=True)
    taps = lax.all_gather(jnp.concatenate([psf_x, psf_y], axis=1), "view", axis=0, tiled=True)
    forward, adjoint, spread, matrix_x, matrix_y = prep(psf_z, taps, table)
    space_index = lax.axis_index("space").astype(I32).reshape(1)
    view_index = lax.axis_index("view").astype(I32).reshape(1)
    sent = z_pair(forward, adjoint, arrived)
    returned = lax.all_to_all(
        sent.reshape(VIEWS * DEVS, HALF, TILE),
        ("view", "space"),
        split_axis=0,
        concat_axis=0,
        tiled=True,
    ).reshape(VIEWS, HALF * DEVS, TILE)
    column_blur = column(space_index, forward, count, arrived)
    updated = back(view_index, tissue_mask, spread, matrix_x, matrix_y, estimate, returned)
    updated = lax.all_to_all(updated, "view", split_axis=0, concat_axis=0, tiled=True)
    return updated, column_blur[None]


def solution(mesh):
    placed = (
        P("space", None, None),
        P("view", "space", None, None),
        P("view", None),
        P("view", None),
        P("view", None),
        P(),
        P(),
    )
    return jax.shard_map(
        shards,
        mesh=mesh,
        in_specs=placed,
        out_specs=(P("space", None, None), P("view", None, "space", None)),
        check_vma=False,
    )
```

time: 150 us -> 134 us (0.89)
  between operations: 14.1 us -> 0.76 us
  waiting for transfers between devices: 75.6 us -> 63.2 us
  Pallas kernels: 14.3 us -> 18.9 us
  starting transfers between devices: 30 us -> 33.6 us
    all_to_all x1 -> x2, waiting for transfers between devices: 13.9 us -> 34.9 us  [the longest x1 21.9 us: shards(): lax.all_to_all(sent.reshape(VIEWS * DEVS, HALF, TILE), ('view', 'space'),...]
    all_gather x1 -> x0, waiting for transfers between devices: 20.6 us -> none  [shards(): updated = lax.all_gather(updated, 'view', axis=0, tiled=True)]
    all_to_all x1, waiting for transfers between devices: 41 us -> 28.3 us  [shards(): lax.all_to_all(message, 'space', split_axis=0, concat_axis=0, tiled=True)]
    pallas_call x3 -> x5, Pallas kernels: 14.3 us -> 18.9 us  [the longest x1 9.69 us: pack(): call(pack_kernel, 'pack', (shape(DEVS, MSG, TILE), shape(8, HALF * DEVS,...]
    all_to_all x1 -> x2, starting transfers between devices: 11.4 us -> 15 us  [the longest x1 11.4 us: shards(): lax.all_to_all(sent.reshape(VIEWS * DEVS, HALF, TILE), ('view', 'space'),...]
    unnamed x23 -> x31, local copies, waits for them, and re-layouts: 7.38 us -> 8.8 us
  transfers between devices with their start and end apart: 3 -> 3, of which waited for: 3 -> 3; matrix products, arithmetic and copies ran while one was open for 0% -> 0% of each run, Pallas kernels for 0% -> 2%
where the time goes in v2:
time: 134 us
  waiting for transfers between devices  63.2 us (47%)
  starting transfers between devices  33.6 us (25%)
  Pallas kernels  18.9 us (14%)
  local copies, waits for them, and re-layouts  8.8 us (7%)
  blocking collectives  8.23 us (6%)
    all_to_all x1, waiting for transfers between devices, shards(): lax.all_to_all(message, 'space', split_axis=0, concat_axis=0, tiled=True)  28.3 us
    all_to_all x1, waiting for transfers between devices, shards(): lax.all_to_all(sent.reshape(VIEWS * DEVS, HALF, TILE), ('view', 'space'),...  21.9 us
    all_to_all x1, starting transfers between devices, shards(): lax.all_to_all(message, 'space', split_axis=0, concat_axis=0, tiled=True)  18.6 us
    all_to_all x1, waiting for transfers between devices, shards(): lax.all_to_all(updated, 'view', split_axis=0, concat_axis=0, tiled=True)  13 us
    all_to_all x1, starting transfers between devices, shards(): lax.all_to_all(sent.reshape(VIEWS * DEVS, HALF, TILE), ('view', 'space'),...  11.4 us
    pallas_call x1, Pallas kernels, pack(): call(pack_kernel, 'pack', (shape(DEVS, MSG, TILE), shape(8, HALF * DEVS,...  9.69 us
    unnamed x31, local copies, waits for them, and re-layouts  8.8 us
    all_gather x1, blocking collectives, shards(): lax.all_gather(jnp.concatenate([psf_x, psf_y], axis=1), 'view', axis=0, t...  8.23 us
  transfers between devices with their start and end apart: 3, of which 3 were waited for; matrix products, arithmetic and copies ran while one was open for 0% of the time, Pallas kernels for 2%

profile of v2, /device:TPU:1, one launch (start us, length us, event | category | flops | bytes accessed | tf_op | source)
XLA Modules:
  0.0 133.5 jit_solution(4225596365789233060)
XLA Ops:
  0.6 9.7 %pack.1 = (bf16[128,48,128]{2,1,0:T(8,128)(2,1)}, s32[8,512]{1,0:T(8,128)}, s32[128,128]{1,0:T(8,128)}) custom-call(s32[8]{0:T(128)} %mask_ref.3, f32[1,31]{1,0:T(1,128)} %px_ref.1, f32[1,31]{1,0:T(1,128)} %py_ref.1, s32[1,1024]{1,0:T(1,128)} %bitcast.12, bf16[4,512,256]{2,1,0:T(8,128)(2,1)} %est_ref.1, bf16[1,4,512,256]{3,2,1,0:T(8,128)(2,1)} %meas_hbm.1), custom_call_target="tpu_custom_call" | custom-call | flops 2000000000 | bytes 4000000 | tf_op jit(solution)/shard_map/pack/pallas_call | solution.py:280
  10.3 0.0 copy-start.13
  10.3 0.0 copy-start.14
  10.4 0.0 copy-start.11
  10.4 18.6 %all-to-all-start = ((bf16[128,48,128]{2,1,0:T(8,128)(2,1)}), bf16[128,48,128]{2,1,0:T(8,128)(2,1)S(1)}, u32[]{:S(2)}, u32[]{:S(2)}) async-start(bf16[128,48,128]{2,1,0:T(8,128)(2,1)} %get-tuple-element.16), calls=%async_computation | async-start | bytes 3145728 | tf_op jit(solution)/shard_map/all_to_all | solution.py:374
  29.0 0.1 maximum_bitcast_fusion
  29.0 8.2 %all-gather = f32[4,1,62]{2,1,0:T(1,128)S(1)} all-gather(f32[1,1,62]{2,1,0:T(1,128)S(1)} %maximum_bitcast_fusion), channel_id=1, replica_groups=mesh['view'=4,'space'=128] {'view'}, dimensions={0}, use_global_device_ids=true | all-gather | bytes 1240 | tf_op jit(solution)/shard_map/all_gather | solution.py:375
  37.3 1.5 %prep.1 = (bf16[256,512]{1,0:T(8,128)(2,1)S(1)}, bf16[256,512]{1,0:T(8,128)(2,1)S(1)}, bf16[2,512,512]{2,1,0:T(8,128)(2,1)S(1)}, bf16[512,2048]{1,0:T(8,128)(2,1)S(1)}, bf16[4,256,256]{2,1,0:T(8,128)(2,1)S(1)}) custom-call(f32[1,63]{1,0:T(1,128)S(1)} %copy-done.11, f32[4,62]{1,0:T(4,128)S(1)} %bitcast.10, s32[8,512]{1,0:T(8,128)S(1)} %copy-done.12), custom_call_target="tpu_custom_call" | custom-call | flops 1000000000 | bytes 4000000 | tf_op jit(solution)/shard_map/prep/pallas_call | solution.py:301
  38.8 1.3 copy-done
  40.1 1.0 copy-done.3
  41.1 0.7 copy-done.7
  41.7 28.3 %all-to-all-done.in_ref = bf16[128,48,128]{2,1,0:T(8,128)(2,1)S(1)} async-done(((bf16[128,48,128]{2,1,0:T(8,128)(2,1)}), bf16[128,48,128]{2,1,0:T(8,128)(2,1)S(1)}, u32[]{:S(2)}, u32[]{:S(2)}) %all-to-all-start) | async-done | bytes 1572896 | tf_op jit(solution)/shard_map/all_to_all | solution.py:374
  70.0 0.9 copy-done.8
  71.0 2.1 %zpair.1 = bf16[4,512,128]{2,1,0:T(8,128)(2,1)} custom-call(bf16[256,512]{1,0:T(8,128)(2,1)S(1)} %get-tuple-element.14.forward_ref, bf16[256,512]{1,0:T(8,128)(2,1)S(1)} %copy-done.8, bf16[128,48,128]{2,1,0:T(8,128)(2,1)S(1)} %all-to-all-done.in_ref), custom_call_target="tpu_custom_call" | custom-call | flops 540000000 | bytes 3000000 | tf_op jit(solution)/shard_map/zpair/pallas_call | solution.py:321
  73.1 11.4 %all-to-all-start.1 = ((bf16[512,4,128]{2,1,0:T(4,128)(2,1)}), bf16[512,4,128]{2,1,0:T(4,128)(2,1)S(1)}, u32[]{:S(2)}, u32[]{:S(2)}) async-start(bf16[512,4,128]{2,1,0:T(4,128)(2,1)} %bitcast.4), calls=%async_computation.1 | async-start | bytes 1048576 | tf_op jit(solution)/shard_map/all_to_all | solution.py:380
  84.5 21.9 %all-to-all-done.1 = bf16[512,4,128]{2,1,0:T(4,128)(2,1)S(1)} async-done(((bf16[512,4,128]{2,1,0:T(4,128)(2,1)}), bf16[512,4,128]{2,1,0:T(4,128)(2,1)S(1)}, u32[]{:S(2)}, u32[]{:S(2)}) %all-to-all-start.1) | async-done | bytes 524320 | tf_op jit(solution)/shard_map/all_to_all | solution.py:380
  106.3 1.6 %copy-done.1 = bf16[512,2048]{1,0:T(8,128)(2,1)S(1)} copy-done((bf16[512,2048]{1,0:T(8,128)(2,1)S(1)}, bf16[512,2048]{1,0:T(8,128)(2,1)}, u32[]{:S(2)}) %copy-start.1) | copy-done | bytes 2097176
  107.9 1.2 copy-done.4
  109.1 1.0 copy-done.6
  110.2 4.0 %back.1 = bf16[4,512,256]{2,1,0:T(8,128)(2,1)} custom-call(s32[1]{0:T(128)} %bitcast.me_ref, s32[8]{0:T(128)S(1)} %copy-done.10, bf16[2,512,512]{2,1,0:T(8,128)(2,1)S(1)} %copy-done.4, bf16[512,2048]{1,0:T(8,128)(2,1)S(1)} %copy-done.1, bf16[4,256,256]{2,1,0:T(8,128)(2,1)S(1)} %copy-done.6, bf16[4,512,256]{2,1,0:T(8,128)(2,1)S(1)} %copy-done.2, ...), custom_call_target="tpu_custom_call" | custom-call | flops 1400000000 | bytes 5000000 | tf_op jit(solution)/shard_map/back/pallas_call | solution.py:349
  114.2 3.6 %all-to-all-start.2 = ((bf16[4,512,256]{2,1,0:T(8,128)(2,1)}), bf16[4,512,256]{2,1,0:T(8,128)(2,1)S(1)}, u32[]{:S(2)}, u32[]{:S(2)}) async-start(bf16[4,512,256]{2,1,0:T(8,128)(2,1)} %back.1), calls=%async_computation.2 | async-start | bytes 2097152 | tf_op jit(solution)/shard_map/all_to_all | solution.py:389
  117.8 1.7 %column.1 = bf16[512,8,128]{2,1,0:T(8,128)(2,1)} custom-call(s32[1]{0:T(128)} %bitcast.6.me_ref, bf16[256,512]{1,0:T(8,128)(2,1)S(1)} %get-tuple-element.14.forward_ref, s32[128,128]{1,0:T(8,128)S(1)} %copy-done.9, bf16[128,48,128]{2,1,0:T(8,128)(2,1)S(1)} %all-to-all-done.in_ref), custom_call_target="tpu_custom_call" | custom-call | flops 540000000 | bytes 3000000 | tf_op jit(solution)/shard_map/column/pallas_call | solution.py:335
  119.5 13.0 %all-to-all-done.2 = bf16[4,512,256]{2,1,0:T(8,128)(2,1)S(1)} async-done(((bf16[4,512,256]{2,1,0:T(8,128)(2,1)}), bf16[4,512,256]{2,1,0:T(8,128)(2,1)S(1)}, u32[]{:S(2)}, u32[]{:S(2)}) %all-to-all-start.2) | async-done | bytes 1048608 | tf_op jit(solution)/shard_map/all_to_all | solution.py:389
  132.6 1.0 copy.11
  (20 shorter events, 0.0 us)
Async XLA Ops:
  10.3 18.6 %copy-start.13 = (f32[1,31]{1,0:T(1,128)S(1)}, f32[1,31]{1,0:T(1,128)}, u32[]{:S(2)}) copy-start(f32[1,31]{1,0:T(1,128)} %py_ref.1) | copy-start | bytes 376
  10.3 18.6 %copy-start.14 = (f32[1,31]{1,0:T(1,128)S(1)}, f32[1,31]{1,0:T(1,128)}, u32[]{:S(2)}) copy-start(f32[1,31]{1,0:T(1,128)} %px_ref.1) | copy-start | bytes 376
  10.4 26.9 %copy-start.11 = (f32[1,63]{1,0:T(1,128)S(1)}, f32[1,63]{1,0:T(1,128)}, u32[]{:S(2)}) copy-start(f32[1,63]{1,0:T(1,128)} %pz_ref.1) | copy-start | bytes 760
  10.4 26.9 %copy-start.12 = (s32[8,512]{1,0:T(8,128)S(1)}, s32[8,512]{1,0:T(8,128)}, u32[]{:S(2)}) copy-start(s32[8,512]{1,0:T(8,128)} %get-tuple-element.10.table_ref) | copy-start | bytes 49156
  10.4 59.7 %all-to-all-start = ((bf16[128,48,128]{2,1,0:T(8,128)(2,1)}), bf16[128,48,128]{2,1,0:T(8,128)(2,1)S(1)}, u32[]{:S(2)}, u32[]{:S(2)}) async-start(bf16[128,48,128]{2,1,0:T(8,128)(2,1)} %get-tuple-element.16), calls=%async_computation | async-start | bytes 3145728 | tf_op jit(solution)/shard_map/all_to_all | solution.py:374
  38.8 1.3 copy-start
  40.1 1.0 copy-start.3
  41.1 0.7 copy-start.7
  41.7 31.3 %copy-start.5 = (bf16[4,256,256]{2,1,0:T(8,128)(2,1)}, bf16[4,256,256]{2,1,0:T(8,128)(2,1)S(1)}, u32[]{:S(2)}) copy-start(bf16[4,256,256]{2,1,0:T(8,128)(2,1)S(1)} %get-tuple-element.13.y_ref) | copy-start | bytes 1572868
  70.0 1.0 copy-start.8
  71.0 35.3 %copy-start.2 = (bf16[4,512,256]{2,1,0:T(8,128)(2,1)S(1)}, bf16[4,512,256]{2,1,0:T(8,128)(2,1)}, u32[]{:S(2)}) copy-start(bf16[4,512,256]{2,1,0:T(8,128)(2,1)} %est_ref.1) | copy-start | bytes 3145732
  71.0 35.3 %copy-start.10 = (s32[8]{0:T(128)S(1)}, s32[8]{0:T(128)}, u32[]{:S(2)}) copy-start(s32[8]{0:T(128)} %mask_ref.3) | copy-start | bytes 100
  73.1 33.3 %all-to-all-start.1 = ((bf16[512,4,128]{2,1,0:T(4,128)(2,1)}), bf16[512,4,128]{2,1,0:T(4,128)(2,1)S(1)}, u32[]{:S(2)}, u32[]{:S(2)}) async-start(bf16[512,4,128]{2,1,0:T(4,128)(2,1)} %bitcast.4), calls=%async_computation.1 | async-start | bytes 1048576 | tf_op jit(solution)/shard_map/all_to_all | solution.py:380
  106.3 1.6 %copy-start.1 = (bf16[512,2048]{1,0:T(8,128)(2,1)S(1)}, bf16[512,2048]{1,0:T(8,128)(2,1)}, u32[]{:S(2)}) copy-start(bf16[512,2048]{1,0:T(8,128)(2,1)} %copy-done) | copy-start | bytes 6291460
  107.9 1.2 copy-start.4
  109.1 1.0 copy-start.6
  114.2 3.7 %copy-start.9 = (s32[128,128]{1,0:T(8,128)S(1)}, s32[128,128]{1,0:T(8,128)}, u32[]{:S(2)}) copy-start(s32[128,128]{1,0:T(8,128)} %get-tuple-element.17.count_ref) | copy-start | bytes 196612
  114.2 18.4 %all-to-all-start.2 = ((bf16[4,512,256]{2,1,0:T(8,128)(2,1)}), bf16[4,512,256]{2,1,0:T(8,128)(2,1)S(1)}, u32[]{:S(2)}, u32[]{:S(2)}) async-start(bf16[4,512,256]{2,1,0:T(8,128)(2,1)} %back.1), calls=%async_computation.2 | async-start | bytes 2097152 | tf_op jit(solution)/shard_map/all_to_all | solution.py:389

commit v3 on v2

--- a/solution.py
+++ b/solution.py
@@ -16,12 +16,14 @@
 MSG = 3 * SLAB * HALF
 TAPS_XY, TAPS_Z = 31, 63
 ZB = 256
-PACK_LIMIT, LIMIT = 60, 24
+XB = 128
+WIDE_LIMIT, LIMIT = 60, 24
 OUT_PARTS = 4
 
 SMEM = pl.BlockSpec(memory_space=pltpu.SMEM)
 VMEM = pl.BlockSpec(memory_space=pltpu.VMEM)
 ANY = pl.BlockSpec(memory_space=pl.ANY)
+HBM = pl.BlockSpec(memory_space=pltpu.HBM)
 
 
 def shape(*dims, dtype=BF16):
@@ -170,7 +172,7 @@
         copy.wait()
 
 
-def prep_kernel(pz_ref, taps_ref, table_ref, forward_ref, adjoint_ref, spread_ref, x_ref, y_ref):
+def prep_kernel(pz_ref, px_ref, py_ref, forward_ref, adjoint_ref, rows_ref):
     group = SLAB * HALF
     edge = ZB // 2
     half_z = TAPS_Z // 2
@@ -186,22 +188,21 @@
     part = ZB // SLAB
     source = r % part // HALF * group + r // part * HALF + r % HALF
     adjoint_ref[...] = dot(one_hot(iota((ZB, ZB), 1) == source), adjoint).astype(BF16)
-
-    units = table_ref[0:1, :]
-    here = units // 2 == iota((NX, units.shape[1]), 0)
-    for t in range(2):
-        spread_ref[t] = one_hot(here & (units % 2 == t))
     half_xy = TAPS_XY // 2
     for view in range(VIEWS):
-        x_ref[:, view * NX : (view + 1) * NX] = band(
-            placed_taps(lambda m: taps_ref[view, m], TAPS_XY, NX, lambda m: half_xy - m), NX, half_xy
+        rows_ref[view : view + 1, :] = placed_taps(
+            lambda m: px_ref[view, m], TAPS_XY, 2 * XB, lambda m: XB // 2 + half_xy - m
         )
-        y_ref[view] = band(
-            placed_taps(lambda m: taps_ref[view, TAPS_XY + m], TAPS_XY, NY, lambda m: m - half_xy), NY, half_xy
+        rows_ref[VIEWS + view : VIEWS + view + 1, :] = placed_taps(
+            lambda m: py_ref[view, m], TAPS_XY, NY, lambda m: m - half_xy
         )
 
 
-def z_kernel(forward_ref, adjoint_ref, in_ref, back_ref, padded, ratio):
+def z_kernel(forward_hbm, adjoint_hbm, in_ref, back_ref, forward_ref, adjoint_ref, padded, ratio, sems):
+    forward_copy = pltpu.make_async_copy(forward_hbm, forward_ref, sems.at[0])
+    adjoint_copy = pltpu.make_async_copy(adjoint_hbm, adjoint_ref, sems.at[1])
+    forward_copy.start()
+    adjoint_copy.start()
     group = SLAB * HALF
     rows = DEVS * group
     edge = ZB // 2
@@ -209,11 +210,13 @@
         ref[0:edge, :] = jnp.zeros((edge, TILE), BF16)
         ref[edge + rows :, :] = jnp.zeros((edge, TILE), BF16)
     padded[edge : edge + rows, :] = in_ref[:, 0:group, :].reshape(rows, TILE)
+    forward_copy.wait()
     for block in range(rows // ZB):
         own = dot(forward_ref[...], padded[block * ZB : block * ZB + 2 * ZB, :])
         seen = in_ref[block * ZB // group : (block + 1) * ZB // group, 2 * group :, :].reshape(ZB, TILE)
         ratio[edge + block * ZB : edge + (block + 1) * ZB, :] = (seen.astype(F32) / own).astype(BF16)
     part = ZB // SLAB
+    adjoint_copy.wait()
     for block in range(rows // ZB):
         values = dot(adjoint_ref[...], ratio[block * ZB : block * ZB + 2 * ZB, :]).astype(BF16)
         for plane in range(SLAB):
@@ -243,32 +246,56 @@
         column_ref[block * planes : (block + 1) * planes] = both.reshape(planes, 8, TILE).astype(BF16)
 
 
-def back_kernel(me_ref, mask_ref, spread_ref, x_ref, y_ref, est_ref, in_ref, out_ref, stacked):
+def back_kernel(
+    me_ref, mask_ref, table_ref, rows_ref, in_ref, est_hbm, out_hbm,
+    est_ref, padded, out_ref, est_sem, out_sems,
+):
+    est_copy = pltpu.make_async_copy(est_hbm.at[me_ref[0]], est_ref, est_sem)
+    est_copy.start()
+    edge = XB // 2
     cols = jnp.concatenate([in_ref[view] for view in range(VIEWS)], axis=1)
+    units = table_ref[0:1, :]
+    here = units // 2 == iota((NX, HALF * DEVS), 0)
     tile_row = iota((NX, 1), 0) // TILE
     back_z = []
     for t in range(2):
-        found = dot(spread_ref[t], cols)
+        found = dot(one_hot(here & (units % 2 == t)), cols)
         tissue = jnp.zeros((NX, 1), I32)
         for i in range(NX // TILE):
             tissue = jnp.where(tile_row == i, mask_ref[2 * i + t], tissue)
         back_z.append(jnp.where(tissue > 0, found, 1.0).astype(BF16))
+    bands = []
     for view in range(VIEWS):
+        bands.append(rolled(rows_ref[view : view + 1, :], XB).astype(BF16))
+        matrix_y = band(rows_ref[VIEWS + view : VIEWS + view + 1, :], NY, TAPS_XY // 2)
         lanes = slice(view * TILE, (view + 1) * TILE)
         one_view = jnp.concatenate([back_z[0][:, lanes], back_z[1][:, lanes]], axis=1)
-        stacked[view * NX : (view + 1) * NX, :] = dot(one_view, y_ref[view]).astype(BF16)
-    summed = dot(x_ref[...], stacked[...])
-    updated = (est_ref[0].astype(F32) * summed / VIEWS).astype(BF16)
-    for view in range(VIEWS):
-        out_ref[view] = updated
-
-
-def call(kernel, name, out_shape, in_specs, scratch, limit, flops=0, moved=0):
+        padded[view, 0:edge, :] = jnp.zeros((edge, NY), BF16)
+        padded[view, edge + NX :, :] = jnp.zeros((edge, NY), BF16)
+        padded[view, edge : edge + NX, :] = dot(one_view, matrix_y).astype(BF16)
+    est_copy.wait()
+    writes = []
+    for block in range(NX // XB):
+        here = pl.ds(block * XB, XB)
+        summed = jnp.zeros((XB, NY), F32)
+        for view in range(VIEWS):
+            summed += dot(bands[view], padded[view, block * XB : block * XB + 2 * XB, :])
+        out_ref[here, :] = (est_ref[here, :].astype(F32) * summed / VIEWS).astype(BF16)
+        for view in range(VIEWS):
+            writes.append(
+                pltpu.make_async_copy(out_ref.at[here, :], out_hbm.at[view, here, :], out_sems.at[block, view])
+            )
+            writes[-1].start()
+    for write in writes:
+        write.wait()
+
+
+def call(kernel, name, out_shape, in_specs, out_specs, scratch, limit, flops, moved):
     return pl.pallas_call(
         kernel,
         out_shape=out_shape,
         in_specs=in_specs,
-        out_specs=jax.tree.map(lambda s: ANY if name == "pack" and s.shape == (DEVS, MSG, TILE) else VMEM, out_shape),
+        out_specs=out_specs,
         scratch_shapes=scratch,
         compiler_params=pltpu.CompilerParams(vmem_limit_bytes=limit * 1024 * 1024),
         cost_estimate=pl.CostEstimate(flops=flops, bytes_accessed=moved, transcendentals=0),
@@ -282,6 +309,7 @@
         "pack",
         (shape(DEVS, MSG, TILE), shape(8, HALF * DEVS, dtype=I32), shape(DEVS, TILE, dtype=I32)),
         [SMEM, SMEM, SMEM, VMEM, ANY, ANY],
+        (ANY, VMEM, VMEM),
         [
             pltpu.VMEM((SLAB, NX, NY), BF16),
             pltpu.VMEM((1, SLAB, NX, NY), BF16),
@@ -291,29 +319,24 @@
             pltpu.SemaphoreType.DMA,
             pltpu.SemaphoreType.DMA((OUT_PARTS,)),
         ],
-        PACK_LIMIT,
+        WIDE_LIMIT,
         flops=2_000_000_000,
         moved=4_000_000,
     )(tissue_mask, psf_x, psf_y, column_owner.reshape(1, UNITS), estimate, measured)
 
 
-def prep(psf_z, taps, table):
+def prep(psf_z, taps_x, taps_y):
     return call(
         prep_kernel,
         "prep",
-        (
-            shape(ZB, 2 * ZB),
-            shape(ZB, 2 * ZB),
-            shape(2, NX, HALF * DEVS),
-            shape(NX, VIEWS * NX),
-            shape(VIEWS, NY, NY),
-        ),
-        [SMEM, SMEM, VMEM],
+        (shape(ZB, 2 * ZB), shape(ZB, 2 * ZB), shape(2 * VIEWS, NY, dtype=F32)),
+        [SMEM, SMEM, SMEM],
+        (VMEM, VMEM, VMEM),
         [],
         LIMIT,
         flops=1_000_000_000,
         moved=4_000_000,
-    )(psf_z, taps, table)
+    )(psf_z, taps_x, taps_y)
 
 
 def z_pair(forward, adjoint, arrived):
@@ -322,8 +345,15 @@
         z_kernel,
         "zpair",
         shape(VIEWS, HALF * DEVS, TILE),
-        [VMEM, VMEM, VMEM],
-        [pltpu.VMEM((rows + ZB, TILE), BF16), pltpu.VMEM((rows + ZB, TILE), BF16)],
+        [HBM, HBM, VMEM],
+        VMEM,
+        [
+            pltpu.VMEM((ZB, 2 * ZB), BF16),
+            pltpu.VMEM((ZB, 2 * ZB), BF16),
+            pltpu.VMEM((rows + ZB, TILE), BF16),
+            pltpu.VMEM((rows + ZB, TILE), BF16),
+            pltpu.SemaphoreType.DMA((2,)),
+        ],
         LIMIT,
         flops=540_000_000,
         moved=3_000_000,
@@ -337,43 +367,39 @@
         "column",
         shape(SLAB * DEVS, 2 * HALF, TILE),
         [SMEM, VMEM, VMEM, VMEM],
+        VMEM,
         [pltpu.VMEM((rows + ZB, 2 * TILE), BF16)],
-        LIMIT,
+        WIDE_LIMIT,
         flops=540_000_000,
         moved=3_000_000,
     )(space_index, forward, count, arrived)
 
 
-def back(view_index, tissue_mask, spread, matrix_x, matrix_y, estimate, returned):
-    whole = lambda *dims: pl.BlockSpec(dims, lambda i, me: (0,) * len(dims))
-    return pl.pallas_call(
+def back(view_index, tissue_mask, table, rows, returned, estimate):
+    return call(
         back_kernel,
-        grid_spec=pltpu.PrefetchScalarGridSpec(
-            num_scalar_prefetch=1,
-            grid=(1,),
-            in_specs=[
-                SMEM,
-                whole(2, NX, HALF * DEVS),
-                whole(NX, VIEWS * NX),
-                whole(VIEWS, NY, NY),
-                pl.BlockSpec((1, NX, NY), lambda i, me: (me[0], 0, 0)),
-                whole(VIEWS, HALF * DEVS, TILE),
-            ],
-            out_specs=whole(VIEWS, NX, NY),
-            scratch_shapes=[pltpu.VMEM((VIEWS * NX, NY), BF16)],
-        ),
-        out_shape=shape(VIEWS, NX, NY),
-        compiler_params=pltpu.CompilerParams(vmem_limit_bytes=LIMIT * 1024 * 1024),
-        cost_estimate=pl.CostEstimate(flops=1_400_000_000, bytes_accessed=5_000_000, transcendentals=0),
-        name="back",
-    )(view_index, tissue_mask, spread, matrix_x, matrix_y, estimate, returned)
+        "back",
+        shape(VIEWS, NX, NY),
+        [SMEM, SMEM, VMEM, VMEM, VMEM, HBM],
+        HBM,
+        [
+            pltpu.VMEM((NX, NY), BF16),
+            pltpu.VMEM((VIEWS, NX + XB, NY), BF16),
+            pltpu.VMEM((NX, NY), BF16),
+            pltpu.SemaphoreType.DMA,
+            pltpu.SemaphoreType.DMA((NX // XB, VIEWS)),
+        ],
+        LIMIT,
+        flops=1_400_000_000,
+        moved=5_000_000,
+    )(view_index, tissue_mask, table, rows, returned, estimate)
 
 
 def shards(estimate, measured, psf_x, psf_y, psf_z, tissue_mask, column_owner):
     message, table, count = pack(estimate, measured, psf_x, psf_y, tissue_mask, column_owner)
     arrived = lax.all_to_all(message, "space", split_axis=0, concat_axis=0, tiled=True)
     taps = lax.all_gather(jnp.concatenate([psf_x, psf_y], axis=1), "view", axis=0, tiled=True)
-    forward, adjoint, spread, matrix_x, matrix_y = prep(psf_z, taps, table)
+    forward, adjoint, rows = prep(psf_z, taps[:, :TAPS_XY], taps[:, TAPS_XY:])
     space_index = lax.axis_index("space").astype(I32).reshape(1)
     view_index = lax.axis_index("view").astype(I32).reshape(1)
     sent = z_pair(forward, adjoint, arrived)
@@ -385,7 +411,7 @@
         tiled=True,
     ).reshape(VIEWS, HALF * DEVS, TILE)
     column_blur = column(space_index, forward, count, arrived)
-    updated = back(view_index, tissue_mask, spread, matrix_x, matrix_y, estimate, returned)
+    updated = back(view_index, tissue_mask, table, rows, returned, estimate)
     updated = lax.all_to_all(updated, "view", split_axis=0, concat_axis=0, tiled=True)
     return updated, column_blur[None]
 

time: 134 us -> 128 us (0.955)
  local copies, waits for them, and re-layouts: 8.8 us -> 1.08 us
  waiting for transfers between devices: 63.2 us -> 64.9 us
    unnamed x31 -> x17, local copies, waits for them, and re-layouts: 8.8 us -> 1.01 us
    all_to_all x1, waiting for transfers between devices: 28.3 us -> 31.6 us  [shards(): lax.all_to_all(message, 'space', split_axis=0, concat_axis=0, tiled=True)]
    all_to_all x1, waiting for transfers between devices: 13 us -> 11.4 us  [shards(): lax.all_to_all(updated, 'view', split_axis=0, concat_axis=0, tiled=True)]
    pallas_call x1, Pallas kernels: 1.72 us -> 3.25 us  [column(): call(column_kernel, 'column', shape(SLAB * DEVS, 2 * HALF, TILE), [SMEM,...]
  transfers between devices with their start and end apart: 3 -> 3, of which waited for: 3 -> 3; matrix products, arithmetic and copies ran while one was open for 0% -> 0% of each run, Pallas kernels for 2% -> 3%
where the time goes in v3:
time: 128 us
  waiting for transfers between devices  64.9 us (51%)
  starting transfers between devices  33.5 us (26%)
  Pallas kernels  19.4 us (15%)
  blocking collectives  8.22 us (6%)
    all_to_all x1, waiting for transfers between devices, shards(): lax.all_to_all(message, 'space', split_axis=0, concat_axis=0, tiled=True)  31.6 us
    all_to_all x1, waiting for transfers between devices, shards(): lax.all_to_all(sent.reshape(VIEWS * DEVS, HALF, TILE), ('view', 'space'),...  21.9 us
    all_to_all x1, starting transfers between devices, shards(): lax.all_to_all(message, 'space', split_axis=0, concat_axis=0, tiled=True)  18.6 us
    all_to_all x1, waiting for transfers between devices, shards(): lax.all_to_all(updated, 'view', split_axis=0, concat_axis=0, tiled=True)  11.4 us
    all_to_all x1, starting transfers between devices, shards(): lax.all_to_all(sent.reshape(VIEWS * DEVS, HALF, TILE), ('view', 'space'),...  11.4 us
    pallas_call x1, Pallas kernels, pack(): call(pack_kernel, 'pack', (shape(DEVS, MSG, TILE), shape(8, HALF * DEVS,...  9.73 us
    all_gather x1, blocking collectives, shards(): lax.all_gather(jnp.concatenate([psf_x, psf_y], axis=1), 'view', axis=0, t...  8.22 us
    all_to_all x1, starting transfers between devices, shards(): lax.all_to_all(updated, 'view', split_axis=0, concat_axis=0, tiled=True)  3.53 us
  transfers between devices with their start and end apart: 3, of which 3 were waited for; matrix products, arithmetic and copies ran while one was open for 0% of the time, Pallas kernels for 3%

profile of v3, /device:TPU:1, one launch (start us, length us, event | category | flops | bytes accessed | tf_op | source)
XLA Modules:
  0.0 127.8 jit_solution(4389090450908410100)
XLA Ops:
  0.6 9.7 %pack.1 = (bf16[128,48,128]{2,1,0:T(8,128)(2,1)}, s32[8,512]{1,0:T(8,128)}, s32[128,128]{1,0:T(8,128)}) custom-call(s32[8]{0:T(128)} %mask_ref.3, f32[1,31]{1,0:T(1,128)} %px_ref.1, f32[1,31]{1,0:T(1,128)} %py_ref.1, s32[1,1024]{1,0:T(1,128)} %bitcast.12, bf16[4,512,256]{2,1,0:T(8,128)(2,1)} %est_hbm.3, bf16[1,4,512,256]{3,2,1,0:T(8,128)(2,1)} %meas_hbm.1), custom_call_target="tpu_custom_call" | custom-call | flops 2000000000 | bytes 4000000 | tf_op jit(solution)/shard_map/pack/pallas_call | solution.py:307
  10.4 0.0 copy-start.6
  10.4 0.0 copy-start.7
  10.4 0.0 copy-start.3
  10.4 18.6 %all-to-all-start = ((bf16[128,48,128]{2,1,0:T(8,128)(2,1)}), bf16[128,48,128]{2,1,0:T(8,128)(2,1)S(1)}, u32[]{:S(2)}, u32[]{:S(2)}) async-start(bf16[128,48,128]{2,1,0:T(8,128)(2,1)} %get-tuple-element.12), calls=%async_computation | async-start | bytes 3145728 | tf_op jit(solution)/shard_map/all_to_all | solution.py:400
  29.0 0.0 copy-done.6
  29.0 0.1 maximum_bitcast_fusion
  29.1 8.2 %all-gather = f32[4,1,62]{2,1,0:T(1,128)S(1)} all-gather(f32[1,1,62]{2,1,0:T(1,128)S(1)} %maximum_bitcast_fusion), channel_id=1, replica_groups=mesh['view'=4,'space'=128] {'view'}, dimensions={0}, use_global_device_ids=true | all-gather | bytes 1240 | tf_op jit(solution)/shard_map/all_gather | solution.py:401
  37.3 0.1 fusion
  37.4 1.1 prep.1
  38.5 0.0 copy-start.1
  38.5 31.6 %all-to-all-done.in_ref = bf16[128,48,128]{2,1,0:T(8,128)(2,1)S(1)} async-done(((bf16[128,48,128]{2,1,0:T(8,128)(2,1)}), bf16[128,48,128]{2,1,0:T(8,128)(2,1)S(1)}, u32[]{:S(2)}, u32[]{:S(2)}) %all-to-all-start) | async-done | bytes 1572896 | tf_op jit(solution)/shard_map/all_to_all | solution.py:400
  70.1 2.3 %zpair.1 = bf16[4,512,128]{2,1,0:T(8,128)(2,1)} custom-call(bf16[256,512]{1,0:T(8,128)(2,1)S(1)} %get-tuple-element.10.forward_hbm.forward_ref, bf16[256,512]{1,0:T(8,128)(2,1)S(1)} %get-tuple-element.11.adjoint_hbm, bf16[128,48,128]{2,1,0:T(8,128)(2,1)S(1)} %all-to-all-done.in_ref), custom_call_target="tpu_custom_call" | custom-call | flops 540000000 | bytes 3000000 | tf_op jit(solution)/shard_map/zpair/pallas_call | solution.py:344
  72.4 0.0 copy-done.1
  72.4 0.0 copy-done
  72.4 11.4 %all-to-all-start.1 = ((bf16[512,4,128]{2,1,0:T(4,128)(2,1)}), bf16[512,4,128]{2,1,0:T(4,128)(2,1)S(1)}, u32[]{:S(2)}, u32[]{:S(2)}) async-start(bf16[512,4,128]{2,1,0:T(4,128)(2,1)} %bitcast.4), calls=%async_computation.1 | async-start | bytes 1048576 | tf_op jit(solution)/shard_map/all_to_all | solution.py:406
  83.8 21.9 %all-to-all-done.1 = bf16[512,4,128]{2,1,0:T(4,128)(2,1)S(1)} async-done(((bf16[512,4,128]{2,1,0:T(4,128)(2,1)}), bf16[512,4,128]{2,1,0:T(4,128)(2,1)S(1)}, u32[]{:S(2)}, u32[]{:S(2)}) %all-to-all-start.1) | async-done | bytes 524320 | tf_op jit(solution)/shard_map/all_to_all | solution.py:406
  105.7 0.0 copy-done.2
  105.7 0.0 copy-done.5
  105.7 3.0 %back.1 = bf16[4,512,256]{2,1,0:T(8,128)(2,1)} custom-call(s32[1]{0:T(128)} %bitcast.me_ref, s32[8]{0:T(128)S(1)} %copy-done.4, s32[8,512]{1,0:T(8,128)S(1)} %copy-done.5, f32[8,256]{1,0:T(8,128)S(1)} %get-tuple-element.9.rows_ref, bf16[4,512,128]{2,1,0:T(8,128)(2,1)S(1)} %bitcast.9, bf16[4,512,256]{2,1,0:T(8,128)(2,1)S(1)} %copy-done.2), custom_call_target="tpu_custom_call" | custom-call | flops 1400000000 | bytes 5000000 | tf_op jit(solution)/shard_map/back/pallas_call | solution.py:379
  108.6 3.5 %all-to-all-start.2 = ((bf16[4,512,256]{2,1,0:T(8,128)(2,1)}), bf16[4,512,256]{2,1,0:T(8,128)(2,1)S(1)}, u32[]{:S(2)}, u32[]{:S(2)}) async-start(bf16[4,512,256]{2,1,0:T(8,128)(2,1)} %back.1), calls=%async_computation.2 | async-start | bytes 2097152 | tf_op jit(solution)/shard_map/all_to_all | solution.py:415
  112.2 3.3 %column.1 = bf16[512,8,128]{2,1,0:T(8,128)(2,1)} custom-call(s32[1]{0:T(128)} %bitcast.6.me_ref, bf16[256,512]{1,0:T(8,128)(2,1)} %copy-done.1, s32[128,128]{1,0:T(8,128)} %get-tuple-element.13.count_ref, bf16[128,48,128]{2,1,0:T(8,128)(2,1)} %copy-done), custom_call_target="tpu_custom_call" | custom-call | flops 540000000 | bytes 3000000 | tf_op jit(solution)/shard_map/column/pallas_call | solution.py:365
  115.4 11.4 %all-to-all-done.2 = bf16[4,512,256]{2,1,0:T(8,128)(2,1)S(1)} async-done(((bf16[4,512,256]{2,1,0:T(8,128)(2,1)}), bf16[4,512,256]{2,1,0:T(8,128)(2,1)S(1)}, u32[]{:S(2)}, u32[]{:S(2)}) %all-to-all-start.2) | async-done | bytes 1048608 | tf_op jit(solution)/shard_map/all_to_all | solution.py:415
  126.9 1.0 copy.11
  (7 shorter events, 0.0 us)
Async XLA Ops:
  10.4 18.6 %copy-start.6 = (f32[1,31]{1,0:T(1,128)S(1)}, f32[1,31]{1,0:T(1,128)}, u32[]{:S(2)}) copy-start(f32[1,31]{1,0:T(1,128)} %px_ref.1) | copy-start | bytes 376
  10.4 18.6 %copy-start.7 = (f32[1,31]{1,0:T(1,128)S(1)}, f32[1,31]{1,0:T(1,128)}, u32[]{:S(2)}) copy-start(f32[1,31]{1,0:T(1,128)} %py_ref.1) | copy-start | bytes 376
  10.4 27.0 %copy-start.3 = (f32[1,63]{1,0:T(1,128)S(1)}, f32[1,63]{1,0:T(1,128)}, u32[]{:S(2)}) copy-start(f32[1,63]{1,0:T(1,128)} %pz_ref.1) | copy-start | bytes 760
  10.4 59.7 %all-to-all-start = ((bf16[128,48,128]{2,1,0:T(8,128)(2,1)}), bf16[128,48,128]{2,1,0:T(8,128)(2,1)S(1)}, u32[]{:S(2)}, u32[]{:S(2)}) async-start(bf16[128,48,128]{2,1,0:T(8,128)(2,1)} %get-tuple-element.12), calls=%async_computation | async-start | bytes 3145728 | tf_op jit(solution)/shard_map/all_to_all | solution.py:400
  38.5 33.9 %copy-start.1 = (bf16[256,512]{1,0:T(8,128)(2,1)}, bf16[256,512]{1,0:T(8,128)(2,1)S(1)}, u32[]{:S(2)}) copy-start(bf16[256,512]{1,0:T(8,128)(2,1)S(1)} %get-tuple-element.10.forward_hbm.forward_ref) | copy-start | bytes 786436
  70.1 2.3 %copy-start = (bf16[128,48,128]{2,1,0:T(8,128)(2,1)}, bf16[128,48,128]{2,1,0:T(8,128)(2,1)S(1)}, u32[]{:S(2)}) copy-start(bf16[128,48,128]{2,1,0:T(8,128)(2,1)S(1)} %all-to-all-done.in_ref) | copy-start | bytes 4718596
  70.1 35.6 %copy-start.2 = (bf16[4,512,256]{2,1,0:T(8,128)(2,1)S(1)}, bf16[4,512,256]{2,1,0:T(8,128)(2,1)}, u32[]{:S(2)}) copy-start(bf16[4,512,256]{2,1,0:T(8,128)(2,1)} %est_hbm.3) | copy-start | bytes 3145732
  70.1 35.6 %copy-start.4 = (s32[8]{0:T(128)S(1)}, s32[8]{0:T(128)}, u32[]{:S(2)}) copy-start(s32[8]{0:T(128)} %mask_ref.3) | copy-start | bytes 100
  70.1 35.6 %copy-start.5 = (s32[8,512]{1,0:T(8,128)S(1)}, s32[8,512]{1,0:T(8,128)}, u32[]{:S(2)}) copy-start(s32[8,512]{1,0:T(8,128)} %get-tuple-element.8.table_ref) | copy-start | bytes 49156
  72.4 33.2 %all-to-all-start.1 = ((bf16[512,4,128]{2,1,0:T(4,128)(2,1)}), bf16[512,4,128]{2,1,0:T(4,128)(2,1)S(1)}, u32[]{:S(2)}, u32[]{:S(2)}) async-start(bf16[512,4,128]{2,1,0:T(4,128)(2,1)} %bitcast.4), calls=%async_computation.1 | async-start | bytes 1048576 | tf_op jit(solution)/shard_map/all_to_all | solution.py:406
  108.6 18.2 %all-to-all-start.2 = ((bf16[4,512,256]{2,1,0:T(8,128)(2,1)}), bf16[4,512,256]{2,1,0:T(8,128)(2,1)S(1)}, u32[]{:S(2)}, u32[]{:S(2)}) async-start(bf16[4,512,256]{2,1,0:T(8,128)(2,1)} %back.1), calls=%async_computation.2 | async-start | bytes 2097152 | tf_op jit(solution)/shard_map/all_to_all | solution.py:415

commit v4 on v3

v4 whole, which is shorter than its diff:
```python
import jax
import jax.numpy as jnp
from jax import lax
from jax.experimental import pallas as pl
from jax.experimental.pallas import tpu as pltpu
from jax.sharding import PartitionSpec as P

F32 = jnp.float32
BF16 = jnp.bfloat16
I32 = jnp.int32

VIEWS, DEVS = 4, 128
SLAB, NX, NY, TILE = 4, 512, 256, 128
UNITS = 1024
HALF = 4
MSG = 3 * SLAB * HALF
TAPS_XY, TAPS_Z = 31, 63
ZB = 256
XB = 128
WIDE_LIMIT, LIMIT = 60, 24

SMEM = pl.BlockSpec(memory_space=pltpu.SMEM)
VMEM = pl.BlockSpec(memory_space=pltpu.VMEM)
ANY = pl.BlockSpec(memory_space=pl.ANY)
HBM = pl.BlockSpec(memory_space=pltpu.HBM)


def shape(*dims, dtype=BF16):
    return jax.ShapeDtypeStruct(dims, dtype)


def iota(shape, dim):
    return lax.broadcasted_iota(I32, shape, dim)


def placed_taps(read, count, lanes, place):
    lane = iota((1, lanes), 1)
    total = read(0)
    for m in range(1, count):
        total = total + read(m)
    row = jnp.zeros((1, lanes), F32)
    for m in range(count):
        row = jnp.where(lane == place(m) % lanes, read(m), row)
    return (row / jnp.full((1, lanes), total, F32)).astype(BF16).astype(F32)


def rolled(row, rows):
    return pltpu.roll(
        jnp.broadcast_to(row, (rows, row.shape[1])), 0, 1, stride=1, stride_axis=0
    )


def band(row, n, half):
    distance = jnp.abs(iota((n, n), 1) - iota((n, n), 0))
    return jnp.where(distance <= half, rolled(row, n), 0.0).astype(BF16)


def dot(a, b, dims=((1,), (0,))):
    return lax.dot_general(a, b, (dims, ((), ())), preferred_element_type=F32)


def one_hot(condition):
    return jnp.where(condition, 1.0, 0.0).astype(BF16)


def slot_rows(mask_ref, owner_ref):
    pairs = UNITS // ZB
    square = (DEVS, TILE)
    device = iota(square, 0).astype(F32)
    w = iota((ZB, ZB), 1)
    unit = 2 * (w % TILE) + w // TILE
    deal = one_hot(iota((ZB, ZB), 0) == unit)
    owners = jnp.concatenate([owner_ref[0:1, i * ZB : (i + 1) * ZB] for i in range(pairs)] * 2, axis=0)
    owners = dot(owners.astype(F32).astype(BF16), deal)
    row = iota((ZB, ZB), 0)
    earlier = one_hot(2 * (row % TILE) + row // TILE < unit)
    sums = jnp.concatenate([earlier, jnp.ones((ZB, TILE), BF16)], axis=1)
    count = jnp.zeros(square, F32)
    owner, member, before = [], [], []
    for pair in range(pairs):
        for t in range(2):
            here = owners[pair : pair + 1, t * TILE : (t + 1) * TILE]
            owner.append(jnp.where(mask_ref[2 * pair + t] > 0, here, -1.0))
            member.append(device == owner[-1])
        found = dot(jnp.concatenate([one_hot(m) for m in member[-2:]], axis=1), sums)
        before.append(found[:, :TILE] + count)
        before.append(found[:, TILE:ZB] + count)
        count += found[:, ZB:]
    over = jnp.maximum(count - HALF, 0.0)
    free = jnp.maximum(HALF - count, 0.0)
    lower = one_hot(iota((DEVS, DEVS), 1) < iota((DEVS, DEVS), 0))
    starts = dot(lower, jnp.concatenate([over, free], axis=1).astype(BF16))
    over_start, free_start = starts[:, :TILE], starts[:, TILE:]
    free_end = free_start + free
    place = (count - free_start) * DEVS + device
    balanced, overflow = [], []
    for mine, inside, ahead in zip(owner, member, before):
        position = jnp.sum(jnp.where(inside, ahead, 0.0), axis=0, keepdims=True)
        start = jnp.sum(jnp.where(inside, over_start, 0.0), axis=0, keepdims=True)
        rank = start + position - HALF
        found = jnp.where((free_start <= rank) & (rank < free_end), place + rank * DEVS, 0.0)
        filled = jnp.sum(found, axis=0, keepdims=True)
        own = position * DEVS + mine
        balanced.append(jnp.where(mine < 0, -1.0, jnp.where(position < HALF, own, filled)))
        overflow.append(jnp.where((mine >= 0) & (position >= HALF), own - HALF * DEVS, -1.0))
    return balanced, overflow, count


def tissue_tiles(mask_ref):
    tiles = UNITS // TILE
    found = jnp.int32(0)
    chosen = [jnp.int32(0)] * (tiles // 2)
    for tile in range(tiles):
        here = mask_ref[tile] > 0
        chosen = [jnp.where(here & (found == i), tile, old) for i, old in enumerate(chosen)]
        found += here.astype(I32)
    return chosen


def pack_kernel(
    mask_ref, px_ref, py_ref, owner_ref, est_hbm, meas_hbm, out_hbm, table_ref, count_ref,
    est_ref, meas_ref, along, places, matrix_y, out_ref, est_sem, meas_sem, out_sem,
):
    est_copy = pltpu.make_async_copy(est_hbm, est_ref, est_sem)
    meas_copy = pltpu.make_async_copy(meas_hbm, meas_ref, meas_sem)
    meas_copy.start()
    est_copy.start()
    slots = HALF * DEVS
    group = SLAB * HALF
    tiles = UNITS // TILE
    balanced, overflow, count = slot_rows(mask_ref, owner_ref)
    count_ref[...] = count.astype(I32)
    table_ref[...] = jnp.concatenate(balanced, axis=0).astype(I32)
    places[...] = jnp.concatenate(balanced + overflow, axis=0)
    chosen = tissue_tiles(mask_ref)
    row_of = [pl.multiple_of(tile // 2 * TILE, TILE) for tile in chosen]
    lane_of = [pl.multiple_of(tile % 2 * TILE, TILE) for tile in chosen]
    index = iota((slots, TILE), 0).astype(F32)
    pick, pick_more = [
        jnp.concatenate([one_hot(index == places[pl.ds(first + tile, 1), :]) for tile in chosen], axis=1)
        for first in (0, tiles)
    ]
    half_xy = TAPS_XY // 2
    matrix_x = band(placed_taps(lambda m: px_ref[0, m], TAPS_XY, NX, lambda m: m - half_xy), NX, half_xy)
    matrix_y[...] = band(placed_taps(lambda m: py_ref[0, m], TAPS_XY, NY, lambda m: half_xy - m), NY, half_xy)

    block = ZB // group
    r = iota((ZB, ZB), 0)
    turn = one_hot(iota((ZB, ZB), 1) == r % group * block + r // group)
    copies = []

    def rows_of(values, i):
        return jnp.concatenate(
            [
                values[slot * DEVS + i * block : slot * DEVS + (i + 1) * block, plane * TILE : (plane + 1) * TILE]
                for plane in range(SLAB)
                for slot in range(HALF)
            ],
            axis=0,
        )

    meas_copy.wait()
    seen = jnp.concatenate(
        [
            jnp.concatenate(
                [meas_ref[0, plane, pl.ds(row, TILE), pl.ds(lane, TILE)] for plane in range(SLAB)], axis=1
            )
            for row, lane in zip(row_of, lane_of)
        ],
        axis=0,
    )
    seen = dot(pick, seen).astype(BF16)
    est_copy.wait()
    for plane in range(SLAB):
        along[plane] = dot(matrix_x, est_ref[plane]).astype(BF16)
    blurred = []
    for row, lane in zip(row_of, lane_of):
        rows = jnp.concatenate([along[plane, pl.ds(row, TILE), :] for plane in range(SLAB)], axis=0)
        tile = dot(rows, matrix_y[:, pl.ds(lane, TILE)]).astype(BF16)
        blurred.append(
            jnp.concatenate([tile[plane * TILE : (plane + 1) * TILE] for plane in range(SLAB)], axis=1)
        )
    blurred = jnp.concatenate(blurred, axis=0)
    parts = [dot(pick, blurred).astype(BF16), dot(pick_more, blurred).astype(BF16), seen]
    for i in range(DEVS // block):
        turned = dot(turn, jnp.concatenate([rows_of(part, i) for part in parts], axis=1)).astype(BF16)
        for k in range(len(parts)):
            out_ref[i * block : (i + 1) * block, k * group : (k + 1) * group, :] = turned[
                :, k * TILE : (k + 1) * TILE
            ].reshape(block, group, TILE)
        here = pl.ds(i * block, block)
        copies.append(pltpu.make_async_copy(out_ref.at[here], out_hbm.at[here], out_sem.at[i]))
        copies[-1].start()
    for copy in copies:
        copy.wait()


def prep_kernel(pz_ref, px_ref, py_ref, table_ref, forward_ref, adjoint_ref, rows_ref, units_ref):
    group = SLAB * HALF
    edge = ZB // 2
    half_z = TAPS_Z // 2
    near = edge - HALF * half_z
    far = edge + HALF * half_z
    forward_ref[...] = rolled(
        placed_taps(lambda m: pz_ref[0, m], TAPS_Z, 2 * ZB, lambda m: near + HALF * m), ZB
    ).astype(BF16)
    adjoint = rolled(
        placed_taps(lambda m: pz_ref[0, m], TAPS_Z, 2 * ZB, lambda m: far - HALF * m), ZB
    ).astype(BF16)
    r = iota((ZB, ZB), 0)
    part = ZB // SLAB
    source = r % part // HALF * group + r // part * HALF + r % HALF
    adjoint_ref[...] = dot(one_hot(iota((ZB, ZB), 1) == source), adjoint).astype(BF16)
    half_xy = TAPS_XY // 2
    for view in range(VIEWS):
        rows_ref[view : view + 1, :] = placed_taps(
            lambda m: px_ref[view, m], TAPS_XY, 2 * XB, lambda m: XB // 2 + half_xy - m
        )
        rows_ref[VIEWS + view : VIEWS + view + 1, :] = placed_taps(
            lambda m: py_ref[view, m], TAPS_XY, NY, lambda m: m - half_xy
        )
    slots = HALF * DEVS
    tiles = UNITS // TILE
    table = table_ref[...].astype(F32)
    table = jnp.concatenate([table] * (TILE // tiles), axis=0).T.astype(I32)
    total = jnp.zeros((1, slots), I32)
    for tile in range(tiles):
        place = table[:, tile : tile + 1]
        place = jnp.where(place < 0, -1, place % DEVS * HALF + place // DEVS)
        unit = 2 * (tile // 2 * TILE + iota((TILE, slots), 0)) + tile % 2
        total += jnp.sum(jnp.where(place == iota((TILE, slots), 1), unit, 0), axis=0, keepdims=True)
    units_ref[...] = jnp.broadcast_to(total, (8, slots))


def z_kernel(forward_ref, adjoint_ref, in_ref, back_hbm, ratio, back_ref, sems):
    group = SLAB * HALF
    rows = DEVS * group
    blocks = rows // ZB
    edge = ZB // 2
    block = ZB // group
    none = jnp.zeros((edge, TILE), BF16)

    def window(block_at):
        first, last = block_at * block - block // 2, (block_at + 1) * block + block // 2
        inner = in_ref[max(first, 0) : min(last, DEVS), 0:group, :]
        inner = inner.reshape(inner.shape[0] * group, TILE)
        return jnp.concatenate([none] * (first < 0) + [inner] + [none] * (last > DEVS), axis=0)

    ratio[0:edge, :] = none
    ratio[edge + rows :, :] = none
    for i in range(blocks // 2):
        pair = (i, i + blocks // 2)
        both = dot(forward_ref[...], jnp.concatenate([window(j) for j in pair], axis=1))
        for half, j in enumerate(pair):
            seen = in_ref[j * block : (j + 1) * block, 2 * group :, :].reshape(ZB, TILE)
            ratio[edge + j * ZB : edge + (j + 1) * ZB, :] = (
                seen.astype(F32) / both[:, half * TILE : (half + 1) * TILE]
            ).astype(BF16)
    part = ZB // SLAB
    copies = []
    for i in range(blocks // 2):
        pair = (i, i + blocks // 2)
        both = dot(
            adjoint_ref[...], jnp.concatenate([ratio[j * ZB : j * ZB + 2 * ZB, :] for j in pair], axis=1)
        ).astype(BF16)
        for half, j in enumerate(pair):
            for plane in range(SLAB):
                back_ref[plane, j * part : (j + 1) * part, :] = both[
                    plane * part : (plane + 1) * part, half * TILE : (half + 1) * TILE
                ]
        if i % 2:
            for half, j in enumerate(pair):
                here = pl.ds((j - 1) * part, 2 * part)
                copies.append(
                    pltpu.make_async_copy(back_ref.at[:, here, :], back_hbm.at[:, here, :], sems.at[i // 2, half])
                )
                copies[-1].start()
    for copy in copies:
        copy.wait()


def column_kernel(me_ref, forward_ref, count_ref, in_ref, column_ref, padded):
    group = SLAB * HALF
    rows = DEVS * group
    edge = ZB // 2
    padded[0:edge, :] = jnp.zeros((edge, 2 * TILE), BF16)
    padded[edge + rows :, :] = jnp.zeros((edge, 2 * TILE), BF16)
    padded[edge : edge + rows, 0:TILE] = in_ref[:, 0:group, :].reshape(rows, TILE)
    padded[edge : edge + rows, TILE:] = in_ref[:, group : 2 * group, :].reshape(rows, TILE)
    count = count_ref[pl.ds(me_ref[0], 1), :].reshape(1, 1, TILE)
    planes = ZB // HALF
    pairs = planes // 2
    sub = iota((pairs, 8, TILE), 1)
    live = sub < count
    for block in range(rows // ZB):
        values = dot(forward_ref[...], padded[block * ZB : block * ZB + 2 * ZB, :])
        own = values[:, :TILE].reshape(pairs, 8, TILE)
        more = values[:, TILE:].reshape(pairs, 8, TILE)
        first = jnp.where(sub < HALF, own, pltpu.roll(more, HALF, 1))
        second = jnp.where(sub < HALF, pltpu.roll(own, HALF, 1), more)
        both = jnp.stack([jnp.where(live, first, 0.0), jnp.where(live, second, 0.0)], axis=1)
        column_ref[block * planes : (block + 1) * planes] = both.reshape(planes, 8, TILE).astype(BF16)


def back_kernel(
    me_ref, mask_ref, units_ref, rows_ref, in_ref, est_hbm, out_hbm,
    est_ref, back_z, padded, out_ref, est_sem, out_sems,
):
    est_copy = pltpu.make_async_copy(est_hbm.at[me_ref[0]], est_ref, est_sem)
    est_copy.start()
    edge = XB // 2
    cols = jnp.concatenate([in_ref[view] for view in range(VIEWS)], axis=1)
    units = units_ref[0:1, :]
    slots = HALF * DEVS
    chosen = tissue_tiles(mask_ref)
    here = [units == 2 * (tile // 2 * TILE + iota((TILE, slots), 0)) + tile % 2 for tile in chosen]
    found = dot(jnp.concatenate([one_hot(h) for h in here], axis=0), cols).astype(BF16)
    back_z[...] = jnp.ones((VIEWS, NX, NY), BF16)
    for i, tile in enumerate(chosen):
        row = pl.multiple_of(tile // 2 * TILE, TILE)
        lane = pl.multiple_of(tile % 2 * TILE, TILE)
        for view in range(VIEWS):
            back_z[view, pl.ds(row, TILE), pl.ds(lane, TILE)] = found[
                i * TILE : (i + 1) * TILE, view * TILE : (view + 1) * TILE
            ]
    bands = []
    for view in range(VIEWS):
        bands.append(rolled(rows_ref[view : view + 1, :], XB).astype(BF16))
        matrix_y = band(rows_ref[VIEWS + view : VIEWS + view + 1, :], NY, TAPS_XY // 2)
        padded[view, 0:edge, :] = jnp.zeros((edge, NY), BF16)
        padded[view, edge + NX :, :] = jnp.zeros((edge, NY), BF16)
        padded[view, edge : edge + NX, :] = dot(back_z[view], matrix_y).astype(BF16)
    est_copy.wait()
    writes = []
    for block in range(NX // XB):
        here = pl.ds(block * XB, XB)
        summed = jnp.zeros((XB, NY), F32)
        for view in range(VIEWS):
            summed += dot(bands[view], padded[view, block * XB : block * XB + 2 * XB, :])
        out_ref[here, :] = (est_ref[here, :].astype(F32) * summed / VIEWS).astype(BF16)
        for view in range(VIEWS):
            writes.append(
                pltpu.make_async_copy(out_ref.at[here, :], out_hbm.at[view, here, :], out_sems.at[block, view])
            )
            writes[-1].start()
    for write in writes:
        write.wait()


def call(kernel, name, out_shape, in_specs, out_specs, scratch, limit, flops, moved):
    return pl.pallas_call(
        kernel,
        out_shape=out_shape,
        in_specs=in_specs,
        out_specs=out_specs,
        scratch_shapes=scratch,
        compiler_params=pltpu.CompilerParams(vmem_limit_bytes=limit * 1024 * 1024),
        cost_estimate=pl.CostEstimate(flops=flops, bytes_accessed=moved, transcendentals=0),
        name=name,
    )


def pack(estimate, measured, psf_x, psf_y, tissue_mask, column_owner):
    return call(
        pack_kernel,
        "pack",
        (shape(DEVS, MSG, TILE), shape(UNITS // TILE, TILE, dtype=I32), shape(DEVS, TILE, dtype=I32)),
        [SMEM, SMEM, SMEM, VMEM, ANY, ANY],
        (ANY, VMEM, VMEM),
        [
            pltpu.VMEM((SLAB, NX, NY), BF16),
            pltpu.VMEM((1, SLAB, NX, NY), BF16),
            pltpu.VMEM((SLAB, NX, NY), BF16),
            pltpu.VMEM((2 * UNITS // TILE, TILE), F32),
            pltpu.VMEM((NY, NY), BF16),
            pltpu.VMEM((DEVS, MSG, TILE), BF16),
            pltpu.SemaphoreType.DMA,
            pltpu.SemaphoreType.DMA,
            pltpu.SemaphoreType.DMA((DEVS * SLAB * HALF // ZB,)),
        ],
        WIDE_LIMIT,
        flops=2_000_000_000,
        moved=4_000_000,
    )(tissue_mask, psf_x, psf_y, column_owner.reshape(1, UNITS), estimate, measured)


def prep(psf_z, taps_x, taps_y, table):
    return call(
        prep_kernel,
        "prep",
        (
            shape(ZB, 2 * ZB),
            shape(ZB, 2 * ZB),
            shape(2 * VIEWS, NY, dtype=F32),
            shape(8, HALF * DEVS, dtype=I32),
        ),
        [SMEM, SMEM, SMEM, VMEM],
        (VMEM,) * 4,
        [],
        LIMIT,
        flops=1_000_000_000,
        moved=4_000_000,
    )(psf_z, taps_x, taps_y, table)


def z_pair(forward, adjoint, arrived):
    rows = DEVS * SLAB * HALF
    return call(
        z_kernel,
        "zpair",
        shape(VIEWS, HALF * DEVS, TILE),
        [VMEM, VMEM, VMEM],
        ANY,
        [
            pltpu.VMEM((rows + ZB, TILE), BF16),
            pltpu.VMEM((VIEWS, HALF * DEVS, TILE), BF16),
            pltpu.SemaphoreType.DMA((rows // ZB // 4, 2)),
        ],
        LIMIT,
        flops=540_000_000,
        moved=3_000_000,
    )(forward, adjoint, arrived)


def column(space_index, forward, count, arrived):
    rows = DEVS * SLAB * HALF
    return call(
        column_kernel,
        "column",
        shape(SLAB * DEVS, 2 * HALF, TILE),
        [SMEM, VMEM, VMEM, VMEM],
        VMEM,
        [pltpu.VMEM((rows + ZB, 2 * TILE), BF16)],
        WIDE_LIMIT,
        flops=540_000_000,
        moved=3_000_000,
    )(space_index, forward, count, arrived)


def back(view_index, tissue_mask, units, rows, returned, estimate):
    return call(
        back_kernel,
        "back",
        shape(VIEWS, NX, NY),
        [SMEM, SMEM, VMEM, VMEM, VMEM, HBM],
        HBM,
        [
            pltpu.VMEM((NX, NY), BF16),
            pltpu.VMEM((VIEWS, NX, NY), BF16),
            pltpu.VMEM((VIEWS, NX + XB, NY), BF16),
            pltpu.VMEM((NX, NY), BF16),
            pltpu.SemaphoreType.DMA,
            pltpu.SemaphoreType.DMA((NX // XB, VIEWS)),
        ],
        LIMIT,
        flops=1_400_000_000,
        moved=5_000_000,
    )(view_index, tissue_mask, units, rows, returned, estimate)


def shards(estimate, measured, psf_x, psf_y, psf_z, tissue_mask, column_owner):
    message, table, count = pack(estimate, measured, psf_x, psf_y, tissue_mask, column_owner)
    arrived = lax.all_to_all(message, "space", split_axis=0, concat_axis=0, tiled=True)
    taps = lax.all_gather(jnp.concatenate([psf_x, psf_y], axis=1), "view", axis=0, tiled=True)
    forward, adjoint, rows, units = prep(psf_z, taps[:, :TAPS_XY], taps[:, TAPS_XY:], table)
    space_index = lax.axis_index("space").astype(I32).reshape(1)
    view_index = lax.axis_index("view").astype(I32).reshape(1)
    sent = z_pair(forward, adjoint, arrived)
    returned = lax.all_to_all(
        sent.reshape(VIEWS * DEVS, HALF, TILE),
        ("view", "space"),
        split_axis=0,
        concat_axis=0,
        tiled=True,
    ).reshape(VIEWS, HALF * DEVS, TILE)
    column_blur = column(space_index, forward, count, arrived)
    updated = back(view_index, tissue_mask, units, rows, returned, estimate)
    updated = lax.all_to_all(updated, "view", split_axis=0, concat_axis=0, tiled=True)
    return updated, column_blur[None]


def solution(mesh):
    placed = (
        P("space", None, None),
        P("view", "space", None, None),
        P("view", None),
        P("view", None),
        P("view", None),
        P(),
        P(),
    )
    return jax.shard_map(
        shards,
        mesh=mesh,
        in_specs=placed,
        out_specs=(P("space", None, None), P("view", None, "space", None)),
        check_vma=False,
    )
```

time: 128 us -> 125 us (0.977)
  Pallas kernels: 19.4 us -> 16 us
    pallas_call x2, Pallas kernels: 12 us -> 8.35 us  [the longest x1 6.69 us: pack(): call(pack_kernel, 'pack', (shape(DEVS, MSG, TILE), shape(UNITS // TILE, T...]
  transfers between devices with their start and end apart: 3 -> 3, of which waited for: 3 -> 3; matrix products, arithmetic and copies ran while one was open for 0% -> 0% of each run, Pallas kernels for 3% -> 4%
where the time goes in v4:
time: 125 us; the launch traced here: 124 us
  waiting for transfers between devices  64.5 us (52%)
  starting transfers between devices  33.5 us (27%)
  Pallas kernels  16 us (13%)
  blocking collectives  8.22 us (7%)
    all_to_all x1, waiting for transfers between devices, shards(): lax.all_to_all(message, 'space', split_axis=0, concat_axis=0, tiled=True)  31.2 us
    all_to_all x1, waiting for transfers between devices, shards(): lax.all_to_all(sent.reshape(VIEWS * DEVS, HALF, TILE), ('view', 'space'),...  21.9 us
    all_to_all x1, starting transfers between devices, shards(): lax.all_to_all(message, 'space', split_axis=0, concat_axis=0, tiled=True)  18.6 us
    all_to_all x1, waiting for transfers between devices, shards(): lax.all_to_all(updated, 'view', split_axis=0, concat_axis=0, tiled=True)  11.4 us
    all_to_all x1, starting transfers between devices, shards(): lax.all_to_all(sent.reshape(VIEWS * DEVS, HALF, TILE), ('view', 'space'),...  11.4 us
    all_gather x1, blocking collectives, shards(): lax.all_gather(jnp.concatenate([psf_x, psf_y], axis=1), 'view', axis=0, t...  8.22 us
    pallas_call x1, Pallas kernels, pack(): call(pack_kernel, 'pack', (shape(DEVS, MSG, TILE), shape(UNITS // TILE, T...  6.69 us
    all_to_all x1, starting transfers between devices, shards(): lax.all_to_all(updated, 'view', split_axis=0, concat_axis=0, tiled=True)  3.53 us
  transfers between devices with their start and end apart: 3, of which 3 were waited for; matrix products, arithmetic and copies ran while one was open for 0% of the time, Pallas kernels for 4%

profile of v4, /device:TPU:1, one launch (start us, length us, event | category | flops | bytes accessed | tf_op | source)
XLA Modules:
  0.0 124.1 jit_solution(7722064732567244736)
XLA Ops:
  0.6 6.7 %pack.1 = (bf16[128,48,128]{2,1,0:T(8,128)(2,1)}, s32[8,128]{1,0:T(8,128)}, s32[128,128]{1,0:T(8,128)}) custom-call(s32[8]{0:T(128)} %mask_ref.3, f32[1,31]{1,0:T(1,128)} %px_ref.1, f32[1,31]{1,0:T(1,128)} %py_ref.1, s32[1,1024]{1,0:T(1,128)} %bitcast.12, bf16[4,512,256]{2,1,0:T(8,128)(2,1)} %est_hbm.3, bf16[1,4,512,256]{3,2,1,0:T(8,128)(2,1)} %meas_hbm.1), custom_call_target="tpu_custom_call" | custom-call | flops 2000000000 | bytes 4000000 | tf_op jit(solution)/shard_map/pack/pallas_call | solution.py:364
  7.3 0.0 copy-start.6
  7.3 0.0 copy-start.7
  7.4 0.0 copy-start.3
  7.4 0.0 copy-start.5
  7.4 18.6 %all-to-all-start = ((bf16[128,48,128]{2,1,0:T(8,128)(2,1)}), bf16[128,48,128]{2,1,0:T(8,128)(2,1)S(1)}, u32[]{:S(2)}, u32[]{:S(2)}) async-start(bf16[128,48,128]{2,1,0:T(8,128)(2,1)} %get-tuple-element.14), calls=%async_computation | async-start | bytes 3145728 | tf_op jit(solution)/shard_map/all_to_all | solution.py:463
  26.0 0.0 copy-done.6
  26.0 0.0 copy-done.7
  26.0 0.1 maximum_bitcast_fusion
  26.0 8.2 %all-gather = f32[4,1,62]{2,1,0:T(1,128)S(1)} all-gather(f32[1,1,62]{2,1,0:T(1,128)S(1)} %maximum_bitcast_fusion), channel_id=1, replica_groups=mesh['view'=4,'space'=128] {'view'}, dimensions={0}, use_global_device_ids=true | all-gather | bytes 1240 | tf_op jit(solution)/shard_map/all_gather | solution.py:464
  34.3 0.1 fusion
  34.3 0.0 copy-done.5
  34.3 1.5 %prep.1 = (bf16[256,512]{1,0:T(8,128)(2,1)S(1)}, bf16[256,512]{1,0:T(8,128)(2,1)S(1)}, f32[8,256]{1,0:T(8,128)S(1)}, s32[8,512]{1,0:T(8,128)S(1)}) custom-call(f32[1,63]{1,0:T(1,128)S(1)} %copy-done.3, f32[4,31]{1,0:T(4,128)S(1)} %get-tuple-element.17.px_ref, f32[4,31]{1,0:T(4,128)S(1)} %get-tuple-element.16.py_ref, s32[8,128]{1,0:T(8,128)S(1)} %copy-done.5), custom_call_target="tpu_custom_call" | custom-call | flops 1000000000 | bytes 4000000 | tf_op jit(solution)/shard_map/prep/pallas_call | solution.py:388
  35.8 0.0 copy-start.1
  35.8 31.2 %all-to-all-done.in_ref = bf16[128,48,128]{2,1,0:T(8,128)(2,1)S(1)} async-done(((bf16[128,48,128]{2,1,0:T(8,128)(2,1)}), bf16[128,48,128]{2,1,0:T(8,128)(2,1)S(1)}, u32[]{:S(2)}, u32[]{:S(2)}) %all-to-all-start) | async-done | bytes 1572896 | tf_op jit(solution)/shard_map/all_to_all | solution.py:463
  67.1 1.7 %zpair.1 = bf16[4,512,128]{2,1,0:T(8,128)(2,1)} custom-call(bf16[256,512]{1,0:T(8,128)(2,1)S(1)} %get-tuple-element.12.forward_ref, bf16[256,512]{1,0:T(8,128)(2,1)S(1)} %get-tuple-element.13.adjoint_ref, bf16[128,48,128]{2,1,0:T(8,128)(2,1)S(1)} %all-to-all-done.in_ref), custom_call_target="tpu_custom_call" | custom-call | flops 540000000 | bytes 3000000 | tf_op jit(solution)/shard_map/zpair/pallas_call | solution.py:408
  68.7 11.4 %all-to-all-start.1 = ((bf16[512,4,128]{2,1,0:T(4,128)(2,1)}), bf16[512,4,128]{2,1,0:T(4,128)(2,1)S(1)}, u32[]{:S(2)}, u32[]{:S(2)}) async-start(bf16[512,4,128]{2,1,0:T(4,128)(2,1)} %bitcast.4), calls=%async_computation.1 | async-start | bytes 1048576 | tf_op jit(solution)/shard_map/all_to_all | solution.py:469
  80.1 21.9 %all-to-all-done.1 = bf16[512,4,128]{2,1,0:T(4,128)(2,1)S(1)} async-done(((bf16[512,4,128]{2,1,0:T(4,128)(2,1)}), bf16[512,4,128]{2,1,0:T(4,128)(2,1)S(1)}, u32[]{:S(2)}, u32[]{:S(2)}) %all-to-all-start.1) | async-done | bytes 524320 | tf_op jit(solution)/shard_map/all_to_all | solution.py:469
  102.0 0.0 copy-done.4
  102.0 2.9 %back.1 = bf16[4,512,256]{2,1,0:T(8,128)(2,1)} custom-call(s32[1]{0:T(128)} %bitcast.me_ref, s32[8]{0:T(128)S(1)} %copy-done.4, s32[8,512]{1,0:T(8,128)S(1)} %get-tuple-element.10.units_ref, f32[8,256]{1,0:T(8,128)S(1)} %get-tuple-element.11.rows_ref, bf16[4,512,128]{2,1,0:T(8,128)(2,1)S(1)} %bitcast.9, bf16[4,512,256]{2,1,0:T(8,128)(2,1)S(1)} %copy-done.2), custom_call_target="tpu_custom_call" | custom-call | flops 1400000000 | bytes 5000000 | tf_op jit(solution)/shard_map/back/pallas_call | solution.py:441
  104.9 3.5 %all-to-all-start.2 = ((bf16[4,512,256]{2,1,0:T(8,128)(2,1)}), bf16[4,512,256]{2,1,0:T(8,128)(2,1)S(1)}, u32[]{:S(2)}, u32[]{:S(2)}) async-start(bf16[4,512,256]{2,1,0:T(8,128)(2,1)} %back.1), calls=%async_computation.2 | async-start | bytes 2097152 | tf_op jit(solution)/shard_map/all_to_all | solution.py:478
  108.5 3.3 %column.1 = bf16[512,8,128]{2,1,0:T(8,128)(2,1)} custom-call(s32[1]{0:T(128)} %bitcast.6.me_ref, bf16[256,512]{1,0:T(8,128)(2,1)} %copy-done.1, s32[128,128]{1,0:T(8,128)} %get-tuple-element.15.count_ref, bf16[128,48,128]{2,1,0:T(8,128)(2,1)} %copy-done), custom_call_target="tpu_custom_call" | custom-call | flops 540000000 | bytes 3000000 | tf_op jit(solution)/shard_map/column/pallas_call | solution.py:427
  111.7 11.4 %all-to-all-done.2 = bf16[4,512,256]{2,1,0:T(8,128)(2,1)S(1)} async-done(((bf16[4,512,256]{2,1,0:T(8,128)(2,1)}), bf16[4,512,256]{2,1,0:T(8,128)(2,1)S(1)}, u32[]{:S(2)}, u32[]{:S(2)}) %all-to-all-start.2) | async-done | bytes 1048608 | tf_op jit(solution)/shard_map/all_to_all | solution.py:478
  123.2 1.0 copy.11
  (7 shorter events, 0.0 us)
Async XLA Ops:
  7.3 18.6 %copy-start.6 = (f32[1,31]{1,0:T(1,128)S(1)}, f32[1,31]{1,0:T(1,128)}, u32[]{:S(2)}) copy-start(f32[1,31]{1,0:T(1,128)} %py_ref.1) | copy-start | bytes 376
  7.3 18.6 %copy-start.7 = (f32[1,31]{1,0:T(1,128)S(1)}, f32[1,31]{1,0:T(1,128)}, u32[]{:S(2)}) copy-start(f32[1,31]{1,0:T(1,128)} %px_ref.1) | copy-start | bytes 376
  7.4 27.0 %copy-start.3 = (f32[1,63]{1,0:T(1,128)S(1)}, f32[1,63]{1,0:T(1,128)}, u32[]{:S(2)}) copy-start(f32[1,63]{1,0:T(1,128)} %pz_ref.1) | copy-start | bytes 760
  7.4 27.0 %copy-start.5 = (s32[8,128]{1,0:T(8,128)S(1)}, s32[8,128]{1,0:T(8,128)}, u32[]{:S(2)}) copy-start(s32[8,128]{1,0:T(8,128)} %get-tuple-element.9.table_ref) | copy-start | bytes 12292
  7.4 59.7 %all-to-all-start = ((bf16[128,48,128]{2,1,0:T(8,128)(2,1)}), bf16[128,48,128]{2,1,0:T(8,128)(2,1)S(1)}, u32[]{:S(2)}, u32[]{:S(2)}) async-start(bf16[128,48,128]{2,1,0:T(8,128)(2,1)} %get-tuple-element.14), calls=%async_computation | async-start | bytes 3145728 | tf_op jit(solution)/shard_map/all_to_all | solution.py:463
  35.8 32.9 %copy-start.1 = (bf16[256,512]{1,0:T(8,128)(2,1)}, bf16[256,512]{1,0:T(8,128)(2,1)S(1)}, u32[]{:S(2)}) copy-start(bf16[256,512]{1,0:T(8,128)(2,1)S(1)} %get-tuple-element.12.forward_ref) | copy-start | bytes 786436
  67.0 1.7 %copy-start = (bf16[128,48,128]{2,1,0:T(8,128)(2,1)}, bf16[128,48,128]{2,1,0:T(8,128)(2,1)S(1)}, u32[]{:S(2)}) copy-start(bf16[128,48,128]{2,1,0:T(8,128)(2,1)S(1)} %all-to-all-done.in_ref) | copy-start | bytes 4718596
  67.1 35.0 %copy-start.2 = (bf16[4,512,256]{2,1,0:T(8,128)(2,1)S(1)}, bf16[4,512,256]{2,1,0:T(8,128)(2,1)}, u32[]{:S(2)}) copy-start(bf16[4,512,256]{2,1,0:T(8,128)(2,1)} %est_hbm.3) | copy-start | bytes 3145732
  67.1 35.0 %copy-start.4 = (s32[8]{0:T(128)S(1)}, s32[8]{0:T(128)}, u32[]{:S(2)}) copy-start(s32[8]{0:T(128)} %mask_ref.3) | copy-start | bytes 100
  68.7 33.3 %all-to-all-start.1 = ((bf16[512,4,128]{2,1,0:T(4,128)(2,1)}), bf16[512,4,128]{2,1,0:T(4,128)(2,1)S(1)}, u32[]{:S(2)}, u32[]{:S(2)}) async-start(bf16[512,4,128]{2,1,0:T(4,128)(2,1)} %bitcast.4), calls=%async_computation.1 | async-start | bytes 1048576 | tf_op jit(solution)/shard_map/all_to_all | solution.py:469
  104.9 18.2 %all-to-all-start.2 = ((bf16[4,512,256]{2,1,0:T(8,128)(2,1)}), bf16[4,512,256]{2,1,0:T(8,128)(2,1)S(1)}, u32[]{:S(2)}, u32[]{:S(2)}) async-start(bf16[4,512,256]{2,1,0:T(8,128)(2,1)} %back.1), calls=%async_computation.2 | async-start | bytes 2097152 | tf_op jit(solution)/shard_map/all_to_all | solution.py:478

commit v5 on v4

--- a/solution.py
+++ b/solution.py
@@ -118,19 +118,36 @@
 
 
 def pack_kernel(
-    mask_ref, px_ref, py_ref, owner_ref, est_hbm, meas_hbm, out_hbm, table_ref, count_ref,
-    est_ref, meas_ref, along, places, matrix_y, out_ref, est_sem, meas_sem, out_sem,
+    mask_hbm, px_hbm, py_hbm, owner_hbm, est_hbm, meas_hbm, out_hbm, table_hbm, count_hbm,
+    mask_ref, px_ref, py_ref, owner_ref, est_ref, meas_ref, along, places, matrix_y,
+    out_ref, table_ref, count_ref, sems, out_sem,
 ):
-    est_copy = pltpu.make_async_copy(est_hbm, est_ref, est_sem)
-    meas_copy = pltpu.make_async_copy(meas_hbm, meas_ref, meas_sem)
-    meas_copy.start()
-    est_copy.start()
+    reads = [
+        pltpu.make_async_copy(source, target, sems.at[i])
+        for i, (source, target) in enumerate(
+            zip(
+                (mask_hbm, owner_hbm, px_hbm, py_hbm, meas_hbm, est_hbm),
+                (mask_ref, owner_ref, px_ref, py_ref, meas_ref, est_ref),
+            )
+        )
+    ]
+    for copy in reads:
+        copy.start()
+    meas_copy, est_copy = reads[4:]
+    for copy in reads[:2]:
+        copy.wait()
     slots = HALF * DEVS
     group = SLAB * HALF
     tiles = UNITS // TILE
     balanced, overflow, count = slot_rows(mask_ref, owner_ref)
     count_ref[...] = count.astype(I32)
     table_ref[...] = jnp.concatenate(balanced, axis=0).astype(I32)
+    copies = [
+        pltpu.make_async_copy(table_ref, table_hbm, sems.at[6]),
+        pltpu.make_async_copy(count_ref, count_hbm, sems.at[7]),
+    ]
+    for copy in copies:
+        copy.start()
     places[...] = jnp.concatenate(balanced + overflow, axis=0)
     chosen = tissue_tiles(mask_ref)
     row_of = [pl.multiple_of(tile // 2 * TILE, TILE) for tile in chosen]
@@ -140,6 +157,8 @@
         jnp.concatenate([one_hot(index == places[pl.ds(first + tile, 1), :]) for tile in chosen], axis=1)
         for first in (0, tiles)
     ]
+    for copy in reads[2:4]:
+        copy.wait()
     half_xy = TAPS_XY // 2
     matrix_x = band(placed_taps(lambda m: px_ref[0, m], TAPS_XY, NX, lambda m: m - half_xy), NX, half_xy)
     matrix_y[...] = band(placed_taps(lambda m: py_ref[0, m], TAPS_XY, NY, lambda m: half_xy - m), NY, half_xy)
@@ -147,7 +166,6 @@
     block = ZB // group
     r = iota((ZB, ZB), 0)
     turn = one_hot(iota((ZB, ZB), 1) == r % group * block + r // group)
-    copies = []
 
     def rows_of(values, i):
         return jnp.concatenate(
@@ -279,7 +297,7 @@
         copy.wait()
 
 
-def column_kernel(me_ref, forward_ref, count_ref, in_ref, column_ref, padded):
+def column_kernel(forward_ref, count_ref, in_ref, column_ref, padded):
     group = SLAB * HALF
     rows = DEVS * group
     edge = ZB // 2
@@ -287,7 +305,7 @@
     padded[edge + rows :, :] = jnp.zeros((edge, 2 * TILE), BF16)
     padded[edge : edge + rows, 0:TILE] = in_ref[:, 0:group, :].reshape(rows, TILE)
     padded[edge : edge + rows, TILE:] = in_ref[:, group : 2 * group, :].reshape(rows, TILE)
-    count = count_ref[pl.ds(me_ref[0], 1), :].reshape(1, 1, TILE)
+    count = count_ref[pl.ds(lax.axis_index("space"), 1), :].reshape(1, 1, TILE)
     planes = ZB // HALF
     pairs = planes // 2
     sub = iota((pairs, 8, TILE), 1)
@@ -303,19 +321,28 @@
 
 
 def back_kernel(
-    me_ref, mask_ref, units_ref, rows_ref, in_ref, est_hbm, out_hbm,
-    est_ref, back_z, padded, out_ref, est_sem, out_sems,
+    mask_hbm, units_ref, rows_ref, in_ref, est_hbm, out_hbm,
+    mask_ref, est_ref, back_z, padded, out_ref, mask_sem, est_sem, out_sems,
 ):
-    est_copy = pltpu.make_async_copy(est_hbm.at[me_ref[0]], est_ref, est_sem)
+    mask_copy = pltpu.make_async_copy(mask_hbm, mask_ref, mask_sem)
+    est_copy = pltpu.make_async_copy(est_hbm.at[lax.axis_index("view")], est_ref, est_sem)
+    mask_copy.start()
     est_copy.start()
     edge = XB // 2
+    back_z[...] = jnp.ones((VIEWS, NX, NY), BF16)
+    bands, matrix_y = [], []
+    for view in range(VIEWS):
+        bands.append(rolled(rows_ref[view : view + 1, :], XB).astype(BF16))
+        matrix_y.append(band(rows_ref[VIEWS + view : VIEWS + view + 1, :], NY, TAPS_XY // 2))
+        padded[view, 0:edge, :] = jnp.zeros((edge, NY), BF16)
+        padded[view, edge + NX :, :] = jnp.zeros((edge, NY), BF16)
     cols = jnp.concatenate([in_ref[view] for view in range(VIEWS)], axis=1)
     units = units_ref[0:1, :]
     slots = HALF * DEVS
+    mask_copy.wait()
     chosen = tissue_tiles(mask_ref)
     here = [units == 2 * (tile // 2 * TILE + iota((TILE, slots), 0)) + tile % 2 for tile in chosen]
     found = dot(jnp.concatenate([one_hot(h) for h in here], axis=0), cols).astype(BF16)
-    back_z[...] = jnp.ones((VIEWS, NX, NY), BF16)
     for i, tile in enumerate(chosen):
         row = pl.multiple_of(tile // 2 * TILE, TILE)
         lane = pl.multiple_of(tile % 2 * TILE, TILE)
@@ -323,13 +350,8 @@
             back_z[view, pl.ds(row, TILE), pl.ds(lane, TILE)] = found[
                 i * TILE : (i + 1) * TILE, view * TILE : (view + 1) * TILE
             ]
-    bands = []
     for view in range(VIEWS):
-        bands.append(rolled(rows_ref[view : view + 1, :], XB).astype(BF16))
-        matrix_y = band(rows_ref[VIEWS + view : VIEWS + view + 1, :], NY, TAPS_XY // 2)
-        padded[view, 0:edge, :] = jnp.zeros((edge, NY), BF16)
-        padded[view, edge + NX :, :] = jnp.zeros((edge, NY), BF16)
-        padded[view, edge : edge + NX, :] = dot(back_z[view], matrix_y).astype(BF16)
+        padded[view, edge : edge + NX, :] = dot(back_z[view], matrix_y[view]).astype(BF16)
     est_copy.wait()
     writes = []
     for block in range(NX // XB):
@@ -365,17 +387,22 @@
         pack_kernel,
         "pack",
         (shape(DEVS, MSG, TILE), shape(UNITS // TILE, TILE, dtype=I32), shape(DEVS, TILE, dtype=I32)),
-        [SMEM, SMEM, SMEM, VMEM, ANY, ANY],
-        (ANY, VMEM, VMEM),
+        [ANY] * 6,
+        (ANY, ANY, ANY),
         [
+            pltpu.SMEM((UNITS // TILE,), I32),
+            pltpu.SMEM((1, TAPS_XY), F32),
+            pltpu.SMEM((1, TAPS_XY), F32),
+            pltpu.VMEM((1, UNITS), I32),
             pltpu.VMEM((SLAB, NX, NY), BF16),
             pltpu.VMEM((1, SLAB, NX, NY), BF16),
             pltpu.VMEM((SLAB, NX, NY), BF16),
             pltpu.VMEM((2 * UNITS // TILE, TILE), F32),
             pltpu.VMEM((NY, NY), BF16),
             pltpu.VMEM((DEVS, MSG, TILE), BF16),
-            pltpu.SemaphoreType.DMA,
-            pltpu.SemaphoreType.DMA,
+            pltpu.VMEM((UNITS // TILE, TILE), I32),
+            pltpu.VMEM((DEVS, TILE), I32),
+            pltpu.SemaphoreType.DMA((8,)),
             pltpu.SemaphoreType.DMA((DEVS * SLAB * HALF // ZB,)),
         ],
         WIDE_LIMIT,
@@ -422,40 +449,42 @@
     )(forward, adjoint, arrived)
 
 
-def column(space_index, forward, count, arrived):
+def column(forward, count, arrived):
     rows = DEVS * SLAB * HALF
     return call(
         column_kernel,
         "column",
         shape(SLAB * DEVS, 2 * HALF, TILE),
-        [SMEM, VMEM, VMEM, VMEM],
+        [VMEM, VMEM, VMEM],
         VMEM,
         [pltpu.VMEM((rows + ZB, 2 * TILE), BF16)],
         WIDE_LIMIT,
         flops=540_000_000,
         moved=3_000_000,
-    )(space_index, forward, count, arrived)
-
-
-def back(view_index, tissue_mask, units, rows, returned, estimate):
+    )(forward, count, arrived)
+
+
+def back(tissue_mask, units, rows, returned, estimate):
     return call(
         back_kernel,
         "back",
         shape(VIEWS, NX, NY),
-        [SMEM, SMEM, VMEM, VMEM, VMEM, HBM],
+        [ANY, VMEM, VMEM, VMEM, HBM],
         HBM,
         [
+            pltpu.SMEM((UNITS // TILE,), I32),
             pltpu.VMEM((NX, NY), BF16),
             pltpu.VMEM((VIEWS, NX, NY), BF16),
             pltpu.VMEM((VIEWS, NX + XB, NY), BF16),
             pltpu.VMEM((NX, NY), BF16),
+            pltpu.SemaphoreType.DMA,
             pltpu.SemaphoreType.DMA,
             pltpu.SemaphoreType.DMA((NX // XB, VIEWS)),
         ],
         LIMIT,
         flops=1_400_000_000,
         moved=5_000_000,
-    )(view_index, tissue_mask, units, rows, returned, estimate)
+    )(tissue_mask, units, rows, returned, estimate)
 
 
 def shards(estimate, measured, psf_x, psf_y, psf_z, tissue_mask, column_owner):
@@ -463,8 +492,6 @@
     arrived = lax.all_to_all(message, "space", split_axis=0, concat_axis=0, tiled=True)
     taps = lax.all_gather(jnp.concatenate([psf_x, psf_y], axis=1), "view", axis=0, tiled=True)
     forward, adjoint, rows, units = prep(psf_z, taps[:, :TAPS_XY], taps[:, TAPS_XY:], table)
-    space_index = lax.axis_index("space").astype(I32).reshape(1)
-    view_index = lax.axis_index("view").astype(I32).reshape(1)
     sent = z_pair(forward, adjoint, arrived)
     returned = lax.all_to_all(
         sent.reshape(VIEWS * DEVS, HALF, TILE),
@@ -473,8 +500,8 @@
         concat_axis=0,
         tiled=True,
     ).reshape(VIEWS, HALF * DEVS, TILE)
-    column_blur = column(space_index, forward, count, arrived)
-    updated = back(view_index, tissue_mask, units, rows, returned, estimate)
+    column_blur = column(forward, count, arrived)
+    updated = back(tissue_mask, units, rows, returned, estimate)
     updated = lax.all_to_all(updated, "view", split_axis=0, concat_axis=0, tiled=True)
     return updated, column_blur[None]
 

time: 125 us -> 123 us (0.984)
  blocking collectives: 8.22 us -> 41.3 us
  waiting for transfers between devices: 64.5 us -> 42.7 us
  starting transfers between devices: 33.5 us -> 22.1 us
  Pallas kernels: 16 us -> 14.2 us
    all_to_all x0 -> x1, blocking collectives: none -> 33.1 us  [shards(): lax.all_to_all(sent.reshape(VIEWS * DEVS, HALF, TILE), ('view', 'space'),...]
    all_to_all x1 -> x0, waiting for transfers between devices: 21.9 us -> none  [shards(): lax.all_to_all(sent.reshape(VIEWS * DEVS, HALF, TILE), ('view', 'space'),...]
    all_to_all x1 -> x0, starting transfers between devices: 11.4 us -> none  [shards(): lax.all_to_all(sent.reshape(VIEWS * DEVS, HALF, TILE), ('view', 'space'),...]
    pallas_call x1, Pallas kernels: 6.69 us -> 5.44 us  [pack(): call(pack_kernel, 'pack', (shape(DEVS, MSG, TILE), shape(UNITS // TILE, T...]
  transfers between devices with their start and end apart: 3 -> 2, of which waited for: 3 -> 2; matrix products, arithmetic and copies ran while one was open for 0% -> 0% of each run, Pallas kernels for 4% -> 4%
where the time goes in v5:
time: 123 us; the launch traced here: 122 us
  waiting for transfers between devices  42.7 us (35%)
  blocking collectives  41.3 us (34%)
  starting transfers between devices  22.1 us (18%)
  Pallas kernels  14.2 us (12%)
    all_to_all x1, blocking collectives, shards(): lax.all_to_all(sent.reshape(VIEWS * DEVS, HALF, TILE), ('view', 'space'),...  33.1 us
    all_to_all x1, waiting for transfers between devices, shards(): lax.all_to_all(message, 'space', split_axis=0, concat_axis=0, tiled=True)  31.2 us
    all_to_all x1, starting transfers between devices, shards(): lax.all_to_all(message, 'space', split_axis=0, concat_axis=0, tiled=True)  18.6 us
    all_to_all x1, waiting for transfers between devices, shards(): lax.all_to_all(updated, 'view', split_axis=0, concat_axis=0, tiled=True)  11.5 us
    all_gather x1, blocking collectives, shards(): lax.all_gather(jnp.concatenate([psf_x, psf_y], axis=1), 'view', axis=0, t...  8.23 us
    pallas_call x1, Pallas kernels, pack(): call(pack_kernel, 'pack', (shape(DEVS, MSG, TILE), shape(UNITS // TILE, T...  5.44 us
    all_to_all x1, starting transfers between devices, shards(): lax.all_to_all(updated, 'view', split_axis=0, concat_axis=0, tiled=True)  3.53 us
    pallas_call x1, Pallas kernels, column(): call(column_kernel, 'column', shape(SLAB * DEVS, 2 * HALF, TILE), [VMEM,...  3.25 us
  transfers between devices with their start and end apart: 2, of which 2 were waited for; matrix products, arithmetic and copies ran while one was open for 0% of the time, Pallas kernels for 4%

profile of v5, /device:TPU:1, one launch (start us, length us, event | category | flops | bytes accessed | tf_op | source)
XLA Modules:
  0.0 122.2 jit_solution(8755698963877308635)
XLA Ops:
  0.6 5.4 %pack.1 = (bf16[128,48,128]{2,1,0:T(8,128)(2,1)}, s32[8,128]{1,0:T(8,128)}, s32[128,128]{1,0:T(8,128)}) custom-call(s32[8]{0:T(128)} %mask_hbm.3, f32[1,31]{1,0:T(1,128)} %px_hbm.1, f32[1,31]{1,0:T(1,128)} %py_hbm.1, s32[1,1024]{1,0:T(1,128)} %bitcast.11, bf16[4,512,256]{2,1,0:T(8,128)(2,1)} %est_hbm.3, bf16[1,4,512,256]{3,2,1,0:T(8,128)(2,1)} %meas_hbm.1), custom_call_target="tpu_custom_call" | custom-call | flops 2000000000 | bytes 4000000 | tf_op jit(solution)/shard_map/pack/pallas_call | solution.py:386
  6.1 0.0 copy-start.6
  6.1 0.0 copy-start.7
  6.1 0.0 copy-start.3
  6.1 0.0 copy-start.5
  6.1 18.6 %all-to-all-start = ((bf16[128,48,128]{2,1,0:T(8,128)(2,1)}), bf16[128,48,128]{2,1,0:T(8,128)(2,1)S(1)}, u32[]{:S(2)}, u32[]{:S(2)}) async-start(bf16[128,48,128]{2,1,0:T(8,128)(2,1)} %get-tuple-element.14), calls=%async_computation | async-start | bytes 3145728 | tf_op jit(solution)/shard_map/all_to_all | solution.py:492
  24.7 0.0 copy-done.6
  24.7 0.0 copy-done.7
  24.7 0.1 maximum_bitcast_fusion
  24.8 8.2 %all-gather = f32[4,1,62]{2,1,0:T(1,128)S(1)} all-gather(f32[1,1,62]{2,1,0:T(1,128)S(1)} %maximum_bitcast_fusion), channel_id=1, replica_groups=mesh['view'=4,'space'=128] {'view'}, dimensions={0}, use_global_device_ids=true | all-gather | bytes 1240 | tf_op jit(solution)/shard_map/all_gather | solution.py:493
  33.0 0.1 fusion
  33.1 0.0 copy-done.3
  33.1 0.0 copy-done.5
  33.1 1.5 %prep.1 = (bf16[256,512]{1,0:T(8,128)(2,1)S(1)}, bf16[256,512]{1,0:T(8,128)(2,1)S(1)}, f32[8,256]{1,0:T(8,128)S(1)}, s32[8,512]{1,0:T(8,128)S(1)}) custom-call(f32[1,63]{1,0:T(1,128)S(1)} %copy-done.3, f32[4,31]{1,0:T(4,128)S(1)} %get-tuple-element.17.px_ref, f32[4,31]{1,0:T(4,128)S(1)} %get-tuple-element.16.py_ref, s32[8,128]{1,0:T(8,128)S(1)} %copy-done.5), custom_call_target="tpu_custom_call" | custom-call | flops 1000000000 | bytes 4000000 | tf_op jit(solution)/shard_map/prep/pallas_call | solution.py:415
  34.5 0.0 copy-start.1
  34.6 31.2 %all-to-all-done.in_ref = bf16[128,48,128]{2,1,0:T(8,128)(2,1)S(1)} async-done(((bf16[128,48,128]{2,1,0:T(8,128)(2,1)}), bf16[128,48,128]{2,1,0:T(8,128)(2,1)S(1)}, u32[]{:S(2)}, u32[]{:S(2)}) %all-to-all-start) | async-done | bytes 1572896 | tf_op jit(solution)/shard_map/all_to_all | solution.py:492
  65.8 1.3 %zpair.1 = bf16[4,512,128]{2,1,0:T(8,128)(2,1)S(1)} custom-call(bf16[256,512]{1,0:T(8,128)(2,1)S(1)} %get-tuple-element.12.forward_ref, bf16[256,512]{1,0:T(8,128)(2,1)S(1)} %get-tuple-element.13.adjoint_ref, bf16[128,48,128]{2,1,0:T(8,128)(2,1)S(1)} %all-to-all-done.in_ref), custom_call_target="tpu_custom_call" | custom-call | flops 540000000 | bytes 3000000 | tf_op jit(solution)/shard_map/zpair/pallas_call | solution.py:435
  67.1 33.1 %all_to_all.15 = bf16[512,4,128]{2,1,0:T(4,128)(2,1)S(1)} all-to-all(bf16[512,4,128]{2,1,0:T(4,128)(2,1)S(1)} %bitcast.7), channel_id=1, replica_groups=mesh['view'=4,'space'=128] {'view','space'}, dimensions={0} | all-to-all | bytes 1048576 | tf_op jit(solution)/shard_map/all_to_all | solution.py:496
  100.2 0.0 copy-done.2
  100.2 2.8 %back.1 = bf16[4,512,256]{2,1,0:T(8,128)(2,1)} custom-call(s32[8]{0:T(128)S(1)} %copy-done.4, s32[8,512]{1,0:T(8,128)S(1)} %get-tuple-element.10.units_ref, f32[8,256]{1,0:T(8,128)S(1)} %get-tuple-element.11.rows_ref, bf16[4,512,128]{2,1,0:T(8,128)(2,1)S(1)} %bitcast.8, bf16[4,512,256]{2,1,0:T(8,128)(2,1)S(1)} %copy-done.2), custom_call_target="tpu_custom_call" | custom-call | flops 1400000000 | bytes 5000000 | tf_op jit(solution)/shard_map/back/pallas_call | solution.py:468
  103.0 3.5 %all-to-all-start.2 = ((bf16[4,512,256]{2,1,0:T(8,128)(2,1)}), bf16[4,512,256]{2,1,0:T(8,128)(2,1)S(1)}, u32[]{:S(2)}, u32[]{:S(2)}) async-start(bf16[4,512,256]{2,1,0:T(8,128)(2,1)} %back.1), calls=%async_computation.2 | async-start | bytes 2097152 | tf_op jit(solution)/shard_map/all_to_all | solution.py:505
  106.5 3.3 %column.1 = bf16[512,8,128]{2,1,0:T(8,128)(2,1)} custom-call(bf16[256,512]{1,0:T(8,128)(2,1)} %copy-done.1, s32[128,128]{1,0:T(8,128)} %get-tuple-element.15.count_ref, bf16[128,48,128]{2,1,0:T(8,128)(2,1)} %copy-done), custom_call_target="tpu_custom_call" | custom-call | flops 540000000 | bytes 3000000 | tf_op jit(solution)/shard_map/column/pallas_call | solution.py:454
  109.8 11.5 %all-to-all-done.2 = bf16[4,512,256]{2,1,0:T(8,128)(2,1)S(1)} async-done(((bf16[4,512,256]{2,1,0:T(8,128)(2,1)}), bf16[4,512,256]{2,1,0:T(8,128)(2,1)S(1)}, u32[]{:S(2)}, u32[]{:S(2)}) %all-to-all-start.2) | async-done | bytes 1048608 | tf_op jit(solution)/shard_map/all_to_all | solution.py:505
  121.2 1.0 copy.11
  (6 shorter events, 0.0 us)
Async XLA Ops:
  6.1 18.6 %copy-start.6 = (f32[1,31]{1,0:T(1,128)S(1)}, f32[1,31]{1,0:T(1,128)}, u32[]{:S(2)}) copy-start(f32[1,31]{1,0:T(1,128)} %py_hbm.1) | copy-start | bytes 376
  6.1 18.6 %copy-start.7 = (f32[1,31]{1,0:T(1,128)S(1)}, f32[1,31]{1,0:T(1,128)}, u32[]{:S(2)}) copy-start(f32[1,31]{1,0:T(1,128)} %px_hbm.1) | copy-start | bytes 376
  6.1 27.0 %copy-start.3 = (f32[1,63]{1,0:T(1,128)S(1)}, f32[1,63]{1,0:T(1,128)}, u32[]{:S(2)}) copy-start(f32[1,63]{1,0:T(1,128)} %pz_ref.1) | copy-start | bytes 760
  6.1 27.0 %copy-start.5 = (s32[8,128]{1,0:T(8,128)S(1)}, s32[8,128]{1,0:T(8,128)}, u32[]{:S(2)}) copy-start(s32[8,128]{1,0:T(8,128)} %get-tuple-element.9.table_ref) | copy-start | bytes 12292
  6.1 59.7 %all-to-all-start = ((bf16[128,48,128]{2,1,0:T(8,128)(2,1)}), bf16[128,48,128]{2,1,0:T(8,128)(2,1)S(1)}, u32[]{:S(2)}, u32[]{:S(2)}) async-start(bf16[128,48,128]{2,1,0:T(8,128)(2,1)} %get-tuple-element.14), calls=%async_computation | async-start | bytes 3145728 | tf_op jit(solution)/shard_map/all_to_all | solution.py:492
  34.5 65.6 %copy-start.1 = (bf16[256,512]{1,0:T(8,128)(2,1)}, bf16[256,512]{1,0:T(8,128)(2,1)S(1)}, u32[]{:S(2)}) copy-start(bf16[256,512]{1,0:T(8,128)(2,1)S(1)} %get-tuple-element.12.forward_ref) | copy-start | bytes 786436
  65.8 34.4 %copy-start = (bf16[128,48,128]{2,1,0:T(8,128)(2,1)}, bf16[128,48,128]{2,1,0:T(8,128)(2,1)S(1)}, u32[]{:S(2)}) copy-start(bf16[128,48,128]{2,1,0:T(8,128)(2,1)S(1)} %all-to-all-done.in_ref) | copy-start | bytes 4718596
  65.8 34.4 %copy-start.2 = (bf16[4,512,256]{2,1,0:T(8,128)(2,1)S(1)}, bf16[4,512,256]{2,1,0:T(8,128)(2,1)}, u32[]{:S(2)}) copy-start(bf16[4,512,256]{2,1,0:T(8,128)(2,1)} %est_hbm.3) | copy-start | bytes 3145732
  65.8 34.4 %copy-start.4 = (s32[8]{0:T(128)S(1)}, s32[8]{0:T(128)}, u32[]{:S(2)}) copy-start(s32[8]{0:T(128)} %mask_hbm.3) | copy-start | bytes 100
  103.0 18.3 %all-to-all-start.2 = ((bf16[4,512,256]{2,1,0:T(8,128)(2,1)}), bf16[4,512,256]{2,1,0:T(8,128)(2,1)S(1)}, u32[]{:S(2)}, u32[]{:S(2)}) async-start(bf16[4,512,256]{2,1,0:T(8,128)(2,1)} %back.1), calls=%async_computation.2 | async-start | bytes 2097152 | tf_op jit(solution)/shard_map/all_to_all | solution.py:505

commit v6 on v5

--- a/solution.py
+++ b/solution.py
@@ -126,14 +126,14 @@
         pltpu.make_async_copy(source, target, sems.at[i])
         for i, (source, target) in enumerate(
             zip(
-                (mask_hbm, owner_hbm, px_hbm, py_hbm, meas_hbm, est_hbm),
-                (mask_ref, owner_ref, px_ref, py_ref, meas_ref, est_ref),
+                (mask_hbm, owner_hbm, px_hbm, py_hbm, est_hbm, meas_hbm),
+                (mask_ref, owner_ref, px_ref, py_ref, est_ref, meas_ref),
             )
         )
     ]
     for copy in reads:
         copy.start()
-    meas_copy, est_copy = reads[4:]
+    est_copy, meas_copy = reads[4:]
     for copy in reads[:2]:
         copy.wait()
     slots = HALF * DEVS
@@ -149,6 +149,15 @@
     for copy in copies:
         copy.start()
     places[...] = jnp.concatenate(balanced + overflow, axis=0)
+    for copy in reads[2:4]:
+        copy.wait()
+    half_xy = TAPS_XY // 2
+    matrix_x = band(placed_taps(lambda m: px_ref[0, m], TAPS_XY, NX, lambda m: m - half_xy), NX, half_xy)
+    matrix_y[...] = band(placed_taps(lambda m: py_ref[0, m], TAPS_XY, NY, lambda m: half_xy - m), NY, half_xy)
+
+    est_copy.wait()
+    for plane in range(SLAB):
+        along[plane] = dot(matrix_x, est_ref[plane]).astype(BF16)
     chosen = tissue_tiles(mask_ref)
     row_of = [pl.multiple_of(tile // 2 * TILE, TILE) for tile in chosen]
     lane_of = [pl.multiple_of(tile % 2 * TILE, TILE) for tile in chosen]
@@ -157,12 +166,6 @@
         jnp.concatenate([one_hot(index == places[pl.ds(first + tile, 1), :]) for tile in chosen], axis=1)
         for first in (0, tiles)
     ]
-    for copy in reads[2:4]:
-        copy.wait()
-    half_xy = TAPS_XY // 2
-    matrix_x = band(placed_taps(lambda m: px_ref[0, m], TAPS_XY, NX, lambda m: m - half_xy), NX, half_xy)
-    matrix_y[...] = band(placed_taps(lambda m: py_ref[0, m], TAPS_XY, NY, lambda m: half_xy - m), NY, half_xy)
-
     block = ZB // group
     r = iota((ZB, ZB), 0)
     turn = one_hot(iota((ZB, ZB), 1) == r % group * block + r // group)
@@ -188,9 +191,6 @@
         axis=0,
     )
     seen = dot(pick, seen).astype(BF16)
-    est_copy.wait()
-    for plane in range(SLAB):
-        along[plane] = dot(matrix_x, est_ref[plane]).astype(BF16)
     blurred = []
     for row, lane in zip(row_of, lane_of):
         rows = jnp.concatenate([along[plane, pl.ds(row, TILE), :] for plane in range(SLAB)], axis=0)
@@ -321,8 +321,8 @@
 
 
 def back_kernel(
-    mask_hbm, units_ref, rows_ref, in_ref, est_hbm, out_hbm,
-    mask_ref, est_ref, back_z, padded, out_ref, mask_sem, est_sem, out_sems,
+    mask_hbm, units_ref, rows_ref, in_ref, est_hbm, out_ref,
+    mask_ref, est_ref, back_z, padded, mask_sem, est_sem,
 ):
     mask_copy = pltpu.make_async_copy(mask_hbm, mask_ref, mask_sem)
     est_copy = pltpu.make_async_copy(est_hbm.at[lax.axis_index("view")], est_ref, est_sem)
@@ -353,20 +353,14 @@
     for view in range(VIEWS):
         padded[view, edge : edge + NX, :] = dot(back_z[view], matrix_y[view]).astype(BF16)
     est_copy.wait()
-    writes = []
     for block in range(NX // XB):
         here = pl.ds(block * XB, XB)
         summed = jnp.zeros((XB, NY), F32)
         for view in range(VIEWS):
             summed += dot(bands[view], padded[view, block * XB : block * XB + 2 * XB, :])
-        out_ref[here, :] = (est_ref[here, :].astype(F32) * summed / VIEWS).astype(BF16)
+        updated = (est_ref[here, :].astype(F32) * summed / VIEWS).astype(BF16)
         for view in range(VIEWS):
-            writes.append(
-                pltpu.make_async_copy(out_ref.at[here, :], out_hbm.at[view, here, :], out_sems.at[block, view])
-            )
-            writes[-1].start()
-    for write in writes:
-        write.wait()
+            out_ref[view, here, :] = updated
 
 
 def call(kernel, name, out_shape, in_specs, out_specs, scratch, limit, flops, moved):
@@ -470,16 +464,14 @@
         "back",
         shape(VIEWS, NX, NY),
         [ANY, VMEM, VMEM, VMEM, HBM],
-        HBM,
+        VMEM,
         [
             pltpu.SMEM((UNITS // TILE,), I32),
             pltpu.VMEM((NX, NY), BF16),
             pltpu.VMEM((VIEWS, NX, NY), BF16),
             pltpu.VMEM((VIEWS, NX + XB, NY), BF16),
-            pltpu.VMEM((NX, NY), BF16),
             pltpu.SemaphoreType.DMA,
             pltpu.SemaphoreType.DMA,
-            pltpu.SemaphoreType.DMA((NX // XB, VIEWS)),
         ],
         LIMIT,
         flops=1_400_000_000,

time: 123 us -> 122 us (level)
  no operation moved by 1% of the time
where the time goes in v6:
time: 122 us
  waiting for transfers between devices  42.7 us (35%)
  blocking collectives  41.3 us (34%)
  starting transfers between devices  22.1 us (18%)
  Pallas kernels  14.1 us (12%)
    all_to_all x1, blocking collectives, shards(): lax.all_to_all(sent.reshape(VIEWS * DEVS, HALF, TILE), ('view', 'space'),...  33.1 us
    all_to_all x1, waiting for transfers between devices, shards(): lax.all_to_all(message, 'space', split_axis=0, concat_axis=0, tiled=True)  31.2 us
    all_to_all x1, starting transfers between devices, shards(): lax.all_to_all(message, 'space', split_axis=0, concat_axis=0, tiled=True)  18.6 us
    all_to_all x1, waiting for transfers between devices, shards(): lax.all_to_all(updated, 'view', split_axis=0, concat_axis=0, tiled=True)  11.4 us
    all_gather x1, blocking collectives, shards(): lax.all_gather(jnp.concatenate([psf_x, psf_y], axis=1), 'view', axis=0, t...  8.23 us
    pallas_call x1, Pallas kernels, pack(): call(pack_kernel, 'pack', (shape(DEVS, MSG, TILE), shape(UNITS // TILE, T...  5.28 us
    all_to_all x1, starting transfers between devices, shards(): lax.all_to_all(updated, 'view', split_axis=0, concat_axis=0, tiled=True)  3.53 us
    pallas_call x1, Pallas kernels, column(): call(column_kernel, 'column', shape(SLAB * DEVS, 2 * HALF, TILE), [VMEM,...  3.26 us
  transfers between devices with their start and end apart: 2, of which 2 were waited for; matrix products, arithmetic and copies ran while one was open for 0% of the time, Pallas kernels for 4%

profile of v6, /device:TPU:1, one launch (start us, length us, event | category | flops | bytes accessed | tf_op | source)
XLA Modules:
  0.0 122.1 jit_solution(810634499404636714)
XLA Ops:
  0.6 5.3 %pack.1 = (bf16[128,48,128]{2,1,0:T(8,128)(2,1)}, s32[8,128]{1,0:T(8,128)}, s32[128,128]{1,0:T(8,128)}) custom-call(s32[8]{0:T(128)} %mask_hbm.3, f32[1,31]{1,0:T(1,128)} %px_hbm.1, f32[1,31]{1,0:T(1,128)} %py_hbm.1, s32[1,1024]{1,0:T(1,128)} %bitcast.11, bf16[4,512,256]{2,1,0:T(8,128)(2,1)} %est_hbm.3, bf16[1,4,512,256]{3,2,1,0:T(8,128)(2,1)} %meas_hbm.1), custom_call_target="tpu_custom_call" | custom-call | flops 2000000000 | bytes 4000000 | tf_op jit(solution)/shard_map/pack/pallas_call | solution.py:380
  5.9 0.0 copy-start.6
  5.9 0.0 copy-start.7
  5.9 0.0 copy-start.3
  6.0 0.0 copy-start.5
  6.0 18.6 %all-to-all-start = ((bf16[128,48,128]{2,1,0:T(8,128)(2,1)}), bf16[128,48,128]{2,1,0:T(8,128)(2,1)S(1)}, u32[]{:S(2)}, u32[]{:S(2)}) async-start(bf16[128,48,128]{2,1,0:T(8,128)(2,1)} %get-tuple-element.14), calls=%async_computation | async-start | bytes 3145728 | tf_op jit(solution)/shard_map/all_to_all | solution.py:484
  24.5 0.0 copy-done.6
  24.5 0.0 copy-done.7
  24.6 0.1 maximum_bitcast_fusion
  24.6 8.2 %all-gather = f32[4,1,62]{2,1,0:T(1,128)S(1)} all-gather(f32[1,1,62]{2,1,0:T(1,128)S(1)} %maximum_bitcast_fusion), channel_id=1, replica_groups=mesh['view'=4,'space'=128] {'view'}, dimensions={0}, use_global_device_ids=true | all-gather | bytes 1240 | tf_op jit(solution)/shard_map/all_gather | solution.py:485
  32.9 0.1 fusion
  32.9 0.0 copy-done.3
  32.9 0.0 copy-done.5
  32.9 1.5 %prep.1 = (bf16[256,512]{1,0:T(8,128)(2,1)S(1)}, bf16[256,512]{1,0:T(8,128)(2,1)S(1)}, f32[8,256]{1,0:T(8,128)S(1)}, s32[8,512]{1,0:T(8,128)S(1)}) custom-call(f32[1,63]{1,0:T(1,128)S(1)} %copy-done.3, f32[4,31]{1,0:T(4,128)S(1)} %get-tuple-element.17.px_ref, f32[4,31]{1,0:T(4,128)S(1)} %get-tuple-element.16.py_ref, s32[8,128]{1,0:T(8,128)S(1)} %copy-done.5), custom_call_target="tpu_custom_call" | custom-call | flops 1000000000 | bytes 4000000 | tf_op jit(solution)/shard_map/prep/pallas_call | solution.py:409
  34.4 0.0 copy-start.1
  34.4 31.2 %all-to-all-done.in_ref = bf16[128,48,128]{2,1,0:T(8,128)(2,1)S(1)} async-done(((bf16[128,48,128]{2,1,0:T(8,128)(2,1)}), bf16[128,48,128]{2,1,0:T(8,128)(2,1)S(1)}, u32[]{:S(2)}, u32[]{:S(2)}) %all-to-all-start) | async-done | bytes 1572896 | tf_op jit(solution)/shard_map/all_to_all | solution.py:484
  65.6 1.3 %zpair.1 = bf16[4,512,128]{2,1,0:T(8,128)(2,1)S(1)} custom-call(bf16[256,512]{1,0:T(8,128)(2,1)S(1)} %get-tuple-element.12.forward_ref, bf16[256,512]{1,0:T(8,128)(2,1)S(1)} %get-tuple-element.13.adjoint_ref, bf16[128,48,128]{2,1,0:T(8,128)(2,1)S(1)} %all-to-all-done.in_ref), custom_call_target="tpu_custom_call" | custom-call | flops 540000000 | bytes 3000000 | tf_op jit(solution)/shard_map/zpair/pallas_call | solution.py:429
  66.9 33.1 %all_to_all.15 = bf16[512,4,128]{2,1,0:T(4,128)(2,1)S(1)} all-to-all(bf16[512,4,128]{2,1,0:T(4,128)(2,1)S(1)} %bitcast.7), channel_id=1, replica_groups=mesh['view'=4,'space'=128] {'view','space'}, dimensions={0} | all-to-all | bytes 1048576 | tf_op jit(solution)/shard_map/all_to_all | solution.py:488
  100.0 0.0 copy-done
  100.0 2.8 %back.1 = bf16[4,512,256]{2,1,0:T(8,128)(2,1)} custom-call(s32[8]{0:T(128)S(1)} %copy-done.4, s32[8,512]{1,0:T(8,128)S(1)} %get-tuple-element.10.units_ref, f32[8,256]{1,0:T(8,128)S(1)} %get-tuple-element.11.rows_ref, bf16[4,512,128]{2,1,0:T(8,128)(2,1)S(1)} %bitcast.8, bf16[4,512,256]{2,1,0:T(8,128)(2,1)S(1)} %copy-done.2), custom_call_target="tpu_custom_call" | custom-call | flops 1400000000 | bytes 5000000 | tf_op jit(solution)/shard_map/back/pallas_call | solution.py:462
  102.9 3.5 %all-to-all-start.2 = ((bf16[4,512,256]{2,1,0:T(8,128)(2,1)}), bf16[4,512,256]{2,1,0:T(8,128)(2,1)S(1)}, u32[]{:S(2)}, u32[]{:S(2)}) async-start(bf16[4,512,256]{2,1,0:T(8,128)(2,1)} %back.1), calls=%async_computation.2 | async-start | bytes 2097152 | tf_op jit(solution)/shard_map/all_to_all | solution.py:497
  106.4 3.3 %column.1 = bf16[512,8,128]{2,1,0:T(8,128)(2,1)} custom-call(bf16[256,512]{1,0:T(8,128)(2,1)} %copy-done.1, s32[128,128]{1,0:T(8,128)} %get-tuple-element.15.count_ref, bf16[128,48,128]{2,1,0:T(8,128)(2,1)} %copy-done), custom_call_target="tpu_custom_call" | custom-call | flops 540000000 | bytes 3000000 | tf_op jit(solution)/shard_map/column/pallas_call | solution.py:448
  109.7 11.4 %all-to-all-done.2 = bf16[4,512,256]{2,1,0:T(8,128)(2,1)S(1)} async-done(((bf16[4,512,256]{2,1,0:T(8,128)(2,1)}), bf16[4,512,256]{2,1,0:T(8,128)(2,1)S(1)}, u32[]{:S(2)}, u32[]{:S(2)}) %all-to-all-start.2) | async-done | bytes 1048608 | tf_op jit(solution)/shard_map/all_to_all | solution.py:497
  121.1 1.0 copy.11
  (6 shorter events, 0.0 us)
Async XLA Ops:
  5.9 18.6 %copy-start.6 = (f32[1,31]{1,0:T(1,128)S(1)}, f32[1,31]{1,0:T(1,128)}, u32[]{:S(2)}) copy-start(f32[1,31]{1,0:T(1,128)} %py_hbm.1) | copy-start | bytes 376
  5.9 18.6 %copy-start.7 = (f32[1,31]{1,0:T(1,128)S(1)}, f32[1,31]{1,0:T(1,128)}, u32[]{:S(2)}) copy-start(f32[1,31]{1,0:T(1,128)} %px_hbm.1) | copy-start | bytes 376
  5.9 27.0 %copy-start.3 = (f32[1,63]{1,0:T(1,128)S(1)}, f32[1,63]{1,0:T(1,128)}, u32[]{:S(2)}) copy-start(f32[1,63]{1,0:T(1,128)} %pz_ref.1) | copy-start | bytes 760
  6.0 27.0 %copy-start.5 = (s32[8,128]{1,0:T(8,128)S(1)}, s32[8,128]{1,0:T(8,128)}, u32[]{:S(2)}) copy-start(s32[8,128]{1,0:T(8,128)} %get-tuple-element.9.table_ref) | copy-start | bytes 12292
  6.0 59.7 %all-to-all-start = ((bf16[128,48,128]{2,1,0:T(8,128)(2,1)}), bf16[128,48,128]{2,1,0:T(8,128)(2,1)S(1)}, u32[]{:S(2)}, u32[]{:S(2)}) async-start(bf16[128,48,128]{2,1,0:T(8,128)(2,1)} %get-tuple-element.14), calls=%async_computation | async-start | bytes 3145728 | tf_op jit(solution)/shard_map/all_to_all | solution.py:484
  34.4 65.6 %copy-start.1 = (bf16[256,512]{1,0:T(8,128)(2,1)}, bf16[256,512]{1,0:T(8,128)(2,1)S(1)}, u32[]{:S(2)}) copy-start(bf16[256,512]{1,0:T(8,128)(2,1)S(1)} %get-tuple-element.12.forward_ref) | copy-start | bytes 786436
  65.6 34.4 %copy-start = (bf16[128,48,128]{2,1,0:T(8,128)(2,1)}, bf16[128,48,128]{2,1,0:T(8,128)(2,1)S(1)}, u32[]{:S(2)}) copy-start(bf16[128,48,128]{2,1,0:T(8,128)(2,1)S(1)} %all-to-all-done.in_ref) | copy-start | bytes 4718596
  65.6 34.4 %copy-start.2 = (bf16[4,512,256]{2,1,0:T(8,128)(2,1)S(1)}, bf16[4,512,256]{2,1,0:T(8,128)(2,1)}, u32[]{:S(2)}) copy-start(bf16[4,512,256]{2,1,0:T(8,128)(2,1)} %est_hbm.3) | copy-start | bytes 3145732
  65.6 34.4 %copy-start.4 = (s32[8]{0:T(128)S(1)}, s32[8]{0:T(128)}, u32[]{:S(2)}) copy-start(s32[8]{0:T(128)} %mask_hbm.3) | copy-start | bytes 100
  102.9 18.2 %all-to-all-start.2 = ((bf16[4,512,256]{2,1,0:T(8,128)(2,1)}), bf16[4,512,256]{2,1,0:T(8,128)(2,1)S(1)}, u32[]{:S(2)}, u32[]{:S(2)}) async-start(bf16[4,512,256]{2,1,0:T(8,128)(2,1)} %back.1), calls=%async_computation.2 | async-start | bytes 2097152 | tf_op jit(solution)/shard_map/all_to_all | solution.py:497

commit v7 on v6

--- a/solution.py
+++ b/solution.py
@@ -452,7 +452,7 @@
         [VMEM, VMEM, VMEM],
         VMEM,
         [pltpu.VMEM((rows + ZB, 2 * TILE), BF16)],
-        WIDE_LIMIT,
+        LIMIT,
         flops=540_000_000,
         moved=3_000_000,
     )(forward, count, arrived)
@@ -492,7 +492,7 @@
         concat_axis=0,
         tiled=True,
     ).reshape(VIEWS, HALF * DEVS, TILE)
-    column_blur = column(forward, count, arrived)
+    returned, column_blur = lax.optimization_barrier((returned, column(forward, count, arrived)))
     updated = back(tissue_mask, units, rows, returned, estimate)
     updated = lax.all_to_all(updated, "view", split_axis=0, concat_axis=0, tiled=True)
     return updated, column_blur[None]

time: 122 us -> 121 us (level); the launches traced: 122 us -> 119 us
  blocking collectives: 41.3 us -> 24.2 us
  waiting for transfers between devices: 42.7 us -> 51.3 us
  starting transfers between devices: 22.1 us -> 30 us
  Pallas kernels: 14.1 us -> 12 us
    all_to_all x1, blocking collectives: 33.1 us -> 15.9 us  [shards(): lax.all_to_all(updated, 'view', split_axis=0, concat_axis=0, tiled=True)]
    all_to_all x1, waiting for transfers between devices: 11.4 us -> 20.1 us  [shards(): lax.all_to_all(sent.reshape(VIEWS * DEVS, HALF, TILE), ('view', 'space'),...]
    all_to_all x1, starting transfers between devices: 3.53 us -> 11.4 us  [shards(): lax.all_to_all(sent.reshape(VIEWS * DEVS, HALF, TILE), ('view', 'space'),...]
    pallas_call x1, Pallas kernels: 3.26 us -> 1.73 us  [column(): call(column_kernel, 'column', shape(SLAB * DEVS, 2 * HALF, TILE), [VMEM,...]
  transfers between devices with their start and end apart: 2 -> 2, of which waited for: 2 -> 2; matrix products, arithmetic and copies ran while one was open for 0% -> 0% of each run, Pallas kernels for 4% -> 3%
where the time goes in v7:
time: 121 us; the launch traced here: 119 us
  waiting for transfers between devices  51.3 us (42%)
  starting transfers between devices  30 us (25%)
  blocking collectives  24.2 us (20%)
  Pallas kernels  12 us (10%)
    all_to_all x1, waiting for transfers between devices, shards(): lax.all_to_all(message, 'space', split_axis=0, concat_axis=0, tiled=True)  31.2 us
    all_to_all x1, waiting for transfers between devices, shards(): lax.all_to_all(sent.reshape(VIEWS * DEVS, HALF, TILE), ('view', 'space'),...  20.1 us
    all_to_all x1, starting transfers between devices, shards(): lax.all_to_all(message, 'space', split_axis=0, concat_axis=0, tiled=True)  18.6 us
    all_to_all x1, blocking collectives, shards(): lax.all_to_all(updated, 'view', split_axis=0, concat_axis=0, tiled=True)  15.9 us
    all_to_all x1, starting transfers between devices, shards(): lax.all_to_all(sent.reshape(VIEWS * DEVS, HALF, TILE), ('view', 'space'),...  11.4 us
    all_gather x1, blocking collectives, shards(): lax.all_gather(jnp.concatenate([psf_x, psf_y], axis=1), 'view', axis=0, t...  8.23 us
    pallas_call x1, Pallas kernels, pack(): call(pack_kernel, 'pack', (shape(DEVS, MSG, TILE), shape(UNITS // TILE, T...  5.27 us
  transfers between devices with their start and end apart: 2, of which 2 were waited for; matrix products, arithmetic and copies ran while one was open for 0% of the time, Pallas kernels for 3%

profile of v7, /device:TPU:1, one launch (start us, length us, event | category | flops | bytes accessed | tf_op | source)
XLA Modules:
  0.0 119.3 jit_solution(13390585699376914977)
XLA Ops:
  0.6 5.3 %pack.1 = (bf16[128,48,128]{2,1,0:T(8,128)(2,1)}, s32[8,128]{1,0:T(8,128)}, s32[128,128]{1,0:T(8,128)}) custom-call(s32[8]{0:T(128)} %mask_hbm.3, f32[1,31]{1,0:T(1,128)} %px_hbm.1, f32[1,31]{1,0:T(1,128)} %py_hbm.1, s32[1,1024]{1,0:T(1,128)} %bitcast.10, bf16[4,512,256]{2,1,0:T(8,128)(2,1)} %est_hbm.3, bf16[1,4,512,256]{3,2,1,0:T(8,128)(2,1)} %meas_hbm.1), custom_call_target="tpu_custom_call" | custom-call | flops 2000000000 | bytes 4000000 | tf_op jit(solution)/shard_map/pack/pallas_call | solution.py:380
  5.9 0.0 copy-start.5
  5.9 0.0 copy-start.6
  5.9 0.0 copy-start.2
  5.9 0.0 copy-start.4
  6.0 18.6 %all-to-all-start = ((bf16[128,48,128]{2,1,0:T(8,128)(2,1)}), bf16[128,48,128]{2,1,0:T(8,128)(2,1)S(1)}, u32[]{:S(2)}, u32[]{:S(2)}) async-start(bf16[128,48,128]{2,1,0:T(8,128)(2,1)} %get-tuple-element.16), calls=%async_computation | async-start | bytes 3145728 | tf_op jit(solution)/shard_map/all_to_all | solution.py:484
  24.5 0.0 copy-done.5
  24.5 0.0 copy-done.6
  24.6 0.1 maximum_bitcast_fusion
  24.6 8.2 %all-gather = f32[4,1,62]{2,1,0:T(1,128)S(1)} all-gather(f32[1,1,62]{2,1,0:T(1,128)S(1)} %maximum_bitcast_fusion), channel_id=1, replica_groups=mesh['view'=4,'space'=128] {'view'}, dimensions={0}, use_global_device_ids=true | all-gather | bytes 1240 | tf_op jit(solution)/shard_map/all_gather | solution.py:485
  32.9 0.1 fusion
  32.9 0.0 copy-done.2
  32.9 1.5 %prep.1 = (bf16[256,512]{1,0:T(8,128)(2,1)S(1)}, bf16[256,512]{1,0:T(8,128)(2,1)S(1)}, f32[8,256]{1,0:T(8,128)S(1)}, s32[8,512]{1,0:T(8,128)S(1)}) custom-call(f32[1,63]{1,0:T(1,128)S(1)} %copy-done.2, f32[4,31]{1,0:T(4,128)S(1)} %get-tuple-element.21.px_ref, f32[4,31]{1,0:T(4,128)S(1)} %get-tuple-element.20.py_ref, s32[8,128]{1,0:T(8,128)S(1)} %copy-done.4), custom_call_target="tpu_custom_call" | custom-call | flops 1000000000 | bytes 4000000 | tf_op jit(solution)/shard_map/prep/pallas_call | solution.py:409
  34.4 31.2 %all-to-all-done.in_ref = bf16[128,48,128]{2,1,0:T(8,128)(2,1)S(1)} async-done(((bf16[128,48,128]{2,1,0:T(8,128)(2,1)}), bf16[128,48,128]{2,1,0:T(8,128)(2,1)S(1)}, u32[]{:S(2)}, u32[]{:S(2)}) %all-to-all-start) | async-done | bytes 1572896 | tf_op jit(solution)/shard_map/all_to_all | solution.py:484
  65.6 1.6 %zpair.1 = bf16[4,512,128]{2,1,0:T(8,128)(2,1)} custom-call(bf16[256,512]{1,0:T(8,128)(2,1)S(1)} %get-tuple-element.14.forward_ref, bf16[256,512]{1,0:T(8,128)(2,1)S(1)} %get-tuple-element.15.adjoint_ref, bf16[128,48,128]{2,1,0:T(8,128)(2,1)S(1)} %all-to-all-done.in_ref), custom_call_target="tpu_custom_call" | custom-call | flops 540000000 | bytes 3000000 | tf_op jit(solution)/shard_map/zpair/pallas_call | solution.py:429
  67.3 11.4 %all-to-all-start.1 = ((bf16[512,4,128]{2,1,0:T(4,128)(2,1)}), bf16[512,4,128]{2,1,0:T(4,128)(2,1)S(1)}, u32[]{:S(2)}, u32[]{:S(2)}) async-start(bf16[512,4,128]{2,1,0:T(4,128)(2,1)} %bitcast.3), calls=%async_computation.1 | async-start | bytes 1048576 | tf_op jit(solution)/shard_map/all_to_all | solution.py:488
  78.7 0.0 copy-start.1
  78.7 0.0 copy-start.3
  78.7 1.7 %column.1 = bf16[512,8,128]{2,1,0:T(8,128)(2,1)} custom-call(bf16[256,512]{1,0:T(8,128)(2,1)S(1)} %get-tuple-element.14.forward_ref, s32[128,128]{1,0:T(8,128)S(1)} %copy-done, bf16[128,48,128]{2,1,0:T(8,128)(2,1)S(1)} %all-to-all-done.in_ref), custom_call_target="tpu_custom_call" | custom-call | flops 540000000 | bytes 3000000 | tf_op jit(solution)/shard_map/column/pallas_call | solution.py:448
  80.4 20.1 %all-to-all-done.1 = bf16[512,4,128]{2,1,0:T(4,128)(2,1)S(1)} async-done(((bf16[512,4,128]{2,1,0:T(4,128)(2,1)}), bf16[512,4,128]{2,1,0:T(4,128)(2,1)S(1)}, u32[]{:S(2)}, u32[]{:S(2)}) %all-to-all-start.1) | async-done | bytes 524320 | tf_op jit(solution)/shard_map/all_to_all | solution.py:488
  100.5 0.0 copy-done.1
  100.5 1.9 %back.1 = bf16[4,512,256]{2,1,0:T(8,128)(2,1)S(1)} custom-call(s32[8]{0:T(128)S(1)} %copy-done.3, s32[8,512]{1,0:T(8,128)S(1)} %get-tuple-element.12.units_ref, f32[8,256]{1,0:T(8,128)S(1)} %get-tuple-element.13.rows_ref, bf16[4,512,128]{2,1,0:T(8,128)(2,1)S(1)} %bitcast.7, bf16[4,512,256]{2,1,0:T(8,128)(2,1)S(1)} %copy-done.1), custom_call_target="tpu_custom_call" | custom-call | flops 1400000000 | bytes 5000000 | tf_op jit(solution)/shard_map/back/pallas_call | solution.py:462
  102.4 15.9 %all_to_all.15 = bf16[4,512,256]{2,1,0:T(8,128)(2,1)S(1)} all-to-all(bf16[4,512,256]{2,1,0:T(8,128)(2,1)S(1)} %back.1), channel_id=1, replica_groups=mesh['view'=4,'space'=128] {'view'}, dimensions={0} | all-to-all | bytes 2097152 | tf_op jit(solution)/shard_map/all_to_all | solution.py:497
  118.3 1.0 copy.11
  (4 shorter events, 0.0 us)
Async XLA Ops:
  5.9 18.6 %copy-start.5 = (f32[1,31]{1,0:T(1,128)S(1)}, f32[1,31]{1,0:T(1,128)}, u32[]{:S(2)}) copy-start(f32[1,31]{1,0:T(1,128)} %py_hbm.1) | copy-start | bytes 376
  5.9 18.6 %copy-start.6 = (f32[1,31]{1,0:T(1,128)S(1)}, f32[1,31]{1,0:T(1,128)}, u32[]{:S(2)}) copy-start(f32[1,31]{1,0:T(1,128)} %px_hbm.1) | copy-start | bytes 376
  5.9 27.0 %copy-start.2 = (f32[1,63]{1,0:T(1,128)S(1)}, f32[1,63]{1,0:T(1,128)}, u32[]{:S(2)}) copy-start(f32[1,63]{1,0:T(1,128)} %pz_ref.1) | copy-start | bytes 760
  5.9 27.0 %copy-start.4 = (s32[8,128]{1,0:T(8,128)S(1)}, s32[8,128]{1,0:T(8,128)}, u32[]{:S(2)}) copy-start(s32[8,128]{1,0:T(8,128)} %get-tuple-element.11.table_ref) | copy-start | bytes 12292
  6.0 59.7 %all-to-all-start = ((bf16[128,48,128]{2,1,0:T(8,128)(2,1)}), bf16[128,48,128]{2,1,0:T(8,128)(2,1)S(1)}, u32[]{:S(2)}, u32[]{:S(2)}) async-start(bf16[128,48,128]{2,1,0:T(8,128)(2,1)} %get-tuple-element.16), calls=%async_computation | async-start | bytes 3145728 | tf_op jit(solution)/shard_map/all_to_all | solution.py:484
  65.6 13.1 %copy-start = (s32[128,128]{1,0:T(8,128)S(1)}, s32[128,128]{1,0:T(8,128)}, u32[]{:S(2)}) copy-start(s32[128,128]{1,0:T(8,128)} %get-tuple-element.17.count_ref) | copy-start | bytes 196612
  67.3 33.2 %all-to-all-start.1 = ((bf16[512,4,128]{2,1,0:T(4,128)(2,1)}), bf16[512,4,128]{2,1,0:T(4,128)(2,1)S(1)}, u32[]{:S(2)}, u32[]{:S(2)}) async-start(bf16[512,4,128]{2,1,0:T(4,128)(2,1)} %bitcast.3), calls=%async_computation.1 | async-start | bytes 1048576 | tf_op jit(solution)/shard_map/all_to_all | solution.py:488
  78.7 21.9 %copy-start.1 = (bf16[4,512,256]{2,1,0:T(8,128)(2,1)S(1)}, bf16[4,512,256]{2,1,0:T(8,128)(2,1)}, u32[]{:S(2)}) copy-start(bf16[4,512,256]{2,1,0:T(8,128)(2,1)} %est_hbm.3) | copy-start | bytes 3145732
  78.7 21.9 %copy-start.3 = (s32[8]{0:T(128)S(1)}, s32[8]{0:T(128)}, u32[]{:S(2)}) copy-start(s32[8]{0:T(128)} %mask_hbm.3) | copy-start | bytes 100

commit v8 on v7

--- a/solution.py
+++ b/solution.py
@@ -22,7 +22,6 @@
 SMEM = pl.BlockSpec(memory_space=pltpu.SMEM)
 VMEM = pl.BlockSpec(memory_space=pltpu.VMEM)
 ANY = pl.BlockSpec(memory_space=pl.ANY)
-HBM = pl.BlockSpec(memory_space=pltpu.HBM)
 
 
 def shape(*dims, dtype=BF16):
@@ -118,22 +117,22 @@
 
 
 def pack_kernel(
-    mask_hbm, px_hbm, py_hbm, owner_hbm, est_hbm, meas_hbm, out_hbm, table_hbm, count_hbm,
-    mask_ref, px_ref, py_ref, owner_ref, est_ref, meas_ref, along, places, matrix_y,
-    out_ref, table_ref, count_ref, sems, out_sem,
+    mask_hbm, px_hbm, py_hbm, pz_hbm, owner_hbm, est_hbm, meas_hbm, out_hbm, table_hbm, count_hbm, rows_hbm,
+    mask_ref, px_ref, py_ref, pz_ref, owner_ref, est_ref, meas_ref, along, places, matrix_y,
+    out_ref, table_ref, count_ref, rows_ref, sems, out_sem,
 ):
     reads = [
         pltpu.make_async_copy(source, target, sems.at[i])
         for i, (source, target) in enumerate(
             zip(
-                (mask_hbm, owner_hbm, px_hbm, py_hbm, est_hbm, meas_hbm),
-                (mask_ref, owner_ref, px_ref, py_ref, est_ref, meas_ref),
+                (mask_hbm, owner_hbm, px_hbm, py_hbm, pz_hbm, est_hbm, meas_hbm),
+                (mask_ref, owner_ref, px_ref, py_ref, pz_ref, est_ref, meas_ref),
             )
         )
     ]
     for copy in reads:
         copy.start()
-    est_copy, meas_copy = reads[4:]
+    est_copy, meas_copy = reads[5:]
     for copy in reads[:2]:
         copy.wait()
     slots = HALF * DEVS
@@ -142,15 +141,23 @@
     balanced, overflow, count = slot_rows(mask_ref, owner_ref)
     count_ref[...] = count.astype(I32)
     table_ref[...] = jnp.concatenate(balanced, axis=0).astype(I32)
+    places[...] = jnp.concatenate(balanced + overflow, axis=0)
+    for copy in reads[2:5]:
+        copy.wait()
+    half_z = TAPS_Z // 2
+    near = ZB // 2 - HALF * half_z
+    far = ZB // 2 + HALF * half_z
+    ahead = placed_taps(lambda m: pz_ref[0, m], TAPS_Z, 2 * ZB, lambda m: near + HALF * m)
+    behind = placed_taps(lambda m: pz_ref[0, m], TAPS_Z, 2 * ZB, lambda m: far - HALF * m)
+    rows_ref[...] = jnp.concatenate([ahead, behind] * 4, axis=0)
     copies = [
-        pltpu.make_async_copy(table_ref, table_hbm, sems.at[6]),
-        pltpu.make_async_copy(count_ref, count_hbm, sems.at[7]),
+        pltpu.make_async_copy(source, target, sems.at[len(reads) + i])
+        for i, (source, target) in enumerate(
+            zip((table_ref, count_ref, rows_ref), (table_hbm, count_hbm, rows_hbm))
+        )
     ]
     for copy in copies:
         copy.start()
-    places[...] = jnp.concatenate(balanced + overflow, axis=0)
-    for copy in reads[2:4]:
-        copy.wait()
     half_xy = TAPS_XY // 2
     matrix_x = band(placed_taps(lambda m: px_ref[0, m], TAPS_XY, NX, lambda m: m - half_xy), NX, half_xy)
     matrix_y[...] = band(placed_taps(lambda m: py_ref[0, m], TAPS_XY, NY, lambda m: half_xy - m), NY, half_xy)
@@ -213,22 +220,9 @@
         copy.wait()
 
 
-def prep_kernel(pz_ref, px_ref, py_ref, table_ref, forward_ref, adjoint_ref, rows_ref, units_ref):
-    group = SLAB * HALF
-    edge = ZB // 2
-    half_z = TAPS_Z // 2
-    near = edge - HALF * half_z
-    far = edge + HALF * half_z
-    forward_ref[...] = rolled(
-        placed_taps(lambda m: pz_ref[0, m], TAPS_Z, 2 * ZB, lambda m: near + HALF * m), ZB
-    ).astype(BF16)
-    adjoint = rolled(
-        placed_taps(lambda m: pz_ref[0, m], TAPS_Z, 2 * ZB, lambda m: far - HALF * m), ZB
-    ).astype(BF16)
-    r = iota((ZB, ZB), 0)
-    part = ZB // SLAB
-    source = r % part // HALF * group + r // part * HALF + r % HALF
-    adjoint_ref[...] = dot(one_hot(iota((ZB, ZB), 1) == source), adjoint).astype(BF16)
+def prep_kernel(px_ref, py_ref, table_ref, est_hbm, rows_ref, units_ref, plane_ref, sem):
+    plane_copy = pltpu.make_async_copy(est_hbm.at[lax.axis_index("view")], plane_ref, sem)
+    plane_copy.start()
     half_xy = TAPS_XY // 2
     for view in range(VIEWS):
         rows_ref[view : view + 1, :] = placed_taps(
@@ -248,15 +242,22 @@
         unit = 2 * (tile // 2 * TILE + iota((TILE, slots), 0)) + tile % 2
         total += jnp.sum(jnp.where(place == iota((TILE, slots), 1), unit, 0), axis=0, keepdims=True)
     units_ref[...] = jnp.broadcast_to(total, (8, slots))
-
-
-def z_kernel(forward_ref, adjoint_ref, in_ref, back_hbm, ratio, back_ref, sems):
+    plane_copy.wait()
+
+
+def z_kernel(rows_ref, in_ref, back_ref, ratio):
     group = SLAB * HALF
     rows = DEVS * group
     blocks = rows // ZB
     edge = ZB // 2
     block = ZB // group
     none = jnp.zeros((edge, TILE), BF16)
+    part = ZB // SLAB
+    forward = rolled(rows_ref[0:1, :], ZB).astype(BF16)
+    r = iota((ZB, ZB), 0)
+    source = r % part // HALF * group + r // part * HALF + r % HALF
+    adjoint = rolled(rows_ref[1:2, :], ZB).astype(BF16)
+    adjoint = dot(one_hot(iota((ZB, ZB), 1) == source), adjoint).astype(BF16)
 
     def window(block_at):
         first, last = block_at * block - block // 2, (block_at + 1) * block + block // 2
@@ -268,36 +269,25 @@
     ratio[edge + rows :, :] = none
     for i in range(blocks // 2):
         pair = (i, i + blocks // 2)
-        both = dot(forward_ref[...], jnp.concatenate([window(j) for j in pair], axis=1))
+        both = dot(forward, jnp.concatenate([window(j) for j in pair], axis=1))
         for half, j in enumerate(pair):
             seen = in_ref[j * block : (j + 1) * block, 2 * group :, :].reshape(ZB, TILE)
             ratio[edge + j * ZB : edge + (j + 1) * ZB, :] = (
                 seen.astype(F32) / both[:, half * TILE : (half + 1) * TILE]
             ).astype(BF16)
-    part = ZB // SLAB
-    copies = []
     for i in range(blocks // 2):
         pair = (i, i + blocks // 2)
         both = dot(
-            adjoint_ref[...], jnp.concatenate([ratio[j * ZB : j * ZB + 2 * ZB, :] for j in pair], axis=1)
+            adjoint, jnp.concatenate([ratio[j * ZB : j * ZB + 2 * ZB, :] for j in pair], axis=1)
         ).astype(BF16)
         for half, j in enumerate(pair):
             for plane in range(SLAB):
                 back_ref[plane, j * part : (j + 1) * part, :] = both[
                     plane * part : (plane + 1) * part, half * TILE : (half + 1) * TILE
                 ]
-        if i % 2:
-            for half, j in enumerate(pair):
-                here = pl.ds((j - 1) * part, 2 * part)
-                copies.append(
-                    pltpu.make_async_copy(back_ref.at[:, here, :], back_hbm.at[:, here, :], sems.at[i // 2, half])
-                )
-                copies[-1].start()
-    for copy in copies:
-        copy.wait()
-
-
-def column_kernel(forward_ref, count_ref, in_ref, column_ref, padded):
+
+
+def column_kernel(rows_ref, count_ref, in_ref, column_ref, padded):
     group = SLAB * HALF
     rows = DEVS * group
     edge = ZB // 2
@@ -306,12 +296,13 @@
     padded[edge : edge + rows, 0:TILE] = in_ref[:, 0:group, :].reshape(rows, TILE)
     padded[edge : edge + rows, TILE:] = in_ref[:, group : 2 * group, :].reshape(rows, TILE)
     count = count_ref[pl.ds(lax.axis_index("space"), 1), :].reshape(1, 1, TILE)
+    forward = rolled(rows_ref[0:1, :], ZB).astype(BF16)
     planes = ZB // HALF
     pairs = planes // 2
     sub = iota((pairs, 8, TILE), 1)
     live = sub < count
     for block in range(rows // ZB):
-        values = dot(forward_ref[...], padded[block * ZB : block * ZB + 2 * ZB, :])
+        values = dot(forward, padded[block * ZB : block * ZB + 2 * ZB, :])
         own = values[:, :TILE].reshape(pairs, 8, TILE)
         more = values[:, TILE:].reshape(pairs, 8, TILE)
         first = jnp.where(sub < HALF, own, pltpu.roll(more, HALF, 1))
@@ -321,13 +312,10 @@
 
 
 def back_kernel(
-    mask_hbm, units_ref, rows_ref, in_ref, est_hbm, out_ref,
-    mask_ref, est_ref, back_z, padded, mask_sem, est_sem,
+    mask_hbm, units_ref, rows_ref, in_ref, est_ref, out_ref, mask_ref, back_z, padded, mask_sem,
 ):
     mask_copy = pltpu.make_async_copy(mask_hbm, mask_ref, mask_sem)
-    est_copy = pltpu.make_async_copy(est_hbm.at[lax.axis_index("view")], est_ref, est_sem)
     mask_copy.start()
-    est_copy.start()
     edge = XB // 2
     back_z[...] = jnp.ones((VIEWS, NX, NY), BF16)
     bands, matrix_y = [], []
@@ -352,7 +340,6 @@
             ]
     for view in range(VIEWS):
         padded[view, edge : edge + NX, :] = dot(back_z[view], matrix_y[view]).astype(BF16)
-    est_copy.wait()
     for block in range(NX // XB):
         here = pl.ds(block * XB, XB)
         summed = jnp.zeros((XB, NY), F32)
@@ -376,17 +363,23 @@
     )
 
 
-def pack(estimate, measured, psf_x, psf_y, tissue_mask, column_owner):
+def pack(estimate, measured, psf_x, psf_y, psf_z, tissue_mask, column_owner):
     return call(
         pack_kernel,
         "pack",
-        (shape(DEVS, MSG, TILE), shape(UNITS // TILE, TILE, dtype=I32), shape(DEVS, TILE, dtype=I32)),
-        [ANY] * 6,
-        (ANY, ANY, ANY),
+        (
+            shape(DEVS, MSG, TILE),
+            shape(UNITS // TILE, TILE, dtype=I32),
+            shape(DEVS, TILE, dtype=I32),
+            shape(8, 2 * ZB, dtype=F32),
+        ),
+        [ANY] * 7,
+        (ANY,) * 4,
         [
             pltpu.SMEM((UNITS // TILE,), I32),
             pltpu.SMEM((1, TAPS_XY), F32),
             pltpu.SMEM((1, TAPS_XY), F32),
+            pltpu.SMEM((1, TAPS_Z), F32),
             pltpu.VMEM((1, UNITS), I32),
             pltpu.VMEM((SLAB, NX, NY), BF16),
             pltpu.VMEM((1, SLAB, NX, NY), BF16),
@@ -396,95 +389,84 @@
             pltpu.VMEM((DEVS, MSG, TILE), BF16),
             pltpu.VMEM((UNITS // TILE, TILE), I32),
             pltpu.VMEM((DEVS, TILE), I32),
-            pltpu.SemaphoreType.DMA((8,)),
+            pltpu.VMEM((8, 2 * ZB), F32),
+            pltpu.SemaphoreType.DMA((10,)),
             pltpu.SemaphoreType.DMA((DEVS * SLAB * HALF // ZB,)),
         ],
         WIDE_LIMIT,
         flops=2_000_000_000,
         moved=4_000_000,
-    )(tissue_mask, psf_x, psf_y, column_owner.reshape(1, UNITS), estimate, measured)
-
-
-def prep(psf_z, taps_x, taps_y, table):
+    )(tissue_mask, psf_x, psf_y, psf_z, column_owner.reshape(1, UNITS), estimate, measured)
+
+
+def prep(taps_x, taps_y, table, estimate):
     return call(
         prep_kernel,
         "prep",
-        (
-            shape(ZB, 2 * ZB),
-            shape(ZB, 2 * ZB),
-            shape(2 * VIEWS, NY, dtype=F32),
-            shape(8, HALF * DEVS, dtype=I32),
-        ),
-        [SMEM, SMEM, SMEM, VMEM],
-        (VMEM,) * 4,
-        [],
+        (shape(2 * VIEWS, NY, dtype=F32), shape(8, HALF * DEVS, dtype=I32), shape(NX, NY)),
+        [SMEM, SMEM, VMEM, ANY],
+        (VMEM,) * 3,
+        [pltpu.SemaphoreType.DMA],
         LIMIT,
-        flops=1_000_000_000,
-        moved=4_000_000,
-    )(psf_z, taps_x, taps_y, table)
-
-
-def z_pair(forward, adjoint, arrived):
-    rows = DEVS * SLAB * HALF
+        flops=10_000_000,
+        moved=1_000_000,
+    )(taps_x, taps_y, table, estimate)
+
+
+def z_pair(rows, arrived):
+    depth = DEVS * SLAB * HALF
     return call(
         z_kernel,
         "zpair",
         shape(VIEWS, HALF * DEVS, TILE),
-        [VMEM, VMEM, VMEM],
-        ANY,
-        [
-            pltpu.VMEM((rows + ZB, TILE), BF16),
-            pltpu.VMEM((VIEWS, HALF * DEVS, TILE), BF16),
-            pltpu.SemaphoreType.DMA((rows // ZB // 4, 2)),
-        ],
+        [VMEM, VMEM],
+        VMEM,
+        [pltpu.VMEM((depth + ZB, TILE), BF16)],
         LIMIT,
         flops=540_000_000,
         moved=3_000_000,
-    )(forward, adjoint, arrived)
-
-
-def column(forward, count, arrived):
-    rows = DEVS * SLAB * HALF
+    )(rows, arrived)
+
+
+def column(rows, count, arrived):
+    depth = DEVS * SLAB * HALF
     return call(
         column_kernel,
         "column",
         shape(SLAB * DEVS, 2 * HALF, TILE),
         [VMEM, VMEM, VMEM],
         VMEM,
-        [pltpu.VMEM((rows + ZB, 2 * TILE), BF16)],
+        [pltpu.VMEM((depth + ZB, 2 * TILE), BF16)],
         LIMIT,
         flops=540_000_000,
         moved=3_000_000,
-    )(forward, count, arrived)
-
-
-def back(tissue_mask, units, rows, returned, estimate):
+    )(rows, count, arrived)
+
+
+def back(tissue_mask, units, rows, returned, plane):
     return call(
         back_kernel,
         "back",
         shape(VIEWS, NX, NY),
-        [ANY, VMEM, VMEM, VMEM, HBM],
+        [ANY, VMEM, VMEM, VMEM, VMEM],
         VMEM,
         [
             pltpu.SMEM((UNITS // TILE,), I32),
-            pltpu.VMEM((NX, NY), BF16),
             pltpu.VMEM((VIEWS, NX, NY), BF16),
             pltpu.VMEM((VIEWS, NX + XB, NY), BF16),
-            pltpu.SemaphoreType.DMA,
             pltpu.SemaphoreType.DMA,
         ],
         LIMIT,
         flops=1_400_000_000,
         moved=5_000_000,
-    )(tissue_mask, units, rows, returned, estimate)
+    )(tissue_mask, units, rows, returned, plane)
 
 
 def shards(estimate, measured, psf_x, psf_y, psf_z, tissue_mask, column_owner):
-    message, table, count = pack(estimate, measured, psf_x, psf_y, tissue_mask, column_owner)
+    message, table, count, rows_z = pack(estimate, measured, psf_x, psf_y, psf_z, tissue_mask, column_owner)
     arrived = lax.all_to_all(message, "space", split_axis=0, concat_axis=0, tiled=True)
-    taps = lax.all_gather(jnp.concatenate([psf_x, psf_y], axis=1), "view", axis=0, tiled=True)
-    forward, adjoint, rows, units = prep(psf_z, taps[:, :TAPS_XY], taps[:, TAPS_XY:], table)
-    sent = z_pair(forward, adjoint, arrived)
+    arrived, psf_x, psf_y = lax.optimization_barrier((arrived, psf_x, psf_y))
+    sent = z_pair(rows_z, arrived)
     returned = lax.all_to_all(
         sent.reshape(VIEWS * DEVS, HALF, TILE),
         ("view", "space"),
@@ -492,8 +474,10 @@
         concat_axis=0,
         tiled=True,
     ).reshape(VIEWS, HALF * DEVS, TILE)
-    returned, column_blur = lax.optimization_barrier((returned, column(forward, count, arrived)))
-    updated = back(tissue_mask, units, rows, returned, estimate)
+    taps = lax.all_gather(jnp.concatenate([psf_x, psf_y], axis=1), "view", axis=0, tiled=True)
+    rows, units, plane = prep(taps[:, :TAPS_XY], taps[:, TAPS_XY:], table, estimate)
+    returned, column_blur = lax.optimization_barrier((returned, column(rows_z, count, arrived)))
+    updated = back(tissue_mask, units, rows, returned, plane)
     updated = lax.all_to_all(updated, "view", split_axis=0, concat_axis=0, tiled=True)
     return updated, column_blur[None]
 

time: 121 us -> 121 us (level)
  blocking collectives: 24.2 us -> 83.2 us
  waiting for transfers between devices: 51.3 us -> 10.9 us
  starting transfers between devices: 30 us -> 11.4 us
    all_to_all x0 -> x1, blocking collectives: none -> 59.5 us  [shards(): lax.all_to_all(message, 'space', split_axis=0, concat_axis=0, tiled=True)]
    all_to_all x1 -> x0, waiting for transfers between devices: 31.2 us -> none  [shards(): lax.all_to_all(message, 'space', split_axis=0, concat_axis=0, tiled=True)]
    all_to_all x1 -> x0, starting transfers between devices: 18.6 us -> none  [shards(): lax.all_to_all(message, 'space', split_axis=0, concat_axis=0, tiled=True)]
    all_to_all x1, waiting for transfers between devices: 20.1 us -> 10.9 us  [shards(): lax.all_to_all(sent.reshape(VIEWS * DEVS, HALF, TILE), ('view', 'space'),...]
  transfers between devices with their start and end apart: 2 -> 1, of which waited for: 2 -> 1; matrix products, arithmetic and copies ran while one was open for 0% -> 0% of each run, Pallas kernels for 3% -> 3%
where the time goes in v8:
time: 121 us; the launch traced here: 119 us
  blocking collectives  83.2 us (69%)
  Pallas kernels  12 us (10%)
  starting transfers between devices  11.4 us (9%)
  waiting for transfers between devices  10.9 us (9%)
    all_to_all x1, blocking collectives, shards(): lax.all_to_all(message, 'space', split_axis=0, concat_axis=0, tiled=True)  59.5 us
    all_to_all x1, blocking collectives, shards(): lax.all_to_all(updated, 'view', split_axis=0, concat_axis=0, tiled=True)  15.9 us
    all_to_all x1, starting transfers between devices, shards(): lax.all_to_all(sent.reshape(VIEWS * DEVS, HALF, TILE), ('view', 'space'),...  11.4 us
    all_to_all x1, waiting for transfers between devices, shards(): lax.all_to_all(sent.reshape(VIEWS * DEVS, HALF, TILE), ('view', 'space'),...  10.9 us
    all_gather x1, blocking collectives, shards(): lax.all_gather(jnp.concatenate([psf_x, psf_y], axis=1), 'view', axis=0, t...  7.76 us
    pallas_call x1, Pallas kernels, pack(): call(pack_kernel, 'pack', (shape(DEVS, MSG, TILE), shape(UNITS // TILE, T...  5.3 us
  transfers between devices with their start and end apart: 1, of which 1 were waited for; matrix products, arithmetic and copies ran while one was open for 0% of the time, Pallas kernels for 3%

profile of v8, /device:TPU:1, one launch (start us, length us, event | category | flops | bytes accessed | tf_op | source)
XLA Modules:
  0.0 119.3 jit_solution(934840671349408119)
XLA Ops:
  0.6 5.3 %pack.1 = (bf16[128,48,128]{2,1,0:T(8,128)(2,1)}, s32[8,128]{1,0:T(8,128)}, s32[128,128]{1,0:T(8,128)}, f32[8,512]{1,0:T(8,128)}) custom-call(s32[8]{0:T(128)} %mask_hbm.3, f32[1,31]{1,0:T(1,128)} %px_hbm.1, f32[1,31]{1,0:T(1,128)} %py_hbm.1, f32[1,63]{1,0:T(1,128)} %pz_hbm.1, s32[1,1024]{1,0:T(1,128)} %bitcast.10, bf16[4,512,256]{2,1,0:T(8,128)(2,1)} %est_hbm.3, ...), custom_call_target="tpu_custom_call" | custom-call | flops 2000000000 | bytes 4000000 | tf_op jit(solution)/shard_map/pack/pallas_call | solution.py:367
  5.9 0.0 copy-start.1
  6.0 59.5 %all_to_all.15.in_ref = bf16[128,48,128]{2,1,0:T(8,128)(2,1)S(1)} all-to-all(bf16[128,48,128]{2,1,0:T(8,128)(2,1)} %get-tuple-element.14), channel_id=1, replica_groups=mesh['view'=4,'space'=128] {'space'}, dimensions={0} | all-to-all | bytes 3145728 | tf_op jit(solution)/shard_map/all_to_all | solution.py:467
  65.5 0.0 copy-done.1
  65.5 0.0 copy-start.5
  65.5 0.0 copy-start.3
  65.5 1.8 %zpair.1 = bf16[4,512,128]{2,1,0:T(8,128)(2,1)} custom-call(f32[8,512]{1,0:T(8,128)S(1)} %copy-done.1, bf16[128,48,128]{2,1,0:T(8,128)(2,1)S(1)} %all_to_all.15.in_ref), custom_call_target="tpu_custom_call" | custom-call | flops 540000000 | bytes 3000000 | tf_op jit(solution)/shard_map/zpair/pallas_call | solution.py:418
  67.4 11.4 %all-to-all-start.1 = ((bf16[512,4,128]{2,1,0:T(4,128)(2,1)}), bf16[512,4,128]{2,1,0:T(4,128)(2,1)S(1)}, u32[]{:S(2)}, u32[]{:S(2)}) async-start(bf16[512,4,128]{2,1,0:T(4,128)(2,1)} %bitcast.3), calls=%async_computation.1 | async-start | bytes 1048576 | tf_op jit(solution)/shard_map/all_to_all | solution.py:470
  78.7 0.0 copy-done.5
  78.8 0.0 copy-done.6
  78.8 0.1 maximum_bitcast_fusion
  78.8 7.8 %all-gather = f32[4,1,62]{2,1,0:T(1,128)S(1)} all-gather(f32[1,1,62]{2,1,0:T(1,128)S(1)} %maximum_bitcast_fusion), channel_id=1, replica_groups=mesh['view'=4,'space'=128] {'view'}, dimensions={0}, use_global_device_ids=true | all-gather | bytes 1240 | tf_op jit(solution)/shard_map/all_gather | solution.py:477
  86.6 0.1 fusion
  86.7 0.0 copy-done
  86.7 0.0 copy-done.3
  86.7 1.3 %prep.1 = (f32[8,256]{1,0:T(8,128)S(1)}, s32[8,512]{1,0:T(8,128)S(1)}, bf16[512,256]{1,0:T(8,128)(2,1)S(1)}) custom-call(f32[4,31]{1,0:T(4,128)S(1)} %get-tuple-element.27.px_ref, f32[4,31]{1,0:T(4,128)S(1)} %get-tuple-element.26.py_ref, s32[8,128]{1,0:T(8,128)S(1)} %copy-done.3, bf16[4,512,256]{2,1,0:T(8,128)(2,1)S(1)} %copy-done), custom_call_target="tpu_custom_call" | custom-call | flops 10000000 | bytes 1000000 | tf_op jit(solution)/shard_map/prep/pallas_call | solution.py:403
  88.0 0.0 copy-start.4
  88.0 0.0 copy-done.2
  88.0 1.8 %column.1 = bf16[512,8,128]{2,1,0:T(8,128)(2,1)} custom-call(f32[8,512]{1,0:T(8,128)S(1)} %copy-done.1, s32[128,128]{1,0:T(8,128)S(1)} %copy-done.2, bf16[128,48,128]{2,1,0:T(8,128)(2,1)S(1)} %all_to_all.15.in_ref), custom_call_target="tpu_custom_call" | custom-call | flops 540000000 | bytes 3000000 | tf_op jit(solution)/shard_map/column/pallas_call | solution.py:433
  89.7 10.9 %all-to-all-done.1 = bf16[512,4,128]{2,1,0:T(4,128)(2,1)S(1)} async-done(((bf16[512,4,128]{2,1,0:T(4,128)(2,1)}), bf16[512,4,128]{2,1,0:T(4,128)(2,1)S(1)}, u32[]{:S(2)}, u32[]{:S(2)}) %all-to-all-start.1) | async-done | bytes 524320 | tf_op jit(solution)/shard_map/all_to_all | solution.py:470
  100.6 0.0 copy-done.4
  100.6 1.8 %back.1 = bf16[4,512,256]{2,1,0:T(8,128)(2,1)S(1)} custom-call(s32[8]{0:T(128)S(1)} %copy-done.4, s32[8,512]{1,0:T(8,128)S(1)} %get-tuple-element.18.units_ref, f32[8,256]{1,0:T(8,128)S(1)} %get-tuple-element.19.rows_ref, bf16[4,512,128]{2,1,0:T(8,128)(2,1)S(1)} %bitcast.7, bf16[512,256]{1,0:T(8,128)(2,1)S(1)} %get-tuple-element.24.est_ref), custom_call_target="tpu_custom_call" | custom-call | flops 1400000000 | bytes 5000000 | tf_op jit(solution)/shard_map/back/pallas_call | solution.py:447
  102.4 15.9 %all_to_all.16 = bf16[4,512,256]{2,1,0:T(8,128)(2,1)S(1)} all-to-all(bf16[4,512,256]{2,1,0:T(8,128)(2,1)S(1)} %back.1), channel_id=1, replica_groups=mesh['view'=4,'space'=128] {'view'}, dimensions={0} | all-to-all | bytes 2097152 | tf_op jit(solution)/shard_map/all_to_all | solution.py:481
  118.3 1.0 copy.11
  (3 shorter events, 0.0 us)
Async XLA Ops:
  5.9 59.5 %copy-start.1 = (f32[8,512]{1,0:T(8,128)S(1)}, f32[8,512]{1,0:T(8,128)}, u32[]{:S(2)}) copy-start(f32[8,512]{1,0:T(8,128)} %get-tuple-element.20.rows_ref) | copy-start | bytes 49156
  65.5 13.3 %copy-start.5 = (f32[1,31]{1,0:T(1,128)S(1)}, f32[1,31]{1,0:T(1,128)}, u32[]{:S(2)}) copy-start(f32[1,31]{1,0:T(1,128)} %py_hbm.1) | copy-start | bytes 376
  65.5 13.3 %copy-start.6 = (f32[1,31]{1,0:T(1,128)S(1)}, f32[1,31]{1,0:T(1,128)}, u32[]{:S(2)}) copy-start(f32[1,31]{1,0:T(1,128)} %px_hbm.1) | copy-start | bytes 376
  65.5 21.2 %copy-start = (bf16[4,512,256]{2,1,0:T(8,128)(2,1)S(1)}, bf16[4,512,256]{2,1,0:T(8,128)(2,1)}, u32[]{:S(2)}) copy-start(bf16[4,512,256]{2,1,0:T(8,128)(2,1)} %est_hbm.3) | copy-start | bytes 3145732
  65.5 21.2 %copy-start.3 = (s32[8,128]{1,0:T(8,128)S(1)}, s32[8,128]{1,0:T(8,128)}, u32[]{:S(2)}) copy-start(s32[8,128]{1,0:T(8,128)} %get-tuple-element.17.table_ref) | copy-start | bytes 12292
  67.3 20.6 %copy-start.2 = (s32[128,128]{1,0:T(8,128)S(1)}, s32[128,128]{1,0:T(8,128)}, u32[]{:S(2)}) copy-start(s32[128,128]{1,0:T(8,128)} %get-tuple-element.22.count_ref) | copy-start | bytes 196612
  67.4 33.3 %all-to-all-start.1 = ((bf16[512,4,128]{2,1,0:T(4,128)(2,1)}), bf16[512,4,128]{2,1,0:T(4,128)(2,1)S(1)}, u32[]{:S(2)}, u32[]{:S(2)}) async-start(bf16[512,4,128]{2,1,0:T(4,128)(2,1)} %bitcast.3), calls=%async_computation.1 | async-start | bytes 1048576 | tf_op jit(solution)/shard_map/all_to_all | solution.py:470
  88.0 12.6 %copy-start.4 = (s32[8]{0:T(128)S(1)}, s32[8]{0:T(128)}, u32[]{:S(2)}) copy-start(s32[8]{0:T(128)} %mask_hbm.3) | copy-start | bytes 100

commit v9 on v7

--- a/solution.py
+++ b/solution.py
@@ -22,7 +22,6 @@
 SMEM = pl.BlockSpec(memory_space=pltpu.SMEM)
 VMEM = pl.BlockSpec(memory_space=pltpu.VMEM)
 ANY = pl.BlockSpec(memory_space=pl.ANY)
-HBM = pl.BlockSpec(memory_space=pltpu.HBM)
 
 
 def shape(*dims, dtype=BF16):
@@ -213,7 +212,7 @@
         copy.wait()
 
 
-def prep_kernel(pz_ref, px_ref, py_ref, table_ref, forward_ref, adjoint_ref, rows_ref, units_ref):
+def bands_kernel(pz_ref, forward_ref, adjoint_ref):
     group = SLAB * HALF
     edge = ZB // 2
     half_z = TAPS_Z // 2
@@ -229,6 +228,11 @@
     part = ZB // SLAB
     source = r % part // HALF * group + r // part * HALF + r % HALF
     adjoint_ref[...] = dot(one_hot(iota((ZB, ZB), 1) == source), adjoint).astype(BF16)
+
+
+def prep_kernel(px_ref, py_ref, table_ref, est_hbm, rows_ref, units_ref, plane_ref, sem):
+    plane_copy = pltpu.make_async_copy(est_hbm.at[lax.axis_index("view")], plane_ref, sem)
+    plane_copy.start()
     half_xy = TAPS_XY // 2
     for view in range(VIEWS):
         rows_ref[view : view + 1, :] = placed_taps(
@@ -248,6 +252,7 @@
         unit = 2 * (tile // 2 * TILE + iota((TILE, slots), 0)) + tile % 2
         total += jnp.sum(jnp.where(place == iota((TILE, slots), 1), unit, 0), axis=0, keepdims=True)
     units_ref[...] = jnp.broadcast_to(total, (8, slots))
+    plane_copy.wait()
 
 
 def z_kernel(forward_ref, adjoint_ref, in_ref, back_hbm, ratio, back_ref, sems):
@@ -321,13 +326,10 @@
 
 
 def back_kernel(
-    mask_hbm, units_ref, rows_ref, in_ref, est_hbm, out_ref,
-    mask_ref, est_ref, back_z, padded, mask_sem, est_sem,
+    mask_hbm, units_ref, rows_ref, in_ref, est_ref, out_ref, mask_ref, back_z, padded, mask_sem,
 ):
     mask_copy = pltpu.make_async_copy(mask_hbm, mask_ref, mask_sem)
-    est_copy = pltpu.make_async_copy(est_hbm.at[lax.axis_index("view")], est_ref, est_sem)
     mask_copy.start()
-    est_copy.start()
     edge = XB // 2
     back_z[...] = jnp.ones((VIEWS, NX, NY), BF16)
     bands, matrix_y = [], []
@@ -352,7 +354,6 @@
             ]
     for view in range(VIEWS):
         padded[view, edge : edge + NX, :] = dot(back_z[view], matrix_y[view]).astype(BF16)
-    est_copy.wait()
     for block in range(NX // XB):
         here = pl.ds(block * XB, XB)
         summed = jnp.zeros((XB, NY), F32)
@@ -405,23 +406,32 @@
     )(tissue_mask, psf_x, psf_y, column_owner.reshape(1, UNITS), estimate, measured)
 
 
-def prep(psf_z, taps_x, taps_y, table):
+def bands(psf_z):
+    return call(
+        bands_kernel,
+        "bands",
+        (shape(ZB, 2 * ZB), shape(ZB, 2 * ZB)),
+        [SMEM],
+        (VMEM, VMEM),
+        [],
+        LIMIT,
+        flops=70_000_000,
+        moved=500_000,
+    )(psf_z)
+
+
+def prep(taps_x, taps_y, table, estimate):
     return call(
         prep_kernel,
         "prep",
-        (
-            shape(ZB, 2 * ZB),
-            shape(ZB, 2 * ZB),
-            shape(2 * VIEWS, NY, dtype=F32),
-            shape(8, HALF * DEVS, dtype=I32),
-        ),
-        [SMEM, SMEM, SMEM, VMEM],
-        (VMEM,) * 4,
-        [],
-        LIMIT,
-        flops=1_000_000_000,
-        moved=4_000_000,
-    )(psf_z, taps_x, taps_y, table)
+        (shape(2 * VIEWS, NY, dtype=F32), shape(8, HALF * DEVS, dtype=I32), shape(NX, NY)),
+        [SMEM, SMEM, VMEM, ANY],
+        (VMEM,) * 3,
+        [pltpu.SemaphoreType.DMA],
+        WIDE_LIMIT,
+        flops=10_000_000,
+        moved=1_000_000,
+    )(taps_x, taps_y, table, estimate)
 
 
 def z_pair(forward, adjoint, arrived):
@@ -458,32 +468,31 @@
     )(forward, count, arrived)
 
 
-def back(tissue_mask, units, rows, returned, estimate):
+def back(tissue_mask, units, rows, returned, plane):
     return call(
         back_kernel,
         "back",
         shape(VIEWS, NX, NY),
-        [ANY, VMEM, VMEM, VMEM, HBM],
+        [ANY, VMEM, VMEM, VMEM, VMEM],
         VMEM,
         [
             pltpu.SMEM((UNITS // TILE,), I32),
-            pltpu.VMEM((NX, NY), BF16),
             pltpu.VMEM((VIEWS, NX, NY), BF16),
             pltpu.VMEM((VIEWS, NX + XB, NY), BF16),
-            pltpu.SemaphoreType.DMA,
             pltpu.SemaphoreType.DMA,
         ],
         LIMIT,
         flops=1_400_000_000,
         moved=5_000_000,
-    )(tissue_mask, units, rows, returned, estimate)
+    )(tissue_mask, units, rows, returned, plane)
 
 
 def shards(estimate, measured, psf_x, psf_y, psf_z, tissue_mask, column_owner):
     message, table, count = pack(estimate, measured, psf_x, psf_y, tissue_mask, column_owner)
+    message, psf_z = lax.optimization_barrier((message, psf_z))
     arrived = lax.all_to_all(message, "space", split_axis=0, concat_axis=0, tiled=True)
-    taps = lax.all_gather(jnp.concatenate([psf_x, psf_y], axis=1), "view", axis=0, tiled=True)
-    forward, adjoint, rows, units = prep(psf_z, taps[:, :TAPS_XY], taps[:, TAPS_XY:], table)
+    forward, adjoint = bands(psf_z)
+    arrived, psf_x, psf_y = lax.optimization_barrier((arrived, psf_x, psf_y))
     sent = z_pair(forward, adjoint, arrived)
     returned = lax.all_to_all(
         sent.reshape(VIEWS * DEVS, HALF, TILE),
@@ -492,8 +501,10 @@
         concat_axis=0,
         tiled=True,
     ).reshape(VIEWS, HALF * DEVS, TILE)
+    taps = lax.all_gather(jnp.concatenate([psf_x, psf_y], axis=1), "view", axis=0, tiled=True)
+    rows, units, plane = prep(taps[:, :TAPS_XY], taps[:, TAPS_XY:], table, estimate)
     returned, column_blur = lax.optimization_barrier((returned, column(forward, count, arrived)))
-    updated = back(tissue_mask, units, rows, returned, estimate)
+    updated = back(tissue_mask, units, rows, returned, plane)
     updated = lax.all_to_all(updated, "view", split_axis=0, concat_axis=0, tiled=True)
     return updated, column_blur[None]
 

time: 121 us -> 121 us (level)
  waiting for transfers between devices: 51.3 us -> 48.9 us
  Pallas kernels: 12 us -> 14.2 us
    all_to_all x1, waiting for transfers between devices: 20.1 us -> 8.72 us  [shards(): lax.all_to_all(sent.reshape(VIEWS * DEVS, HALF, TILE), ('view', 'space'),...]
    all_to_all x1, waiting for transfers between devices: 31.2 us -> 40.1 us  [shards(): lax.all_to_all(message, 'space', split_axis=0, concat_axis=0, tiled=True)]
    pallas_call x2 -> x3, Pallas kernels: 3.33 us -> 5.59 us  [the longest x1 2.85 us: prep(): call(prep_kernel, 'prep', (shape(2 * VIEWS, NY, dtype=F32), shape(8, HALF...]
  transfers between devices with their start and end apart: 2 -> 2, of which waited for: 2 -> 2; matrix products, arithmetic and copies ran while one was open for 0% -> 1% of each run, Pallas kernels for 3% -> 5%
where the time goes in v9:
time: 121 us; the launch traced here: 119 us
  waiting for transfers between devices  48.9 us (40%)
  starting transfers between devices  29.8 us (25%)
  blocking collectives  23.7 us (20%)
  Pallas kernels  14.2 us (12%)
  local copies, waits for them, and re-layouts  1.66 us (1%)
    all_to_all x1, waiting for transfers between devices, shards(): lax.all_to_all(message, 'space', split_axis=0, concat_axis=0, tiled=True)  40.1 us
    all_to_all x1, starting transfers between devices, shards(): lax.all_to_all(message, 'space', split_axis=0, concat_axis=0, tiled=True)  18.4 us
    all_to_all x1, blocking collectives, shards(): lax.all_to_all(updated, 'view', split_axis=0, concat_axis=0, tiled=True)  15.9 us
    all_to_all x1, starting transfers between devices, shards(): lax.all_to_all(sent.reshape(VIEWS * DEVS, HALF, TILE), ('view', 'space'),...  11.4 us
    all_to_all x1, waiting for transfers between devices, shards(): lax.all_to_all(sent.reshape(VIEWS * DEVS, HALF, TILE), ('view', 'space'),...  8.72 us
    all_gather x1, blocking collectives, shards(): lax.all_gather(jnp.concatenate([psf_x, psf_y], axis=1), 'view', axis=0, t...  7.76 us
    pallas_call x1, Pallas kernels, pack(): call(pack_kernel, 'pack', (shape(DEVS, MSG, TILE), shape(UNITS // TILE, T...  5.26 us
    pallas_call x1, Pallas kernels, prep(): call(prep_kernel, 'prep', (shape(2 * VIEWS, NY, dtype=F32), shape(8, HALF...  2.85 us
  transfers between devices with their start and end apart: 2, of which 2 were waited for; matrix products, arithmetic and copies ran while one was open for 1% of the time, Pallas kernels for 5%

profile of v9, /device:TPU:1, one launch (start us, length us, event | category | flops | bytes accessed | tf_op | source)
XLA Modules:
  0.0 119.1 jit_solution(5648585555042120602)
XLA Ops:
  0.6 5.3 %pack.1 = (bf16[128,48,128]{2,1,0:T(8,128)(2,1)}, s32[8,128]{1,0:T(8,128)}, s32[128,128]{1,0:T(8,128)}) custom-call(s32[8]{0:T(128)} %mask_hbm.3, f32[1,31]{1,0:T(1,128)} %px_hbm.1, f32[1,31]{1,0:T(1,128)} %py_hbm.1, s32[1,1024]{1,0:T(1,128)} %bitcast.10, bf16[4,512,256]{2,1,0:T(8,128)(2,1)} %est_hbm.3, bf16[1,4,512,256]{3,2,1,0:T(8,128)(2,1)} %meas_hbm.1), custom_call_target="tpu_custom_call" | custom-call | flops 2000000000 | bytes 4000000 | tf_op jit(solution)/shard_map/pack/pallas_call | solution.py:381
  5.9 0.0 copy-start.4
  5.9 18.4 %all-to-all-start = ((bf16[128,48,128]{2,1,0:T(8,128)(2,1)}), bf16[128,48,128]{2,1,0:T(8,128)(2,1)S(1)}, u32[]{:S(2)}, u32[]{:S(2)}) async-start(bf16[128,48,128]{2,1,0:T(8,128)(2,1)} %get-tuple-element.18), calls=%async_computation | async-start | bytes 3145728 | tf_op jit(solution)/shard_map/all_to_all | solution.py:493
  24.4 0.0 copy-done.4
  24.4 0.9 bands.1
  25.3 40.1 %all-to-all-done.in_ref = bf16[128,48,128]{2,1,0:T(8,128)(2,1)S(1)} async-done(((bf16[128,48,128]{2,1,0:T(8,128)(2,1)}), bf16[128,48,128]{2,1,0:T(8,128)(2,1)S(1)}, u32[]{:S(2)}, u32[]{:S(2)}) %all-to-all-start) | async-done | bytes 1572896 | tf_op jit(solution)/shard_map/all_to_all | solution.py:493
  65.5 1.6 %zpair.1 = bf16[4,512,128]{2,1,0:T(8,128)(2,1)} custom-call(bf16[256,512]{1,0:T(8,128)(2,1)S(1)} %get-tuple-element.25.forward_ref, bf16[256,512]{1,0:T(8,128)(2,1)S(1)} %get-tuple-element.26.adjoint_ref, bf16[128,48,128]{2,1,0:T(8,128)(2,1)S(1)} %all-to-all-done.in_ref), custom_call_target="tpu_custom_call" | custom-call | flops 540000000 | bytes 3000000 | tf_op jit(solution)/shard_map/zpair/pallas_call | solution.py:439
  67.1 0.0 copy-start
  67.1 11.4 %all-to-all-start.1 = ((bf16[512,4,128]{2,1,0:T(4,128)(2,1)}), bf16[512,4,128]{2,1,0:T(4,128)(2,1)S(1)}, u32[]{:S(2)}, u32[]{:S(2)}) async-start(bf16[512,4,128]{2,1,0:T(4,128)(2,1)} %bitcast.3), calls=%async_computation.1 | async-start | bytes 1048576 | tf_op jit(solution)/shard_map/all_to_all | solution.py:497
  78.5 0.0 copy-done.6
  78.5 0.0 copy-done.7
  78.5 0.1 maximum_bitcast_fusion
  78.6 7.8 %all-gather = f32[4,1,62]{2,1,0:T(1,128)S(1)} all-gather(f32[1,1,62]{2,1,0:T(1,128)S(1)} %maximum_bitcast_fusion), channel_id=1, replica_groups=mesh['view'=4,'space'=128] {'view'}, dimensions={0}, use_global_device_ids=true | all-gather | bytes 1240 | tf_op jit(solution)/shard_map/all_gather | solution.py:504
  86.4 0.7 fusion
  87.0 2.8 %prep.1 = (f32[8,256]{1,0:T(8,128)}, s32[8,512]{1,0:T(8,128)}, bf16[512,256]{1,0:T(8,128)(2,1)}) custom-call(f32[4,31]{1,0:T(4,128)} %get-tuple-element.33.px_ref, f32[4,31]{1,0:T(4,128)} %get-tuple-element.32.py_ref, s32[8,128]{1,0:T(8,128)} %get-tuple-element.21.table_ref, bf16[4,512,256]{2,1,0:T(8,128)(2,1)} %est_hbm.3), custom_call_target="tpu_custom_call" | custom-call | flops 10000000 | bytes 1000000 | tf_op jit(solution)/shard_map/prep/pallas_call | solution.py:424
  89.9 0.0 copy-start.5
  89.9 0.0 copy-done
  89.9 1.7 %column.1 = bf16[512,8,128]{2,1,0:T(8,128)(2,1)} custom-call(bf16[256,512]{1,0:T(8,128)(2,1)S(1)} %get-tuple-element.25.forward_ref, s32[128,128]{1,0:T(8,128)S(1)} %copy-done, bf16[128,48,128]{2,1,0:T(8,128)(2,1)S(1)} %all-to-all-done.in_ref), custom_call_target="tpu_custom_call" | custom-call | flops 540000000 | bytes 3000000 | tf_op jit(solution)/shard_map/column/pallas_call | solution.py:458
  91.6 8.7 %all-to-all-done.1 = bf16[512,4,128]{2,1,0:T(4,128)(2,1)S(1)} async-done(((bf16[512,4,128]{2,1,0:T(4,128)(2,1)}), bf16[512,4,128]{2,1,0:T(4,128)(2,1)S(1)}, u32[]{:S(2)}, u32[]{:S(2)}) %all-to-all-start.1) | async-done | bytes 524320 | tf_op jit(solution)/shard_map/all_to_all | solution.py:497
  100.4 0.0 copy-done.1
  100.4 0.0 copy-done.3
  100.4 1.8 %back.1 = bf16[4,512,256]{2,1,0:T(8,128)(2,1)S(1)} custom-call(s32[8]{0:T(128)S(1)} %copy-done.5, s32[8,512]{1,0:T(8,128)S(1)} %copy-done.2, f32[8,256]{1,0:T(8,128)S(1)} %copy-done.3, bf16[4,512,128]{2,1,0:T(8,128)(2,1)S(1)} %bitcast.7, bf16[512,256]{1,0:T(8,128)(2,1)S(1)} %copy-done.1), custom_call_target="tpu_custom_call" | custom-call | flops 1400000000 | bytes 5000000 | tf_op jit(solution)/shard_map/back/pallas_call | solution.py:472
  102.2 15.9 %all_to_all.15 = bf16[4,512,256]{2,1,0:T(8,128)(2,1)S(1)} all-to-all(bf16[4,512,256]{2,1,0:T(8,128)(2,1)S(1)} %back.1), channel_id=1, replica_groups=mesh['view'=4,'space'=128] {'view'}, dimensions={0} | all-to-all | bytes 2097152 | tf_op jit(solution)/shard_map/all_to_all | solution.py:508
  118.1 1.0 copy.11
  (7 shorter events, 0.0 us)
Async XLA Ops:
  5.9 18.4 %copy-start.4 = (f32[1,63]{1,0:T(1,128)S(1)}, f32[1,63]{1,0:T(1,128)}, u32[]{:S(2)}) copy-start(f32[1,63]{1,0:T(1,128)} %pz_ref) | copy-start | bytes 760
  5.9 59.5 %all-to-all-start = ((bf16[128,48,128]{2,1,0:T(8,128)(2,1)}), bf16[128,48,128]{2,1,0:T(8,128)(2,1)S(1)}, u32[]{:S(2)}, u32[]{:S(2)}) async-start(bf16[128,48,128]{2,1,0:T(8,128)(2,1)} %get-tuple-element.18), calls=%async_computation | async-start | bytes 3145728 | tf_op jit(solution)/shard_map/all_to_all | solution.py:493
  65.4 13.1 %copy-start.6 = (f32[1,31]{1,0:T(1,128)S(1)}, f32[1,31]{1,0:T(1,128)}, u32[]{:S(2)}) copy-start(f32[1,31]{1,0:T(1,128)} %py_hbm.1) | copy-start | bytes 376
  65.4 13.1 %copy-start.7 = (f32[1,31]{1,0:T(1,128)S(1)}, f32[1,31]{1,0:T(1,128)}, u32[]{:S(2)}) copy-start(f32[1,31]{1,0:T(1,128)} %px_hbm.1) | copy-start | bytes 376
  67.1 22.8 %copy-start = (s32[128,128]{1,0:T(8,128)S(1)}, s32[128,128]{1,0:T(8,128)}, u32[]{:S(2)}) copy-start(s32[128,128]{1,0:T(8,128)} %get-tuple-element.28.count_ref) | copy-start | bytes 196612
  67.1 33.3 %all-to-all-start.1 = ((bf16[512,4,128]{2,1,0:T(4,128)(2,1)}), bf16[512,4,128]{2,1,0:T(4,128)(2,1)S(1)}, u32[]{:S(2)}, u32[]{:S(2)}) async-start(bf16[512,4,128]{2,1,0:T(4,128)(2,1)} %bitcast.3), calls=%async_computation.1 | async-start | bytes 1048576 | tf_op jit(solution)/shard_map/all_to_all | solution.py:497
  89.9 10.5 %copy-start.1 = (bf16[512,256]{1,0:T(8,128)(2,1)S(1)}, bf16[512,256]{1,0:T(8,128)(2,1)}, u32[]{:S(2)}) copy-start(bf16[512,256]{1,0:T(8,128)(2,1)} %get-tuple-element.30.est_ref) | copy-start | bytes 786436
  89.9 10.5 %copy-start.2 = (s32[8,512]{1,0:T(8,128)S(1)}, s32[8,512]{1,0:T(8,128)}, u32[]{:S(2)}) copy-start(s32[8,512]{1,0:T(8,128)} %get-tuple-element.22.units_ref) | copy-start | bytes 49156
  89.9 10.5 %copy-start.3 = (f32[8,256]{1,0:T(8,128)S(1)}, f32[8,256]{1,0:T(8,128)}, u32[]{:S(2)}) copy-start(f32[8,256]{1,0:T(8,128)} %get-tuple-element.23.rows_ref) | copy-start | bytes 24580
  89.9 10.5 %copy-start.5 = (s32[8]{0:T(128)S(1)}, s32[8]{0:T(128)}, u32[]{:S(2)}) copy-start(s32[8]{0:T(128)} %mask_hbm.3) | copy-start | bytes 100

commit v10 on v9

--- a/solution.py
+++ b/solution.py
@@ -151,12 +151,22 @@
     for copy in reads[2:4]:
         copy.wait()
     half_xy = TAPS_XY // 2
-    matrix_x = band(placed_taps(lambda m: px_ref[0, m], TAPS_XY, NX, lambda m: m - half_xy), NX, half_xy)
+    starts = [min(max(i * XB - XB // 2, 0), NX - 2 * XB) for i in range(NX // XB)]
+    bands_x = {}
+    for i, start in enumerate(starts):
+        lead = i * XB - start
+        if lead not in bands_x:
+            row = placed_taps(lambda m: px_ref[0, m], TAPS_XY, 2 * XB, lambda m: lead + m - half_xy)
+            distance = iota((XB, 2 * XB), 1) - iota((XB, 2 * XB), 0) - lead
+            bands_x[lead] = jnp.where(jnp.abs(distance) <= half_xy, rolled(row, XB), 0.0).astype(BF16)
     matrix_y[...] = band(placed_taps(lambda m: py_ref[0, m], TAPS_XY, NY, lambda m: half_xy - m), NY, half_xy)
 
     est_copy.wait()
     for plane in range(SLAB):
-        along[plane] = dot(matrix_x, est_ref[plane]).astype(BF16)
+        for i, start in enumerate(starts):
+            along[plane, i * XB : (i + 1) * XB, :] = dot(
+                bands_x[i * XB - start], est_ref[plane, start : start + 2 * XB, :]
+            ).astype(BF16)
     chosen = tissue_tiles(mask_ref)
     row_of = [pl.multiple_of(tile // 2 * TILE, TILE) for tile in chosen]
     lane_of = [pl.multiple_of(tile % 2 * TILE, TILE) for tile in chosen]

time: 121 us -> 120 us (level)
  no operation moved by 1% of the time
where the time goes in v10:
time: 120 us; the launch traced here: 119 us
  waiting for transfers between devices  48.9 us (41%)
  starting transfers between devices  29.8 us (25%)
  blocking collectives  23.7 us (20%)
  Pallas kernels  14 us (12%)
  local copies, waits for them, and re-layouts  1.66 us (1%)
    all_to_all x1, waiting for transfers between devices, shards(): lax.all_to_all(message, 'space', split_axis=0, concat_axis=0, tiled=True)  40.1 us
    all_to_all x1, starting transfers between devices, shards(): lax.all_to_all(message, 'space', split_axis=0, concat_axis=0, tiled=True)  18.4 us
    all_to_all x1, blocking collectives, shards(): lax.all_to_all(updated, 'view', split_axis=0, concat_axis=0, tiled=True)  15.9 us
    all_to_all x1, starting transfers between devices, shards(): lax.all_to_all(sent.reshape(VIEWS * DEVS, HALF, TILE), ('view', 'space'),...  11.4 us
    all_to_all x1, waiting for transfers between devices, shards(): lax.all_to_all(sent.reshape(VIEWS * DEVS, HALF, TILE), ('view', 'space'),...  8.72 us
    all_gather x1, blocking collectives, shards(): lax.all_gather(jnp.concatenate([psf_x, psf_y], axis=1), 'view', axis=0, t...  7.76 us
    pallas_call x1, Pallas kernels, pack(): call(pack_kernel, 'pack', (shape(DEVS, MSG, TILE), shape(UNITS // TILE, T...  5.06 us
    pallas_call x1, Pallas kernels, prep(): call(prep_kernel, 'prep', (shape(2 * VIEWS, NY, dtype=F32), shape(8, HALF...  2.85 us
  transfers between devices with their start and end apart: 2, of which 2 were waited for; matrix products, arithmetic and copies ran while one was open for 1% of the time, Pallas kernels for 5%

profile of v10, /device:TPU:1, one launch (start us, length us, event | category | flops | bytes accessed | tf_op | source)
XLA Modules:
  0.0 118.9 jit_solution(16104173171551912209)
XLA Ops:
  0.6 5.1 %pack.1 = (bf16[128,48,128]{2,1,0:T(8,128)(2,1)}, s32[8,128]{1,0:T(8,128)}, s32[128,128]{1,0:T(8,128)}) custom-call(s32[8]{0:T(128)} %mask_hbm.3, f32[1,31]{1,0:T(1,128)} %px_hbm.1, f32[1,31]{1,0:T(1,128)} %py_hbm.1, s32[1,1024]{1,0:T(1,128)} %bitcast.10, bf16[4,512,256]{2,1,0:T(8,128)(2,1)} %est_hbm.3, bf16[1,4,512,256]{3,2,1,0:T(8,128)(2,1)} %meas_hbm.1), custom_call_target="tpu_custom_call" | custom-call | flops 2000000000 | bytes 4000000 | tf_op jit(solution)/shard_map/pack/pallas_call | solution.py:391
  5.7 0.0 copy-start.4
  5.7 18.4 %all-to-all-start = ((bf16[128,48,128]{2,1,0:T(8,128)(2,1)}), bf16[128,48,128]{2,1,0:T(8,128)(2,1)S(1)}, u32[]{:S(2)}, u32[]{:S(2)}) async-start(bf16[128,48,128]{2,1,0:T(8,128)(2,1)} %get-tuple-element.18), calls=%async_computation | async-start | bytes 3145728 | tf_op jit(solution)/shard_map/all_to_all | solution.py:503
  24.1 0.0 copy-done.4
  24.2 0.9 bands.1
  25.1 40.1 %all-to-all-done.in_ref = bf16[128,48,128]{2,1,0:T(8,128)(2,1)S(1)} async-done(((bf16[128,48,128]{2,1,0:T(8,128)(2,1)}), bf16[128,48,128]{2,1,0:T(8,128)(2,1)S(1)}, u32[]{:S(2)}, u32[]{:S(2)}) %all-to-all-start) | async-done | bytes 1572896 | tf_op jit(solution)/shard_map/all_to_all | solution.py:503
  65.2 1.6 %zpair.1 = bf16[4,512,128]{2,1,0:T(8,128)(2,1)} custom-call(bf16[256,512]{1,0:T(8,128)(2,1)S(1)} %get-tuple-element.25.forward_ref, bf16[256,512]{1,0:T(8,128)(2,1)S(1)} %get-tuple-element.26.adjoint_ref, bf16[128,48,128]{2,1,0:T(8,128)(2,1)S(1)} %all-to-all-done.in_ref), custom_call_target="tpu_custom_call" | custom-call | flops 540000000 | bytes 3000000 | tf_op jit(solution)/shard_map/zpair/pallas_call | solution.py:449
  66.9 0.0 copy-start
  66.9 11.4 %all-to-all-start.1 = ((bf16[512,4,128]{2,1,0:T(4,128)(2,1)}), bf16[512,4,128]{2,1,0:T(4,128)(2,1)S(1)}, u32[]{:S(2)}, u32[]{:S(2)}) async-start(bf16[512,4,128]{2,1,0:T(4,128)(2,1)} %bitcast.3), calls=%async_computation.1 | async-start | bytes 1048576 | tf_op jit(solution)/shard_map/all_to_all | solution.py:507
  78.3 0.0 copy-done.6
  78.3 0.0 copy-done.7
  78.3 0.1 maximum_bitcast_fusion
  78.4 7.8 %all-gather = f32[4,1,62]{2,1,0:T(1,128)S(1)} all-gather(f32[1,1,62]{2,1,0:T(1,128)S(1)} %maximum_bitcast_fusion), channel_id=1, replica_groups=mesh['view'=4,'space'=128] {'view'}, dimensions={0}, use_global_device_ids=true | all-gather | bytes 1240 | tf_op jit(solution)/shard_map/all_gather | solution.py:514
  86.2 0.7 fusion
  86.8 2.8 %prep.1 = (f32[8,256]{1,0:T(8,128)}, s32[8,512]{1,0:T(8,128)}, bf16[512,256]{1,0:T(8,128)(2,1)}) custom-call(f32[4,31]{1,0:T(4,128)} %get-tuple-element.33.px_ref, f32[4,31]{1,0:T(4,128)} %get-tuple-element.32.py_ref, s32[8,128]{1,0:T(8,128)} %get-tuple-element.21.table_ref, bf16[4,512,256]{2,1,0:T(8,128)(2,1)} %est_hbm.3), custom_call_target="tpu_custom_call" | custom-call | flops 10000000 | bytes 1000000 | tf_op jit(solution)/shard_map/prep/pallas_call | solution.py:434
  89.7 0.0 copy-start.1
  89.7 0.0 copy-start.2
  89.7 0.0 copy-start.5
  89.7 1.7 %column.1 = bf16[512,8,128]{2,1,0:T(8,128)(2,1)} custom-call(bf16[256,512]{1,0:T(8,128)(2,1)S(1)} %get-tuple-element.25.forward_ref, s32[128,128]{1,0:T(8,128)S(1)} %copy-done, bf16[128,48,128]{2,1,0:T(8,128)(2,1)S(1)} %all-to-all-done.in_ref), custom_call_target="tpu_custom_call" | custom-call | flops 540000000 | bytes 3000000 | tf_op jit(solution)/shard_map/column/pallas_call | solution.py:468
  91.4 8.7 %all-to-all-done.1 = bf16[512,4,128]{2,1,0:T(4,128)(2,1)S(1)} async-done(((bf16[512,4,128]{2,1,0:T(4,128)(2,1)}), bf16[512,4,128]{2,1,0:T(4,128)(2,1)S(1)}, u32[]{:S(2)}, u32[]{:S(2)}) %all-to-all-start.1) | async-done | bytes 524320 | tf_op jit(solution)/shard_map/all_to_all | solution.py:507
  100.2 0.0 copy-done.2
  100.2 1.8 %back.1 = bf16[4,512,256]{2,1,0:T(8,128)(2,1)S(1)} custom-call(s32[8]{0:T(128)S(1)} %copy-done.5, s32[8,512]{1,0:T(8,128)S(1)} %copy-done.2, f32[8,256]{1,0:T(8,128)S(1)} %copy-done.3, bf16[4,512,128]{2,1,0:T(8,128)(2,1)S(1)} %bitcast.7, bf16[512,256]{1,0:T(8,128)(2,1)S(1)} %copy-done.1), custom_call_target="tpu_custom_call" | custom-call | flops 1400000000 | bytes 5000000 | tf_op jit(solution)/shard_map/back/pallas_call | solution.py:482
  102.0 15.9 %all_to_all.15 = bf16[4,512,256]{2,1,0:T(8,128)(2,1)S(1)} all-to-all(bf16[4,512,256]{2,1,0:T(8,128)(2,1)S(1)} %back.1), channel_id=1, replica_groups=mesh['view'=4,'space'=128] {'view'}, dimensions={0} | all-to-all | bytes 2097152 | tf_op jit(solution)/shard_map/all_to_all | solution.py:518
  117.9 1.0 copy.11
  (7 shorter events, 0.0 us)
Async XLA Ops:
  5.7 18.5 %copy-start.4 = (f32[1,63]{1,0:T(1,128)S(1)}, f32[1,63]{1,0:T(1,128)}, u32[]{:S(2)}) copy-start(f32[1,63]{1,0:T(1,128)} %pz_ref) | copy-start | bytes 760
  5.7 59.5 %all-to-all-start = ((bf16[128,48,128]{2,1,0:T(8,128)(2,1)}), bf16[128,48,128]{2,1,0:T(8,128)(2,1)S(1)}, u32[]{:S(2)}, u32[]{:S(2)}) async-start(bf16[128,48,128]{2,1,0:T(8,128)(2,1)} %get-tuple-element.18), calls=%async_computation | async-start | bytes 3145728 | tf_op jit(solution)/shard_map/all_to_all | solution.py:503
  65.2 13.1 %copy-start.6 = (f32[1,31]{1,0:T(1,128)S(1)}, f32[1,31]{1,0:T(1,128)}, u32[]{:S(2)}) copy-start(f32[1,31]{1,0:T(1,128)} %py_hbm.1) | copy-start | bytes 376
  65.2 13.1 %copy-start.7 = (f32[1,31]{1,0:T(1,128)S(1)}, f32[1,31]{1,0:T(1,128)}, u32[]{:S(2)}) copy-start(f32[1,31]{1,0:T(1,128)} %px_hbm.1) | copy-start | bytes 376
  66.9 22.8 %copy-start = (s32[128,128]{1,0:T(8,128)S(1)}, s32[128,128]{1,0:T(8,128)}, u32[]{:S(2)}) copy-start(s32[128,128]{1,0:T(8,128)} %get-tuple-element.28.count_ref) | copy-start | bytes 196612
  66.9 33.3 %all-to-all-start.1 = ((bf16[512,4,128]{2,1,0:T(4,128)(2,1)}), bf16[512,4,128]{2,1,0:T(4,128)(2,1)S(1)}, u32[]{:S(2)}, u32[]{:S(2)}) async-start(bf16[512,4,128]{2,1,0:T(4,128)(2,1)} %bitcast.3), calls=%async_computation.1 | async-start | bytes 1048576 | tf_op jit(solution)/shard_map/all_to_all | solution.py:507
  89.7 10.5 %copy-start.1 = (bf16[512,256]{1,0:T(8,128)(2,1)S(1)}, bf16[512,256]{1,0:T(8,128)(2,1)}, u32[]{:S(2)}) copy-start(bf16[512,256]{1,0:T(8,128)(2,1)} %get-tuple-element.30.est_ref) | copy-start | bytes 786436
  89.7 10.5 %copy-start.2 = (s32[8,512]{1,0:T(8,128)S(1)}, s32[8,512]{1,0:T(8,128)}, u32[]{:S(2)}) copy-start(s32[8,512]{1,0:T(8,128)} %get-tuple-element.22.units_ref) | copy-start | bytes 49156
  89.7 10.5 %copy-start.3 = (f32[8,256]{1,0:T(8,128)S(1)}, f32[8,256]{1,0:T(8,128)}, u32[]{:S(2)}) copy-start(f32[8,256]{1,0:T(8,128)} %get-tuple-element.23.rows_ref) | copy-start | bytes 24580
  89.7 10.5 %copy-start.5 = (s32[8]{0:T(128)S(1)}, s32[8]{0:T(128)}, u32[]{:S(2)}) copy-start(s32[8]{0:T(128)} %mask_hbm.3) | copy-start | bytes 100

commit v11 on v10

--- a/solution.py
+++ b/solution.py
@@ -208,7 +208,8 @@
             jnp.concatenate([tile[plane * TILE : (plane + 1) * TILE] for plane in range(SLAB)], axis=1)
         )
     blurred = jnp.concatenate(blurred, axis=0)
-    parts = [dot(pick, blurred).astype(BF16), dot(pick_more, blurred).astype(BF16), seen]
+    both = dot(jnp.concatenate([pick, pick_more], axis=0), blurred).astype(BF16)
+    parts = [both[:slots], both[slots:], seen]
     for i in range(DEVS // block):
         turned = dot(turn, jnp.concatenate([rows_of(part, i) for part in parts], axis=1)).astype(BF16)
         for k in range(len(parts)):
@@ -370,8 +371,7 @@
         for view in range(VIEWS):
             summed += dot(bands[view], padded[view, block * XB : block * XB + 2 * XB, :])
         updated = (est_ref[here, :].astype(F32) * summed / VIEWS).astype(BF16)
-        for view in range(VIEWS):
-            out_ref[view, here, :] = updated
+        out_ref[0, here, :] = updated
 
 
 def call(kernel, name, out_shape, in_specs, out_specs, scratch, limit, flops, moved):
@@ -482,7 +482,7 @@
     return call(
         back_kernel,
         "back",
-        shape(VIEWS, NX, NY),
+        shape(1, NX, NY),
         [ANY, VMEM, VMEM, VMEM, VMEM],
         VMEM,
         [
@@ -515,8 +515,14 @@
     rows, units, plane = prep(taps[:, :TAPS_XY], taps[:, TAPS_XY:], table, estimate)
     returned, column_blur = lax.optimization_barrier((returned, column(forward, count, arrived)))
     updated = back(tissue_mask, units, rows, returned, plane)
-    updated = lax.all_to_all(updated, "view", split_axis=0, concat_axis=0, tiled=True)
-    return updated, column_blur[None]
+    view = lax.axis_index("view")
+    gathered = jnp.zeros((VIEWS, NX, NY), BF16)
+    for step in (0, 2, 1, 3):
+        plane = updated
+        if step:
+            plane = lax.ppermute(updated, "view", [(i, (i + step) % VIEWS) for i in range(VIEWS)])
+        gathered = lax.dynamic_update_slice(gathered, plane, ((view - step) % VIEWS, 0, 0))
+    return gathered, column_blur[None]
 
 
 def solution(mesh):

time: 120 us -> 121 us (level)
  blocking collectives: 23.7 us -> 7.76 us
  starting transfers between devices: 29.8 us -> 38.8 us
  waiting for transfers between devices: 48.9 us -> 56.9 us
    all_to_all x1 -> x0, blocking collectives: 15.9 us -> none  [shards(): lax.all_to_all(updated, 'view', split_axis=0, concat_axis=0, tiled=True)]
    ppermute x0 -> x3, starting transfers between devices: none -> 8.99 us  [shards(): lax.ppermute(updated, 'view', [(i, (i + step) % VIEWS) for i in range(VIE...]
    ppermute x0 -> x3, waiting for transfers between devices: none -> 8.02 us  [shards(): lax.ppermute(updated, 'view', [(i, (i + step) % VIEWS) for i in range(VIE...]
  transfers between devices with their start and end apart: 2 -> 5, of which waited for: 2 -> 4; matrix products, arithmetic and copies ran while one was open for 1% -> 1% of each run, Pallas kernels for 5% -> 5%
where the time goes in v11:
time: 121 us; the launch traced here: 120 us
  waiting for transfers between devices  56.9 us (47%)
  starting transfers between devices  38.8 us (32%)
  Pallas kernels  14 us (12%)
  blocking collectives  7.76 us (6%)
  local copies, waits for them, and re-layouts  1.82 us (2%)
    all_to_all x1, waiting for transfers between devices, shards(): lax.all_to_all(message, 'space', split_axis=0, concat_axis=0, tiled=True)  40.1 us
    all_to_all x1, starting transfers between devices, shards(): lax.all_to_all(message, 'space', split_axis=0, concat_axis=0, tiled=True)  18.4 us
    all_to_all x1, starting transfers between devices, shards(): lax.all_to_all(sent.reshape(VIEWS * DEVS, HALF, TILE), ('view', 'space'),...  11.4 us
    ppermute x3, starting transfers between devices, shards(): lax.ppermute(updated, 'view', [(i, (i + step) % VIEWS) for i in range(VIE...  8.99 us
    all_to_all x1, waiting for transfers between devices, shards(): lax.all_to_all(sent.reshape(VIEWS * DEVS, HALF, TILE), ('view', 'space'),...  8.74 us
    ppermute x3, waiting for transfers between devices, shards(): lax.ppermute(updated, 'view', [(i, (i + step) % VIEWS) for i in range(VIE...  8.02 us
    all_gather x1, blocking collectives, shards(): lax.all_gather(jnp.concatenate([psf_x, psf_y], axis=1), 'view', axis=0, t...  7.76 us
    pallas_call x1, Pallas kernels, pack(): call(pack_kernel, 'pack', (shape(DEVS, MSG, TILE), shape(UNITS // TILE, T...  5.04 us
  transfers between devices with their start and end apart: 5, of which 4 were waited for; matrix products, arithmetic and copies ran while one was open for 1% of the time, Pallas kernels for 5%

profile of v11, /device:TPU:1, one launch (start us, length us, event | category | flops | bytes accessed | tf_op | source)
XLA Modules:
  0.0 120.3 jit_solution(385701153304200101)
XLA Ops:
  0.6 5.0 %pack.1 = (bf16[128,48,128]{2,1,0:T(8,128)(2,1)}, s32[8,128]{1,0:T(8,128)}, s32[128,128]{1,0:T(8,128)}) custom-call(s32[8]{0:T(128)} %mask_hbm.3, f32[1,31]{1,0:T(1,128)} %px_hbm.1, f32[1,31]{1,0:T(1,128)} %py_hbm.1, s32[1,1024]{1,0:T(1,128)} %bitcast.10, bf16[4,512,256]{2,1,0:T(8,128)(2,1)} %est_hbm.3, bf16[1,4,512,256]{3,2,1,0:T(8,128)(2,1)} %meas_hbm.1), custom_call_target="tpu_custom_call" | custom-call | flops 2000000000 | bytes 4000000 | tf_op jit(solution)/shard_map/pack/pallas_call | solution.py:391
  5.7 0.0 copy-start.4
  5.7 18.4 %all-to-all-start = ((bf16[128,48,128]{2,1,0:T(8,128)(2,1)}), bf16[128,48,128]{2,1,0:T(8,128)(2,1)S(1)}, u32[]{:S(2)}, u32[]{:S(2)}) async-start(bf16[128,48,128]{2,1,0:T(8,128)(2,1)} %get-tuple-element.18), calls=%async_computation | async-start | bytes 3145728 | tf_op jit(solution)/shard_map/all_to_all | solution.py:503
  24.1 0.9 bands.1
  25.1 40.1 %all-to-all-done.in_ref = bf16[128,48,128]{2,1,0:T(8,128)(2,1)S(1)} async-done(((bf16[128,48,128]{2,1,0:T(8,128)(2,1)}), bf16[128,48,128]{2,1,0:T(8,128)(2,1)S(1)}, u32[]{:S(2)}, u32[]{:S(2)}) %all-to-all-start) | async-done | bytes 1572896 | tf_op jit(solution)/shard_map/all_to_all | solution.py:503
  65.2 1.6 %zpair.1 = bf16[4,512,128]{2,1,0:T(8,128)(2,1)} custom-call(bf16[256,512]{1,0:T(8,128)(2,1)S(1)} %get-tuple-element.25.forward_ref, bf16[256,512]{1,0:T(8,128)(2,1)S(1)} %get-tuple-element.26.adjoint_ref, bf16[128,48,128]{2,1,0:T(8,128)(2,1)S(1)} %all-to-all-done.in_ref), custom_call_target="tpu_custom_call" | custom-call | flops 540000000 | bytes 3000000 | tf_op jit(solution)/shard_map/zpair/pallas_call | solution.py:449
  66.9 0.0 copy-start
  66.9 11.4 %all-to-all-start.1 = ((bf16[512,4,128]{2,1,0:T(4,128)(2,1)}), bf16[512,4,128]{2,1,0:T(4,128)(2,1)S(1)}, u32[]{:S(2)}, u32[]{:S(2)}) async-start(bf16[512,4,128]{2,1,0:T(4,128)(2,1)} %bitcast.3), calls=%async_computation.1 | async-start | bytes 1048576 | tf_op jit(solution)/shard_map/all_to_all | solution.py:507
  78.3 0.1 maximum_bitcast_fusion
  78.4 7.8 %all-gather = f32[4,1,62]{2,1,0:T(1,128)S(1)} all-gather(f32[1,1,62]{2,1,0:T(1,128)S(1)} %maximum_bitcast_fusion), channel_id=1, replica_groups=mesh['view'=4,'space'=128] {'view'}, dimensions={0}, use_global_device_ids=true | all-gather | bytes 1240 | tf_op jit(solution)/shard_map/all_gather | solution.py:514
  86.1 0.7 fusion
  86.8 2.8 %prep.1 = (f32[8,256]{1,0:T(8,128)}, s32[8,512]{1,0:T(8,128)}, bf16[512,256]{1,0:T(8,128)(2,1)}) custom-call(f32[4,31]{1,0:T(4,128)} %get-tuple-element.33.px_ref, f32[4,31]{1,0:T(4,128)} %get-tuple-element.32.py_ref, s32[8,128]{1,0:T(8,128)} %get-tuple-element.21.table_ref, bf16[4,512,256]{2,1,0:T(8,128)(2,1)} %est_hbm.3), custom_call_target="tpu_custom_call" | custom-call | flops 10000000 | bytes 1000000 | tf_op jit(solution)/shard_map/prep/pallas_call | solution.py:434
  89.7 0.0 copy-start.5
  89.7 1.7 %column.1 = bf16[512,8,128]{2,1,0:T(8,128)(2,1)} custom-call(bf16[256,512]{1,0:T(8,128)(2,1)S(1)} %get-tuple-element.25.forward_ref, s32[128,128]{1,0:T(8,128)S(1)} %copy-done, bf16[128,48,128]{2,1,0:T(8,128)(2,1)S(1)} %all-to-all-done.in_ref), custom_call_target="tpu_custom_call" | custom-call | flops 540000000 | bytes 3000000 | tf_op jit(solution)/shard_map/column/pallas_call | solution.py:468
  91.4 8.7 %all-to-all-done.1 = bf16[512,4,128]{2,1,0:T(4,128)(2,1)S(1)} async-done(((bf16[512,4,128]{2,1,0:T(4,128)(2,1)}), bf16[512,4,128]{2,1,0:T(4,128)(2,1)S(1)}, u32[]{:S(2)}, u32[]{:S(2)}) %all-to-all-start.1) | async-done | bytes 524320 | tf_op jit(solution)/shard_map/all_to_all | solution.py:507
  100.2 1.8 %back.1 = bf16[1,512,256]{2,1,0:T(8,128)(2,1)S(1)} custom-call(s32[8]{0:T(128)S(1)} %copy-done.5, s32[8,512]{1,0:T(8,128)S(1)} %copy-done.2, f32[8,256]{1,0:T(8,128)S(1)} %copy-done.3, bf16[4,512,128]{2,1,0:T(8,128)(2,1)S(1)} %bitcast.7, bf16[512,256]{1,0:T(8,128)(2,1)S(1)} %copy-done.1), custom_call_target="tpu_custom_call" | custom-call | flops 1400000000 | bytes 5000000 | tf_op jit(solution)/shard_map/back/pallas_call | solution.py:482
  102.0 2.5 %collective-permute-start = (bf16[1,512,256]{2,1,0:T(8,128)(2,1)S(1)}, bf16[1,512,256]{2,1,0:T(8,128)(2,1)S(1)}, u32[]{:S(2)}, u32[]{:S(2)}) collective-permute-start(bf16[1,512,256]{2,1,0:T(8,128)(2,1)S(1)} %back.1), channel_id=1, source_target_pairs={{0,256},{128,384},{256,0},{384,128},{1,257},{129,385},{257,1},{385... | collective-permute-start | bytes 786440 | tf_op jit(solution)/shard_map/ppermute | solution.py:523
  104.5 2.5 %collective-permute-start.1 = (bf16[1,512,256]{2,1,0:T(8,128)(2,1)S(1)}, bf16[1,512,256]{2,1,0:T(8,128)(2,1)S(1)}, u32[]{:S(2)}, u32[]{:S(2)}) collective-permute-start(bf16[1,512,256]{2,1,0:T(8,128)(2,1)S(1)} %back.1), channel_id=1, source_target_pairs={{0,128},{128,256},{256,384},{384,0},{1,129},{129,257},{257,385},{3... | collective-permute-start | bytes 786440 | tf_op jit(solution)/shard_map/ppermute | solution.py:523
  107.0 4.0 %collective-permute-start.2 = (bf16[1,512,256]{2,1,0:T(8,128)(2,1)S(1)}, bf16[1,512,256]{2,1,0:T(8,128)(2,1)S(1)}, u32[]{:S(2)}, u32[]{:S(2)}) collective-permute-start(bf16[1,512,256]{2,1,0:T(8,128)(2,1)S(1)} %back.1), channel_id=1, source_target_pairs={{0,384},{128,0},{256,128},{384,256},{1,385},{129,1},{257,129},{385... | collective-permute-start | bytes 786440 | tf_op jit(solution)/shard_map/ppermute | solution.py:523
  111.1 0.1 broadcast_in_dim.6
  111.2 1.7 %collective-permute-done = bf16[1,512,256]{2,1,0:T(8,128)(2,1)S(1)} collective-permute-done((bf16[1,512,256]{2,1,0:T(8,128)(2,1)S(1)}, bf16[1,512,256]{2,1,0:T(8,128)(2,1)S(1)}, u32[]{:S(2)}, u32[]{:S(2)}) %collective-permute-start) | collective-permute-done | bytes 262176 | tf_op jit(solution)/shard_map/ppermute | solution.py:523
  112.9 6.3 %collective-permute-done.1 = bf16[1,512,256]{2,1,0:T(8,128)(2,1)S(1)} collective-permute-done((bf16[1,512,256]{2,1,0:T(8,128)(2,1)S(1)}, bf16[1,512,256]{2,1,0:T(8,128)(2,1)S(1)}, u32[]{:S(2)}, u32[]{:S(2)}) %collective-permute-start.1) | collective-permute-done | bytes 262176 | tf_op jit(solution)/shard_map/ppermute | solution.py:523
  119.3 0.0 copy-start.6
  119.3 1.0 copy-done.6
  (18 shorter events, 0.1 us)
Async XLA Ops:
  5.7 18.5 %copy-start.4 = (f32[1,63]{1,0:T(1,128)S(1)}, f32[1,63]{1,0:T(1,128)}, u32[]{:S(2)}) copy-start(f32[1,63]{1,0:T(1,128)} %pz_ref) | copy-start | bytes 760
  5.7 59.5 %all-to-all-start = ((bf16[128,48,128]{2,1,0:T(8,128)(2,1)}), bf16[128,48,128]{2,1,0:T(8,128)(2,1)S(1)}, u32[]{:S(2)}, u32[]{:S(2)}) async-start(bf16[128,48,128]{2,1,0:T(8,128)(2,1)} %get-tuple-element.18), calls=%async_computation | async-start | bytes 3145728 | tf_op jit(solution)/shard_map/all_to_all | solution.py:503
  65.2 13.1 %copy-start.7 = (f32[1,31]{1,0:T(1,128)S(1)}, f32[1,31]{1,0:T(1,128)}, u32[]{:S(2)}) copy-start(f32[1,31]{1,0:T(1,128)} %py_hbm.1) | copy-start | bytes 376
  65.2 13.1 %copy-start.8 = (f32[1,31]{1,0:T(1,128)S(1)}, f32[1,31]{1,0:T(1,128)}, u32[]{:S(2)}) copy-start(f32[1,31]{1,0:T(1,128)} %px_hbm.1) | copy-start | bytes 376
  66.9 22.8 %copy-start = (s32[128,128]{1,0:T(8,128)S(1)}, s32[128,128]{1,0:T(8,128)}, u32[]{:S(2)}) copy-start(s32[128,128]{1,0:T(8,128)} %get-tuple-element.28.count_ref) | copy-start | bytes 196612
  66.9 33.3 %all-to-all-start.1 = ((bf16[512,4,128]{2,1,0:T(4,128)(2,1)}), bf16[512,4,128]{2,1,0:T(4,128)(2,1)S(1)}, u32[]{:S(2)}, u32[]{:S(2)}) async-start(bf16[512,4,128]{2,1,0:T(4,128)(2,1)} %bitcast.3), calls=%async_computation.1 | async-start | bytes 1048576 | tf_op jit(solution)/shard_map/all_to_all | solution.py:507
  89.6 10.5 %copy-start.1 = (bf16[512,256]{1,0:T(8,128)(2,1)S(1)}, bf16[512,256]{1,0:T(8,128)(2,1)}, u32[]{:S(2)}) copy-start(bf16[512,256]{1,0:T(8,128)(2,1)} %get-tuple-element.30.est_ref) | copy-start | bytes 786436
  89.6 10.5 %copy-start.2 = (s32[8,512]{1,0:T(8,128)S(1)}, s32[8,512]{1,0:T(8,128)}, u32[]{:S(2)}) copy-start(s32[8,512]{1,0:T(8,128)} %get-tuple-element.22.units_ref) | copy-start | bytes 49156
  89.7 10.5 %copy-start.3 = (f32[8,256]{1,0:T(8,128)S(1)}, f32[8,256]{1,0:T(8,128)}, u32[]{:S(2)}) copy-start(f32[8,256]{1,0:T(8,128)} %get-tuple-element.23.rows_ref) | copy-start | bytes 24580
  89.7 10.5 %copy-start.5 = (s32[8]{0:T(128)S(1)}, s32[8]{0:T(128)}, u32[]{:S(2)}) copy-start(s32[8]{0:T(128)} %mask_hbm.3) | copy-start | bytes 100
  102.0 10.9 %collective-permute-start = (bf16[1,512,256]{2,1,0:T(8,128)(2,1)S(1)}, bf16[1,512,256]{2,1,0:T(8,128)(2,1)S(1)}, u32[]{:S(2)}, u32[]{:S(2)}) collective-permute-start(bf16[1,512,256]{2,1,0:T(8,128)(2,1)S(1)} %back.1), channel_id=1, source_target_pairs={{0,256},{128,384},{256,0},{384,128},{1,257},{129,385},{257,1},{385... | collective-permute-start | bytes 786440 | tf_op jit(solution)/shard_map/ppermute | solution.py:523
  104.5 14.7 %collective-permute-start.1 = (bf16[1,512,256]{2,1,0:T(8,128)(2,1)S(1)}, bf16[1,512,256]{2,1,0:T(8,128)(2,1)S(1)}, u32[]{:S(2)}, u32[]{:S(2)}) collective-permute-start(bf16[1,512,256]{2,1,0:T(8,128)(2,1)S(1)} %back.1), channel_id=1, source_target_pairs={{0,128},{128,256},{256,384},{384,0},{1,129},{129,257},{257,385},{3... | collective-permute-start | bytes 786440 | tf_op jit(solution)/shard_map/ppermute | solution.py:523
  107.0 12.2 %collective-permute-start.2 = (bf16[1,512,256]{2,1,0:T(8,128)(2,1)S(1)}, bf16[1,512,256]{2,1,0:T(8,128)(2,1)S(1)}, u32[]{:S(2)}, u32[]{:S(2)}) collective-permute-start(bf16[1,512,256]{2,1,0:T(8,128)(2,1)S(1)} %back.1), channel_id=1, source_target_pairs={{0,384},{128,0},{256,128},{384,256},{1,385},{129,1},{257,129},{385... | collective-permute-start | bytes 786440 | tf_op jit(solution)/shard_map/ppermute | solution.py:523
  119.3 1.0 copy-start.6

commit v12 on v10

--- a/solution.py
+++ b/solution.py
@@ -208,7 +208,8 @@
             jnp.concatenate([tile[plane * TILE : (plane + 1) * TILE] for plane in range(SLAB)], axis=1)
         )
     blurred = jnp.concatenate(blurred, axis=0)
-    parts = [dot(pick, blurred).astype(BF16), dot(pick_more, blurred).astype(BF16), seen]
+    both = dot(jnp.concatenate([pick, pick_more], axis=0), blurred).astype(BF16)
+    parts = [both[:slots], both[slots:], seen]
     for i in range(DEVS // block):
         turned = dot(turn, jnp.concatenate([rows_of(part, i) for part in parts], axis=1)).astype(BF16)
         for k in range(len(parts)):

time: 120 us -> 120 us (level)
  no operation moved by 1% of the time
where the time goes in v12:
time: 120 us; the launch traced here: 119 us
  waiting for transfers between devices  48.9 us (41%)
  starting transfers between devices  29.8 us (25%)
  blocking collectives  23.7 us (20%)
  Pallas kernels  14 us (12%)
  local copies, waits for them, and re-layouts  1.66 us (1%)
    all_to_all x1, waiting for transfers between devices, shards(): lax.all_to_all(message, 'space', split_axis=0, concat_axis=0, tiled=True)  40.1 us
    all_to_all x1, starting transfers between devices, shards(): lax.all_to_all(message, 'space', split_axis=0, concat_axis=0, tiled=True)  18.4 us
    all_to_all x1, blocking collectives, shards(): lax.all_to_all(updated, 'view', split_axis=0, concat_axis=0, tiled=True)  15.9 us
    all_to_all x1, starting transfers between devices, shards(): lax.all_to_all(sent.reshape(VIEWS * DEVS, HALF, TILE), ('view', 'space'),...  11.4 us
    all_to_all x1, waiting for transfers between devices, shards(): lax.all_to_all(sent.reshape(VIEWS * DEVS, HALF, TILE), ('view', 'space'),...  8.72 us
    all_gather x1, blocking collectives, shards(): lax.all_gather(jnp.concatenate([psf_x, psf_y], axis=1), 'view', axis=0, t...  7.76 us
    pallas_call x1, Pallas kernels, pack(): call(pack_kernel, 'pack', (shape(DEVS, MSG, TILE), shape(UNITS // TILE, T...  5.05 us
    pallas_call x1, Pallas kernels, prep(): call(prep_kernel, 'prep', (shape(2 * VIEWS, NY, dtype=F32), shape(8, HALF...  2.85 us
  transfers between devices with their start and end apart: 2, of which 2 were waited for; matrix products, arithmetic and copies ran while one was open for 1% of the time, Pallas kernels for 5%

profile of v12, /device:TPU:1, one launch (start us, length us, event | category | flops | bytes accessed | tf_op | source)
XLA Modules:
  0.0 118.9 jit_solution(2034422333201534309)
XLA Ops:
  0.6 5.1 %pack.1 = (bf16[128,48,128]{2,1,0:T(8,128)(2,1)}, s32[8,128]{1,0:T(8,128)}, s32[128,128]{1,0:T(8,128)}) custom-call(s32[8]{0:T(128)} %mask_hbm.3, f32[1,31]{1,0:T(1,128)} %px_hbm.1, f32[1,31]{1,0:T(1,128)} %py_hbm.1, s32[1,1024]{1,0:T(1,128)} %bitcast.10, bf16[4,512,256]{2,1,0:T(8,128)(2,1)} %est_hbm.3, bf16[1,4,512,256]{3,2,1,0:T(8,128)(2,1)} %meas_hbm.1), custom_call_target="tpu_custom_call" | custom-call | flops 2000000000 | bytes 4000000 | tf_op jit(solution)/shard_map/pack/pallas_call | solution.py:392
  5.7 0.0 copy-start.4
  5.7 18.4 %all-to-all-start = ((bf16[128,48,128]{2,1,0:T(8,128)(2,1)}), bf16[128,48,128]{2,1,0:T(8,128)(2,1)S(1)}, u32[]{:S(2)}, u32[]{:S(2)}) async-start(bf16[128,48,128]{2,1,0:T(8,128)(2,1)} %get-tuple-element.18), calls=%async_computation | async-start | bytes 3145728 | tf_op jit(solution)/shard_map/all_to_all | solution.py:504
  24.1 0.0 copy-done.4
  24.2 0.9 bands.1
  25.1 40.1 %all-to-all-done.in_ref = bf16[128,48,128]{2,1,0:T(8,128)(2,1)S(1)} async-done(((bf16[128,48,128]{2,1,0:T(8,128)(2,1)}), bf16[128,48,128]{2,1,0:T(8,128)(2,1)S(1)}, u32[]{:S(2)}, u32[]{:S(2)}) %all-to-all-start) | async-done | bytes 1572896 | tf_op jit(solution)/shard_map/all_to_all | solution.py:504
  65.2 1.6 %zpair.1 = bf16[4,512,128]{2,1,0:T(8,128)(2,1)} custom-call(bf16[256,512]{1,0:T(8,128)(2,1)S(1)} %get-tuple-element.25.forward_ref, bf16[256,512]{1,0:T(8,128)(2,1)S(1)} %get-tuple-element.26.adjoint_ref, bf16[128,48,128]{2,1,0:T(8,128)(2,1)S(1)} %all-to-all-done.in_ref), custom_call_target="tpu_custom_call" | custom-call | flops 540000000 | bytes 3000000 | tf_op jit(solution)/shard_map/zpair/pallas_call | solution.py:450
  66.9 0.0 copy-start
  66.9 11.4 %all-to-all-start.1 = ((bf16[512,4,128]{2,1,0:T(4,128)(2,1)}), bf16[512,4,128]{2,1,0:T(4,128)(2,1)S(1)}, u32[]{:S(2)}, u32[]{:S(2)}) async-start(bf16[512,4,128]{2,1,0:T(4,128)(2,1)} %bitcast.3), calls=%async_computation.1 | async-start | bytes 1048576 | tf_op jit(solution)/shard_map/all_to_all | solution.py:508
  78.3 0.0 copy-done.6
  78.3 0.0 copy-done.7
  78.3 0.1 maximum_bitcast_fusion
  78.4 7.8 %all-gather = f32[4,1,62]{2,1,0:T(1,128)S(1)} all-gather(f32[1,1,62]{2,1,0:T(1,128)S(1)} %maximum_bitcast_fusion), channel_id=1, replica_groups=mesh['view'=4,'space'=128] {'view'}, dimensions={0}, use_global_device_ids=true | all-gather | bytes 1240 | tf_op jit(solution)/shard_map/all_gather | solution.py:515
  86.2 0.7 fusion
  86.8 2.8 %prep.1 = (f32[8,256]{1,0:T(8,128)}, s32[8,512]{1,0:T(8,128)}, bf16[512,256]{1,0:T(8,128)(2,1)}) custom-call(f32[4,31]{1,0:T(4,128)} %get-tuple-element.33.px_ref, f32[4,31]{1,0:T(4,128)} %get-tuple-element.32.py_ref, s32[8,128]{1,0:T(8,128)} %get-tuple-element.21.table_ref, bf16[4,512,256]{2,1,0:T(8,128)(2,1)} %est_hbm.3), custom_call_target="tpu_custom_call" | custom-call | flops 10000000 | bytes 1000000 | tf_op jit(solution)/shard_map/prep/pallas_call | solution.py:435
  89.7 0.0 copy-start.1
  89.7 0.0 copy-start.2
  89.7 0.0 copy-start.5
  89.7 1.7 %column.1 = bf16[512,8,128]{2,1,0:T(8,128)(2,1)} custom-call(bf16[256,512]{1,0:T(8,128)(2,1)S(1)} %get-tuple-element.25.forward_ref, s32[128,128]{1,0:T(8,128)S(1)} %copy-done, bf16[128,48,128]{2,1,0:T(8,128)(2,1)S(1)} %all-to-all-done.in_ref), custom_call_target="tpu_custom_call" | custom-call | flops 540000000 | bytes 3000000 | tf_op jit(solution)/shard_map/column/pallas_call | solution.py:469
  91.4 8.7 %all-to-all-done.1 = bf16[512,4,128]{2,1,0:T(4,128)(2,1)S(1)} async-done(((bf16[512,4,128]{2,1,0:T(4,128)(2,1)}), bf16[512,4,128]{2,1,0:T(4,128)(2,1)S(1)}, u32[]{:S(2)}, u32[]{:S(2)}) %all-to-all-start.1) | async-done | bytes 524320 | tf_op jit(solution)/shard_map/all_to_all | solution.py:508
  100.2 0.0 copy-done.2
  100.2 1.8 %back.1 = bf16[4,512,256]{2,1,0:T(8,128)(2,1)S(1)} custom-call(s32[8]{0:T(128)S(1)} %copy-done.5, s32[8,512]{1,0:T(8,128)S(1)} %copy-done.2, f32[8,256]{1,0:T(8,128)S(1)} %copy-done.3, bf16[4,512,128]{2,1,0:T(8,128)(2,1)S(1)} %bitcast.7, bf16[512,256]{1,0:T(8,128)(2,1)S(1)} %copy-done.1), custom_call_target="tpu_custom_call" | custom-call | flops 1400000000 | bytes 5000000 | tf_op jit(solution)/shard_map/back/pallas_call | solution.py:483
  102.0 15.9 %all_to_all.15 = bf16[4,512,256]{2,1,0:T(8,128)(2,1)S(1)} all-to-all(bf16[4,512,256]{2,1,0:T(8,128)(2,1)S(1)} %back.1), channel_id=1, replica_groups=mesh['view'=4,'space'=128] {'view'}, dimensions={0} | all-to-all | bytes 2097152 | tf_op jit(solution)/shard_map/all_to_all | solution.py:519
  117.9 1.0 copy.11
  (7 shorter events, 0.0 us)
Async XLA Ops:
  5.7 18.5 %copy-start.4 = (f32[1,63]{1,0:T(1,128)S(1)}, f32[1,63]{1,0:T(1,128)}, u32[]{:S(2)}) copy-start(f32[1,63]{1,0:T(1,128)} %pz_ref) | copy-start | bytes 760
  5.7 59.5 %all-to-all-start = ((bf16[128,48,128]{2,1,0:T(8,128)(2,1)}), bf16[128,48,128]{2,1,0:T(8,128)(2,1)S(1)}, u32[]{:S(2)}, u32[]{:S(2)}) async-start(bf16[128,48,128]{2,1,0:T(8,128)(2,1)} %get-tuple-element.18), calls=%async_computation | async-start | bytes 3145728 | tf_op jit(solution)/shard_map/all_to_all | solution.py:504
  65.2 13.1 %copy-start.6 = (f32[1,31]{1,0:T(1,128)S(1)}, f32[1,31]{1,0:T(1,128)}, u32[]{:S(2)}) copy-start(f32[1,31]{1,0:T(1,128)} %py_hbm.1) | copy-start | bytes 376
  65.2 13.1 %copy-start.7 = (f32[1,31]{1,0:T(1,128)S(1)}, f32[1,31]{1,0:T(1,128)}, u32[]{:S(2)}) copy-start(f32[1,31]{1,0:T(1,128)} %px_hbm.1) | copy-start | bytes 376
  66.9 22.8 %copy-start = (s32[128,128]{1,0:T(8,128)S(1)}, s32[128,128]{1,0:T(8,128)}, u32[]{:S(2)}) copy-start(s32[128,128]{1,0:T(8,128)} %get-tuple-element.28.count_ref) | copy-start | bytes 196612
  66.9 33.3 %all-to-all-start.1 = ((bf16[512,4,128]{2,1,0:T(4,128)(2,1)}), bf16[512,4,128]{2,1,0:T(4,128)(2,1)S(1)}, u32[]{:S(2)}, u32[]{:S(2)}) async-start(bf16[512,4,128]{2,1,0:T(4,128)(2,1)} %bitcast.3), calls=%async_computation.1 | async-start | bytes 1048576 | tf_op jit(solution)/shard_map/all_to_all | solution.py:508
  89.7 10.5 %copy-start.1 = (bf16[512,256]{1,0:T(8,128)(2,1)S(1)}, bf16[512,256]{1,0:T(8,128)(2,1)}, u32[]{:S(2)}) copy-start(bf16[512,256]{1,0:T(8,128)(2,1)} %get-tuple-element.30.est_ref) | copy-start | bytes 786436
  89.7 10.5 %copy-start.2 = (s32[8,512]{1,0:T(8,128)S(1)}, s32[8,512]{1,0:T(8,128)}, u32[]{:S(2)}) copy-start(s32[8,512]{1,0:T(8,128)} %get-tuple-element.22.units_ref) | copy-start | bytes 49156
  89.7 10.5 %copy-start.3 = (f32[8,256]{1,0:T(8,128)S(1)}, f32[8,256]{1,0:T(8,128)}, u32[]{:S(2)}) copy-start(f32[8,256]{1,0:T(8,128)} %get-tuple-element.23.rows_ref) | copy-start | bytes 24580
  89.7 10.5 %copy-start.5 = (s32[8]{0:T(128)S(1)}, s32[8]{0:T(128)}, u32[]{:S(2)}) copy-start(s32[8]{0:T(128)} %mask_hbm.3) | copy-start | bytes 100

commit v13 on v12

--- a/solution.py
+++ b/solution.py
@@ -241,7 +241,7 @@
     adjoint_ref[...] = dot(one_hot(iota((ZB, ZB), 1) == source), adjoint).astype(BF16)
 
 
-def prep_kernel(px_ref, py_ref, table_ref, est_hbm, rows_ref, units_ref, plane_ref, sem):
+def prep_kernel(mask_ref, px_ref, py_ref, table_ref, est_hbm, rows_ref, units_ref, plane_ref, sem):
     plane_copy = pltpu.make_async_copy(est_hbm.at[lax.axis_index("view")], plane_ref, sem)
     plane_copy.start()
     half_xy = TAPS_XY // 2
@@ -257,10 +257,12 @@
     table = table_ref[...].astype(F32)
     table = jnp.concatenate([table] * (TILE // tiles), axis=0).T.astype(I32)
     total = jnp.zeros((1, slots), I32)
+    rank = jnp.int32(0)
     for tile in range(tiles):
         place = table[:, tile : tile + 1]
         place = jnp.where(place < 0, -1, place % DEVS * HALF + place // DEVS)
-        unit = 2 * (tile // 2 * TILE + iota((TILE, slots), 0)) + tile % 2
+        unit = rank * TILE + iota((TILE, slots), 0)
+        rank += mask_ref[tile]
         total += jnp.sum(jnp.where(place == iota((TILE, slots), 1), unit, 0), axis=0, keepdims=True)
     units_ref[...] = jnp.broadcast_to(total, (8, slots))
     plane_copy.wait()
@@ -352,10 +354,9 @@
     cols = jnp.concatenate([in_ref[view] for view in range(VIEWS)], axis=1)
     units = units_ref[0:1, :]
     slots = HALF * DEVS
+    found = dot(one_hot(units == iota((slots, slots), 0)), cols).astype(BF16)
     mask_copy.wait()
     chosen = tissue_tiles(mask_ref)
-    here = [units == 2 * (tile // 2 * TILE + iota((TILE, slots), 0)) + tile % 2 for tile in chosen]
-    found = dot(jnp.concatenate([one_hot(h) for h in here], axis=0), cols).astype(BF16)
     for i, tile in enumerate(chosen):
         row = pl.multiple_of(tile // 2 * TILE, TILE)
         lane = pl.multiple_of(tile % 2 * TILE, TILE)
@@ -431,18 +432,18 @@
     )(psf_z)
 
 
-def prep(taps_x, taps_y, table, estimate):
+def prep(tissue_mask, taps_x, taps_y, table, estimate):
     return call(
         prep_kernel,
         "prep",
         (shape(2 * VIEWS, NY, dtype=F32), shape(8, HALF * DEVS, dtype=I32), shape(NX, NY)),
-        [SMEM, SMEM, VMEM, ANY],
+        [SMEM, SMEM, SMEM, VMEM, ANY],
         (VMEM,) * 3,
         [pltpu.SemaphoreType.DMA],
         WIDE_LIMIT,
         flops=10_000_000,
         moved=1_000_000,
-    )(taps_x, taps_y, table, estimate)
+    )(tissue_mask, taps_x, taps_y, table, estimate)
 
 
 def z_pair(forward, adjoint, arrived):
@@ -513,7 +514,7 @@
         tiled=True,
     ).reshape(VIEWS, HALF * DEVS, TILE)
     taps = lax.all_gather(jnp.concatenate([psf_x, psf_y], axis=1), "view", axis=0, tiled=True)
-    rows, units, plane = prep(taps[:, :TAPS_XY], taps[:, TAPS_XY:], table, estimate)
+    rows, units, plane = prep(tissue_mask, taps[:, :TAPS_XY], taps[:, TAPS_XY:], table, estimate)
     returned, column_blur = lax.optimization_barrier((returned, column(forward, count, arrived)))
     updated = back(tissue_mask, units, rows, returned, plane)
     updated = lax.all_to_all(updated, "view", split_axis=0, concat_axis=0, tiled=True)

time: 120 us -> 120 us (level)
  no operation moved by 1% of the time
where the time goes in v13:
time: 120 us; the launch traced here: 119 us
  waiting for transfers between devices  48.9 us (41%)
  starting transfers between devices  29.8 us (25%)
  blocking collectives  23.7 us (20%)
  Pallas kernels  13.9 us (12%)
  local copies, waits for them, and re-layouts  1.66 us (1%)
    all_to_all x1, waiting for transfers between devices, shards(): lax.all_to_all(message, 'space', split_axis=0, concat_axis=0, tiled=True)  40.1 us
    all_to_all x1, starting transfers between devices, shards(): lax.all_to_all(message, 'space', split_axis=0, concat_axis=0, tiled=True)  18.4 us
    all_to_all x1, blocking collectives, shards(): lax.all_to_all(updated, 'view', split_axis=0, concat_axis=0, tiled=True)  15.9 us
    all_to_all x1, starting transfers between devices, shards(): lax.all_to_all(sent.reshape(VIEWS * DEVS, HALF, TILE), ('view', 'space'),...  11.4 us
    all_to_all x1, waiting for transfers between devices, shards(): lax.all_to_all(sent.reshape(VIEWS * DEVS, HALF, TILE), ('view', 'space'),...  8.73 us
    all_gather x1, blocking collectives, shards(): lax.all_gather(jnp.concatenate([psf_x, psf_y], axis=1), 'view', axis=0, t...  7.76 us
    pallas_call x1, Pallas kernels, pack(): call(pack_kernel, 'pack', (shape(DEVS, MSG, TILE), shape(UNITS // TILE, T...  5.05 us
    pallas_call x1, Pallas kernels, prep(): call(prep_kernel, 'prep', (shape(2 * VIEWS, NY, dtype=F32), shape(8, HALF...  2.85 us
  transfers between devices with their start and end apart: 2, of which 2 were waited for; matrix products, arithmetic and copies ran while one was open for 1% of the time, Pallas kernels for 5%

profile of v13, /device:TPU:1, one launch (start us, length us, event | category | flops | bytes accessed | tf_op | source)
XLA Modules:
  0.0 118.8 jit_solution(1153695571409159495)
XLA Ops:
  0.6 5.1 %pack.1 = (bf16[128,48,128]{2,1,0:T(8,128)(2,1)}, s32[8,128]{1,0:T(8,128)}, s32[128,128]{1,0:T(8,128)}) custom-call(s32[8]{0:T(128)} %mask_hbm.3, f32[1,31]{1,0:T(1,128)} %px_hbm.1, f32[1,31]{1,0:T(1,128)} %py_hbm.1, s32[1,1024]{1,0:T(1,128)} %bitcast.10, bf16[4,512,256]{2,1,0:T(8,128)(2,1)} %est_hbm.3, bf16[1,4,512,256]{3,2,1,0:T(8,128)(2,1)} %meas_hbm.1), custom_call_target="tpu_custom_call" | custom-call | flops 2000000000 | bytes 4000000 | tf_op jit(solution)/shard_map/pack/pallas_call | solution.py:393
  5.7 0.0 copy-start.5
  5.7 18.4 %all-to-all-start = ((bf16[128,48,128]{2,1,0:T(8,128)(2,1)}), bf16[128,48,128]{2,1,0:T(8,128)(2,1)S(1)}, u32[]{:S(2)}, u32[]{:S(2)}) async-start(bf16[128,48,128]{2,1,0:T(8,128)(2,1)} %get-tuple-element.18), calls=%async_computation | async-start | bytes 3145728 | tf_op jit(solution)/shard_map/all_to_all | solution.py:505
  24.1 0.0 copy-done.5
  24.2 0.9 bands.1
  25.1 40.1 %all-to-all-done.in_ref = bf16[128,48,128]{2,1,0:T(8,128)(2,1)S(1)} async-done(((bf16[128,48,128]{2,1,0:T(8,128)(2,1)}), bf16[128,48,128]{2,1,0:T(8,128)(2,1)S(1)}, u32[]{:S(2)}, u32[]{:S(2)}) %all-to-all-start) | async-done | bytes 1572896 | tf_op jit(solution)/shard_map/all_to_all | solution.py:505
  65.2 1.6 %zpair.1 = bf16[4,512,128]{2,1,0:T(8,128)(2,1)} custom-call(bf16[256,512]{1,0:T(8,128)(2,1)S(1)} %get-tuple-element.25.forward_ref, bf16[256,512]{1,0:T(8,128)(2,1)S(1)} %get-tuple-element.26.adjoint_ref, bf16[128,48,128]{2,1,0:T(8,128)(2,1)S(1)} %all-to-all-done.in_ref), custom_call_target="tpu_custom_call" | custom-call | flops 540000000 | bytes 3000000 | tf_op jit(solution)/shard_map/zpair/pallas_call | solution.py:451
  66.9 0.0 copy-start
  66.9 11.4 %all-to-all-start.1 = ((bf16[512,4,128]{2,1,0:T(4,128)(2,1)}), bf16[512,4,128]{2,1,0:T(4,128)(2,1)S(1)}, u32[]{:S(2)}, u32[]{:S(2)}) async-start(bf16[512,4,128]{2,1,0:T(4,128)(2,1)} %bitcast.3), calls=%async_computation.1 | async-start | bytes 1048576 | tf_op jit(solution)/shard_map/all_to_all | solution.py:509
  78.3 0.0 copy-done.6
  78.3 0.1 maximum_bitcast_fusion
  78.4 7.8 %all-gather = f32[4,1,62]{2,1,0:T(1,128)S(1)} all-gather(f32[1,1,62]{2,1,0:T(1,128)S(1)} %maximum_bitcast_fusion), channel_id=1, replica_groups=mesh['view'=4,'space'=128] {'view'}, dimensions={0}, use_global_device_ids=true | all-gather | bytes 1240 | tf_op jit(solution)/shard_map/all_gather | solution.py:516
  86.2 0.7 fusion
  86.8 2.8 %prep.1 = (f32[8,256]{1,0:T(8,128)}, s32[8,512]{1,0:T(8,128)}, bf16[512,256]{1,0:T(8,128)(2,1)}) custom-call(s32[8]{0:T(128)} %mask_hbm.3, f32[4,31]{1,0:T(4,128)} %get-tuple-element.33.px_ref, f32[4,31]{1,0:T(4,128)} %get-tuple-element.32.py_ref, s32[8,128]{1,0:T(8,128)} %get-tuple-element.21.table_ref, bf16[4,512,256]{2,1,0:T(8,128)(2,1)} %est_hbm.3), custom_call_target="tpu_custom_call" | custom-call | flops 10000000 | bytes 1000000 | tf_op jit(solution)/shard_map/prep/pallas_call | solution.py:436
  89.7 0.0 copy-start.1
  89.7 0.0 copy-start.2
  89.7 0.0 copy-start.3
  89.7 0.0 copy-start.4
  89.7 0.0 copy-done
  89.7 1.7 %column.1 = bf16[512,8,128]{2,1,0:T(8,128)(2,1)} custom-call(bf16[256,512]{1,0:T(8,128)(2,1)S(1)} %get-tuple-element.25.forward_ref, s32[128,128]{1,0:T(8,128)S(1)} %copy-done, bf16[128,48,128]{2,1,0:T(8,128)(2,1)S(1)} %all-to-all-done.in_ref), custom_call_target="tpu_custom_call" | custom-call | flops 540000000 | bytes 3000000 | tf_op jit(solution)/shard_map/column/pallas_call | solution.py:470
  91.4 8.7 %all-to-all-done.1 = bf16[512,4,128]{2,1,0:T(4,128)(2,1)S(1)} async-done(((bf16[512,4,128]{2,1,0:T(4,128)(2,1)}), bf16[512,4,128]{2,1,0:T(4,128)(2,1)S(1)}, u32[]{:S(2)}, u32[]{:S(2)}) %all-to-all-start.1) | async-done | bytes 524320 | tf_op jit(solution)/shard_map/all_to_all | solution.py:509
  100.2 1.7 %back.1 = bf16[4,512,256]{2,1,0:T(8,128)(2,1)S(1)} custom-call(s32[8]{0:T(128)S(1)} %copy-done.1, s32[8,512]{1,0:T(8,128)S(1)} %copy-done.3, f32[8,256]{1,0:T(8,128)S(1)} %copy-done.4, bf16[4,512,128]{2,1,0:T(8,128)(2,1)S(1)} %bitcast.7, bf16[512,256]{1,0:T(8,128)(2,1)S(1)} %copy-done.2), custom_call_target="tpu_custom_call" | custom-call | flops 1400000000 | bytes 5000000 | tf_op jit(solution)/shard_map/back/pallas_call | solution.py:484
  101.9 15.9 %all_to_all.15 = bf16[4,512,256]{2,1,0:T(8,128)(2,1)S(1)} all-to-all(bf16[4,512,256]{2,1,0:T(8,128)(2,1)S(1)} %back.1), channel_id=1, replica_groups=mesh['view'=4,'space'=128] {'view'}, dimensions={0} | all-to-all | bytes 2097152 | tf_op jit(solution)/shard_map/all_to_all | solution.py:520
  117.8 1.0 copy.11
  (7 shorter events, 0.0 us)
Async XLA Ops:
  5.7 18.5 %copy-start.5 = (f32[1,63]{1,0:T(1,128)S(1)}, f32[1,63]{1,0:T(1,128)}, u32[]{:S(2)}) copy-start(f32[1,63]{1,0:T(1,128)} %pz_ref) | copy-start | bytes 760
  5.7 59.5 %all-to-all-start = ((bf16[128,48,128]{2,1,0:T(8,128)(2,1)}), bf16[128,48,128]{2,1,0:T(8,128)(2,1)S(1)}, u32[]{:S(2)}, u32[]{:S(2)}) async-start(bf16[128,48,128]{2,1,0:T(8,128)(2,1)} %get-tuple-element.18), calls=%async_computation | async-start | bytes 3145728 | tf_op jit(solution)/shard_map/all_to_all | solution.py:505
  65.2 13.1 %copy-start.6 = (f32[1,31]{1,0:T(1,128)S(1)}, f32[1,31]{1,0:T(1,128)}, u32[]{:S(2)}) copy-start(f32[1,31]{1,0:T(1,128)} %py_hbm.1) | copy-start | bytes 376
  65.2 13.1 %copy-start.7 = (f32[1,31]{1,0:T(1,128)S(1)}, f32[1,31]{1,0:T(1,128)}, u32[]{:S(2)}) copy-start(f32[1,31]{1,0:T(1,128)} %px_hbm.1) | copy-start | bytes 376
  66.9 22.8 %copy-start = (s32[128,128]{1,0:T(8,128)S(1)}, s32[128,128]{1,0:T(8,128)}, u32[]{:S(2)}) copy-start(s32[128,128]{1,0:T(8,128)} %get-tuple-element.28.count_ref) | copy-start | bytes 196612
  66.9 33.3 %all-to-all-start.1 = ((bf16[512,4,128]{2,1,0:T(4,128)(2,1)}), bf16[512,4,128]{2,1,0:T(4,128)(2,1)S(1)}, u32[]{:S(2)}, u32[]{:S(2)}) async-start(bf16[512,4,128]{2,1,0:T(4,128)(2,1)} %bitcast.3), calls=%async_computation.1 | async-start | bytes 1048576 | tf_op jit(solution)/shard_map/all_to_all | solution.py:509
  89.7 10.5 %copy-start.1 = (s32[8]{0:T(128)S(1)}, s32[8]{0:T(128)}, u32[]{:S(2)}) copy-start(s32[8]{0:T(128)} %mask_hbm.3) | copy-start | bytes 100
  89.7 10.5 %copy-start.2 = (bf16[512,256]{1,0:T(8,128)(2,1)S(1)}, bf16[512,256]{1,0:T(8,128)(2,1)}, u32[]{:S(2)}) copy-start(bf16[512,256]{1,0:T(8,128)(2,1)} %get-tuple-element.30.est_ref) | copy-start | bytes 786436
  89.7 10.5 %copy-start.3 = (s32[8,512]{1,0:T(8,128)S(1)}, s32[8,512]{1,0:T(8,128)}, u32[]{:S(2)}) copy-start(s32[8,512]{1,0:T(8,128)} %get-tuple-element.22.units_ref) | copy-start | bytes 49156
  89.7 10.5 %copy-start.4 = (f32[8,256]{1,0:T(8,128)S(1)}, f32[8,256]{1,0:T(8,128)}, u32[]{:S(2)}) copy-start(f32[8,256]{1,0:T(8,128)} %get-tuple-element.23.rows_ref) | copy-start | bytes 24580
